TPU v7x, 512 devices: a whole 4x8x8 slice. The times are simulated.
512 devices in a mesh: rows: 256 (over y, z, x), rep: 2 (over core).
Axes of the slice: x: 4, y: 8, z: 8, core: 2. Of those that a mesh axis runs over, the one named last changes fastest.
Arguments:
- hamiltonian: bfloat16 [1024, 8, 128, 128], P('rows'), may hold values from -6 to 6
- x_correction: bfloat16 [1024, 8, 128, 128], P('rows'), may hold values from -0.3125 to 0.3125
- block_cols: int32 [1024, 8], P('rows'), may hold values from 0 to 1023, as said below
- block_mask: int32 [1024, 8], P('rows'), may hold values from 0 to 1, as said below
Outputs:
- density: bfloat16 [1024, 8, 128, 128], P('rows', 'rep')
Inputs may be any that keep to these rules, and one draw needn't show every extreme that they name: `block_cols`: in row i the slots with block_mask 1 name distinct block columns at most 4 away from i; slot 0 names i itself. Padding slots hold a column clipped into range. `block_mask`: slot 0 of every row is 1.
All inputs are finite; a program needn't handle non-finite values.
Results may differ from a plain program's by a relative error of at most 0.038.
Values may be sent and summed in bfloat16 or wider, within the bound.
No kernel may reach another device: no remote copies, remote signals or barrier semaphores. Data moves between devices by JAX's collectives and lax.ppermute only.
A program may use at most 64 MiB of HBM per device.

v0:
```python
import math

import jax
import jax.numpy as jnp
from jax import lax
from jax.sharding import PartitionSpec as P

BAND = 4
STEPS = 2


def passed_along(x, axis, by):
    size = lax.axis_size(axis)
    pairs = [(i, i + by) for i in range(size) if 0 <= i + by < size]
    return lax.ppermute(x, axis, pairs)


def offsets_of(rows_here):
    reach = (BAND + rows_here - 1) // rows_here
    return (reach, list(range(reach, 0, -1)) + list(range(-1, -reach - 1, -1)))


def assemble(values, pieces, reach):
    joined = jnp.concatenate(pieces[:reach] + [values] + pieces[reach:], axis=0)
    return joined


def fetch(values):
    rows_here = values.shape[0]
    reach, offsets = offsets_of(rows_here)
    pieces = [passed_along(values, "rows", offset) for offset in offsets]
    return assemble(values, pieces, reach)


def multiply(left, band, block_cols, block_mask, band_cols, band_mask, first_row, start, half):
    rows_here, slots, size, unused = left.shape
    band_rows = band.shape[0]
    cols_out = lax.dynamic_slice_in_dim(block_cols, start, half, 1)
    mask_out = lax.dynamic_slice_in_dim(block_mask, start, half, 1)
    local_row = jnp.clip(block_cols - first_row, 0, band_rows - 1)
    cols_there = band_cols[local_row]
    mask_there = band_mask[local_row]
    match = (
        (cols_there[:, None, :, :] == cols_out[:, :, None, None])
        & (mask_there[:, None, :, :] == 1)
        & (block_mask[:, None, :, None] == 1)
    )
    order = jnp.arange(slots, dtype=jnp.int32)
    slot_there = jnp.sum(jnp.where(match, order, 0), axis=-1)
    found = jnp.any(match, axis=-1)
    flat_index = local_row[:, None, :] * slots + slot_there
    picked = jnp.take(band.reshape(band_rows * slots, size, size), flat_index, axis=0)
    picked = jnp.where(found[:, :, :, None, None], picked, jnp.zeros((), jnp.bfloat16))
    summed = jnp.einsum("itab,istbc->isac", left, picked, preferred_element_type=jnp.float32)
    return (summed * mask_out.astype(jnp.float32)[:, :, None, None]).astype(jnp.bfloat16)


def on_device(hamiltonian, x_correction, block_cols, block_mask):
    rows_here, slots = block_cols.shape
    size = hamiltonian.shape[-1]
    half = slots // 2
    copy_index = lax.axis_index("rep")
    start = copy_index * half
    own_first = lax.axis_index("rows") * rows_here
    first_row = own_first - BAND
    stacked = jnp.stack([block_cols, block_mask], axis=1)
    reach, offsets = offsets_of(rows_here)
    pattern_pieces = [passed_along(stacked, "rows", offset) for offset in offsets]
    band_pattern = assemble(stacked, pattern_pieces, reach)
    band_cols = band_pattern[:, 0, :]
    band_mask = band_pattern[:, 1, :]

    def apply(left, right):
        band = fetch(right)
        return multiply(
            left, band, block_cols, block_mask, band_cols, band_mask, first_row, start, half
        )

    def whole(part):
        return lax.all_gather(part, "rep", axis=1, tiled=True)

    identity = jnp.eye(size, dtype=jnp.float32)
    global_rows = own_first + jnp.arange(rows_here, dtype=jnp.int32)
    on_diag = (block_cols == global_rows[:, None]).astype(jnp.float32)[:, :, None, None]
    xmat = (identity * on_diag + x_correction.astype(jnp.float32)).astype(jnp.bfloat16)
    half_product = whole(apply(xmat, hamiltonian))
    orthogonal_part = apply(half_product, xmat)
    factor = 0.6 / math.sqrt(slots * size)
    diag_part = lax.dynamic_slice_in_dim(on_diag, start, half, 1)
    start_part = (0.5 * identity * diag_part - factor * orthogonal_part.astype(jnp.float32)).astype(
        jnp.bfloat16
    )
    current = whole(start_part)
    result = start_part
    for step in range(STEPS):
        square = whole(apply(current, current))
        cube_part = apply(square, current)
        square_part = lax.dynamic_slice_in_dim(square, start, half, 1)
        result = (
            3.0 * square_part.astype(jnp.float32) - 2.0 * cube_part.astype(jnp.float32)
        ).astype(jnp.bfloat16)
        if step + 1 < STEPS:
            current = whole(result)
    return result


def solution(mesh):
    return jax.shard_map(
        on_device,
        mesh=mesh,
        in_specs=(
            P("rows", None, None, None),
            P("rows", None, None, None),
            P("rows", None),
            P("rows", None),
        ),
        out_specs=P("rows", "rep", None, None),
        check_vma=False,
    )
```

profile of v0, /device:TPU:1, one launch (start us, length us, event | category | flops | bytes accessed | tf_op | source)
XLA Modules:
  0.0 284.9 jit_solution(17778360798513678394)
XLA Ops:
  6.5 0.7 pad_add_fusion.1
  7.2 3.9 %collective-permute-start = (s32[4,2,8]{2,0,1:T(4,128)S(1)}, s32[4,2,8]{2,0,1:T(4,128)S(1)}, u32[]{:S(2)}, u32[]{:S(2)}) collective-permute-start(s32[4,2,8]{2,0,1:T(4,128)S(1)} %pad_add_fusion.1), channel_id=1, source_target_pairs={{0,2},{2,4},{4,6},{6,8},{8,10},{10,12},{12,14},{14,16},{16,18},{18... | collective-permute-start | bytes 776 | tf_op jit(solution)/shard_map/ppermute | solution.py:15
  11.2 1.3 collective-permute-start.1
  12.5 4.1 %collective-permute-start.4 = (bf16[4,8,128,128]{3,2,1,0:T(8,128)(2,1)}, bf16[4,8,128,128]{3,2,1,0:T(8,128)(2,1)S(1)}, u32[]{:S(2)}, u32[]{:S(2)}) collective-permute-start(bf16[4,8,128,128]{3,2,1,0:T(8,128)(2,1)} %param.6), channel_id=1, source_target_pairs={{0,2},{2,4},{4,6},{6,8},{8,10},{10,12},{12,14},{14,16},{16,18},{18... | collective-permute-start | bytes 3145736 | tf_op jit(solution)/shard_map/ppermute | solution.py:15
  16.5 1.3 collective-permute-start.5
  17.9 0.8 compare_convert_fusion
  18.6 2.6 add_convert_fusion
  21.3 5.0 %collective-permute-start.2 = (bf16[4,8,128,128]{3,2,1,0:T(8,128)(2,1)}, bf16[4,8,128,128]{3,2,1,0:T(8,128)(2,1)}, u32[]{:S(2)}, u32[]{:S(2)}) collective-permute-start(bf16[4,8,128,128]{3,2,1,0:T(8,128)(2,1)} %add_convert_fusion), channel_id=1, source_target_pairs={{0,2},{2,4},{4,6},{6,8},{8,10},{10,12},{12,14},{14,16},{16,18},{18... | collective-permute-start | bytes 3145736 | tf_op jit(solution)/shard_map/ppermute | solution.py:15
  26.3 0.7 broadcast_compare_fusion
  26.9 0.7 fusion.67
  27.6 0.1 reshape.89
  27.7 0.8 constant_dynamic-slice_fusion.1
  28.5 0.8 dynamic-slice_convert_fusion
  29.2 1.3 collective-permute-start.3
  30.5 0.7 pad_add_fusion
  31.2 0.6 gather_fusion.1
  31.8 0.6 gather_fusion
  32.4 0.4 select_reduce_fusion
  32.9 0.1 reshape.117
  33.0 0.4 fusion.66
  33.4 1.3 collective-permute-done.4
  34.7 1.0 copy-done
  35.7 2.9 %collective-permute-done.5 = bf16[4,8,128,128]{3,2,1,0:T(8,128)(2,1)} collective-permute-done((bf16[4,8,128,128]{3,2,1,0:T(8,128)(2,1)}, bf16[4,8,128,128]{3,2,1,0:T(8,128)(2,1)}, u32[]{:S(2)}, u32[]{:S(2)}) %collective-permute-start.5) | collective-permute-done | bytes 1048608 | tf_op jit(solution)/shard_map/ppermute | solution.py:15
  38.6 2.0 pad_maximum_fusion.1
  40.7 3.0 %gather_fusion.3 = bf16[128,128,128]{2,1,0:T(8,128)(2,1)} fusion(bf16[96,128,128]{2,1,0:T(8,128)(2,1)S(1)} %bitcast.146, s32[1024]{0:T(1024)S(1)} %pad_clamp_fusion), kind=kCustom, calls=%fused_computation.1.clone | custom fusion | bytes 8389120 | tf_op jit(solution)/shard_map/jit(_take)/gather | solution.py:52
  43.7 6.4 %copy.23 = bf16[128,128,128]{1,2,0:T(8,128)(2,1)} copy(bf16[128,128,128]{2,1,0:T(8,128)(2,1)} %gather_fusion.3) | data formatting | bytes 8388608 | tf_op jit(solution)/shard_map/jit(_take)/gather | solution.py:52
  50.1 4.9 %fusion.55 = bf16[4,4,128,128]{3,2,1,0:T(8,128)(2,1)} fusion(bf16[4,4,8,128,128]{3,4,2,1,0:T(8,128)(2,1)} %bitcast.153, pred[4,4,8]{2,1,0:T(4,128)(4,1)S(1)} %get-tuple-element.6, pred[4,4,8]{2,1,0:T(4,128)(4,1)S(1)} %fusion.66, bf16[4,8,128,128]{3,2,1,0:T(8,128)(2,1)} %add_convert_fusion, f32[4,4]{1,0:T(4,128)S(1)} %dynamic-slice_convert_fusion), kind=kOutput, calls=%fused_computation.70 | convolution fusion | flops 541589504 | bytes 5767488 | tf_op jit(solution)/shard_map/itab,istbc->isac/dot_general | solution.py:54
  55.0 0.0 all-gather.6.cloned.1.call-update
  55.0 0.0 all-gather.8.cloned.1.call-start
  55.1 0.1 constant_dynamic-slice_fusion
  55.2 2.0 collective-permute-done.2
  57.2 3.9 %collective-permute-done.3 = bf16[4,8,128,128]{3,2,1,0:T(8,128)(2,1)} collective-permute-done((bf16[4,8,128,128]{3,2,1,0:T(8,128)(2,1)}, bf16[4,8,128,128]{3,2,1,0:T(8,128)(2,1)}, u32[]{:S(2)}, u32[]{:S(2)}) %collective-permute-start.3) | collective-permute-done | bytes 1048608 | tf_op jit(solution)/shard_map/ppermute | solution.py:15
  61.1 2.0 pad_maximum_fusion
  63.1 3.1 %gather_fusion.2 = bf16[128,128,128]{2,1,0:T(8,128)(2,1)} fusion(bf16[96,128,128]{2,1,0:T(8,128)(2,1)S(1)} %bitcast.144, s32[1024]{0:T(1024)S(1)} %pad_clamp_fusion), kind=kCustom, calls=%fused_computation.clone | custom fusion | bytes 8389120 | tf_op jit(solution)/shard_map/jit(_take)/gather | solution.py:52
  66.2 6.3 %copy.22 = bf16[128,128,128]{1,2,0:T(8,128)(2,1)} copy(bf16[128,128,128]{2,1,0:T(8,128)(2,1)} %gather_fusion.2) | data formatting | bytes 8388608 | tf_op jit(solution)/shard_map/jit(_take)/gather | solution.py:52
  72.6 19.8 %all-gather.6.cloned.1.call-done = bf16[4,8,128,128]{3,2,1,0:T(8,128)(2,1)} async-done(((bf16[4,4,128,128]{3,2,1,0:T(8,128)(2,1)}), bf16[4,8,128,128]{3,2,1,0:T(8,128)(2,1)}) %all-gather.6.cloned.1.call-update) | async-done | bytes 1048592 | tf_op jit(solution)/shard_map/all_gather | solution.py:80
  92.4 4.9 %fusion.53 = bf16[4,4,128,128]{3,2,1,0:T(8,128)(2,1)} fusion(bf16[4,4,8,128,128]{3,4,2,1,0:T(8,128)(2,1)} %bitcast.152, pred[4,4,8]{2,1,0:T(4,128)(4,1)S(1)} %get-tuple-element.6, pred[4,4,8]{2,1,0:T(4,128)(4,1)S(1)} %fusion.66, bf16[4,8,128,128]{3,2,1,0:T(8,128)(2,1)} %all-gather.6.cloned.1.call-done, f32[4,4]{1,0:T(4,128)S(1)} %dynamic-slice_convert_fusion, ...), kind=kOutput, calls=%fused_computation.68 | convolution fusion | flops 542900224 | bytes 5833088 | tf_op jit(solution)/shard_map/itab,istbc->isac/dot_general | solution.py:54
  97.3 0.0 all-gather.10.cloned.1.call-start
  97.4 18.6 %all-gather.8.cloned.1.call-done = bf16[4,8,128,128]{3,2,1,0:T(8,128)(2,1)} async-done(((bf16[4,4,128,128]{3,2,1,0:T(8,128)(2,1)}), bf16[4,8,128,128]{3,2,1,0:T(8,128)(2,1)}) %all-gather.8.cloned.1.call-update) | async-done | bytes 1048592 | tf_op jit(solution)/shard_map/all_gather | solution.py:80
  115.9 2.2 collective-permute-start.6
  118.1 1.3 collective-permute-start.7
  119.4 21.3 %collective-permute-done.6 = bf16[4,8,128,128]{3,2,1,0:T(8,128)(2,1)S(1)} collective-permute-done((bf16[4,8,128,128]{3,2,1,0:T(8,128)(2,1)}, bf16[4,8,128,128]{3,2,1,0:T(8,128)(2,1)S(1)}, u32[]{:S(2)}, u32[]{:S(2)}) %collective-permute-start.6) | collective-permute-done | bytes 1048608 | tf_op jit(solution)/shard_map/ppermute | solution.py:15
  140.7 3.8 %collective-permute-done.7 = bf16[4,8,128,128]{3,2,1,0:T(8,128)(2,1)S(1)} collective-permute-done((bf16[4,8,128,128]{3,2,1,0:T(8,128)(2,1)}, bf16[4,8,128,128]{3,2,1,0:T(8,128)(2,1)S(1)}, u32[]{:S(2)}, u32[]{:S(2)}) %collective-permute-start.7) | collective-permute-done | bytes 1048608 | tf_op jit(solution)/shard_map/ppermute | solution.py:15
  144.4 1.4 pad_maximum_fusion.2
  145.9 3.1 %gather_fusion.4 = bf16[128,128,128]{2,1,0:T(8,128)(2,1)} fusion(bf16[96,128,128]{2,1,0:T(8,128)(2,1)S(1)} %bitcast.147, s32[1024]{0:T(1024)S(1)} %pad_clamp_fusion), kind=kCustom, calls=%fused_computation.2.clone | custom fusion | bytes 8389120 | tf_op jit(solution)/shard_map/jit(_take)/gather | solution.py:52
  149.0 6.4 %copy.25 = bf16[128,128,128]{1,2,0:T(8,128)(2,1)} copy(bf16[128,128,128]{2,1,0:T(8,128)(2,1)} %gather_fusion.4) | data formatting | bytes 8388608 | tf_op jit(solution)/shard_map/jit(_take)/gather | solution.py:52
  155.4 4.6 %fusion.56 = bf16[4,4,128,128]{3,2,1,0:T(8,128)(2,1)} fusion(bf16[4,4,8,128,128]{3,4,2,1,0:T(8,128)(2,1)} %bitcast.150, pred[4,4,8]{2,1,0:T(4,128)(4,1)S(1)} %get-tuple-element.6, pred[4,4,8]{2,1,0:T(4,128)(4,1)S(1)} %fusion.66, bf16[4,8,128,128]{3,2,1,0:T(8,128)(2,1)S(1)} %copy-done.2, f32[4,4]{1,0:T(4,128)S(1)} %dynamic-slice_convert_fusion), kind=kOutput, calls=%fused_computation.71 | convolution fusion | flops 541589504 | bytes 5767488 | tf_op jit(solution)/shard_map/itab,istbc->isac/dot_general | solution.py:54
  160.0 0.0 all-gather.10.cloned.1.call-update
  160.0 0.0 all-gather.12.cloned.1.call-start
  160.1 22.7 %all-gather.10.cloned.1.call-done = bf16[4,8,128,128]{3,2,1,0:T(8,128)(2,1)} async-done(((bf16[4,4,128,128]{3,2,1,0:T(8,128)(2,1)}), bf16[4,8,128,128]{3,2,1,0:T(8,128)(2,1)}) %all-gather.10.cloned.1.call-update) | async-done | bytes 1048592 | tf_op jit(solution)/shard_map/all_gather | solution.py:80
  182.8 5.0 %fusion.47 = bf16[4,4,128,128]{3,2,1,0:T(8,128)(2,1)} fusion(bf16[4,4,8,128,128]{3,4,2,1,0:T(8,128)(2,1)} %bitcast.151, pred[4,4,8]{2,1,0:T(4,128)(4,1)S(1)} %get-tuple-element.6, pred[4,4,8]{2,1,0:T(4,128)(4,1)S(1)} %fusion.66, bf16[4,8,128,128]{3,2,1,0:T(8,128)(2,1)} %all-gather.10.cloned.1.call-done, s32[]{:T(128)S(6)} %select_n.63, ...), kind=kOutput, calls=%fused_computation.62 | convolution fusion | flops 543162368 | bytes 6291780 | tf_op jit(solution)/shard_map/itab,istbc->isac/dot_general | solution.py:54
  187.8 0.0 all-gather.12.cloned.1.call-update
  187.9 0.0 all-gather.14.cloned.1.call-start
  187.9 18.6 %all-gather.12.cloned.1.call-done = bf16[4,8,128,128]{3,2,1,0:T(8,128)(2,1)} async-done(((bf16[4,4,128,128]{3,2,1,0:T(8,128)(2,1)}), bf16[4,8,128,128]{3,2,1,0:T(8,128)(2,1)}) %all-gather.12.cloned.1.call-update) | async-done | bytes 1048592 | tf_op jit(solution)/shard_map/all_gather | solution.py:80
  206.5 2.2 collective-permute-start.8
  208.6 1.5 collective-permute-start.9
  210.1 21.1 %collective-permute-done.8 = bf16[4,8,128,128]{3,2,1,0:T(8,128)(2,1)S(1)} collective-permute-done((bf16[4,8,128,128]{3,2,1,0:T(8,128)(2,1)}, bf16[4,8,128,128]{3,2,1,0:T(8,128)(2,1)S(1)}, u32[]{:S(2)}, u32[]{:S(2)}) %collective-permute-start.8) | collective-permute-done | bytes 1048608 | tf_op jit(solution)/shard_map/ppermute | solution.py:15
  231.2 3.8 %collective-permute-done.9 = bf16[4,8,128,128]{3,2,1,0:T(8,128)(2,1)S(1)} collective-permute-done((bf16[4,8,128,128]{3,2,1,0:T(8,128)(2,1)}, bf16[4,8,128,128]{3,2,1,0:T(8,128)(2,1)S(1)}, u32[]{:S(2)}, u32[]{:S(2)}) %collective-permute-start.9) | collective-permute-done | bytes 1048608 | tf_op jit(solution)/shard_map/ppermute | solution.py:15
  235.0 1.4 pad_maximum_fusion.3
  236.4 3.1 %gather_fusion.5 = bf16[128,128,128]{2,1,0:T(8,128)(2,1)} fusion(bf16[96,128,128]{2,1,0:T(8,128)(2,1)S(1)} %bitcast.145, s32[1024]{0:T(1024)S(1)} %pad_clamp_fusion), kind=kCustom, calls=%fused_computation.3.clone | custom fusion | bytes 8389120 | tf_op jit(solution)/shard_map/jit(_take)/gather | solution.py:52
  239.5 6.4 %copy.28 = bf16[128,128,128]{1,2,0:T(8,128)(2,1)} copy(bf16[128,128,128]{2,1,0:T(8,128)(2,1)} %gather_fusion.5) | data formatting | bytes 8388608 | tf_op jit(solution)/shard_map/jit(_take)/gather | solution.py:52
  245.9 4.6 %fusion.57 = bf16[4,4,128,128]{3,2,1,0:T(8,128)(2,1)} fusion(bf16[4,4,8,128,128]{3,4,2,1,0:T(8,128)(2,1)} %bitcast.148, pred[4,4,8]{2,1,0:T(4,128)(4,1)S(1)} %get-tuple-element.6, pred[4,4,8]{2,1,0:T(4,128)(4,1)S(1)} %fusion.66, bf16[4,8,128,128]{3,2,1,0:T(8,128)(2,1)S(1)} %copy-done.1, f32[4,4]{1,0:T(4,128)S(1)} %dynamic-slice_convert_fusion), kind=kOutput, calls=%fused_computation.72 | convolution fusion | flops 541589504 | bytes 5767488 | tf_op jit(solution)/shard_map/itab,istbc->isac/dot_general | solution.py:54
  250.6 22.8 %all-gather.14.cloned.1.call-done = bf16[4,8,128,128]{3,2,1,0:T(8,128)(2,1)} async-done(((bf16[4,4,128,128]{3,2,1,0:T(8,128)(2,1)}), bf16[4,8,128,128]{3,2,1,0:T(8,128)(2,1)}) %all-gather.14.cloned.1.call-update) | async-done | bytes 1048592 | tf_op jit(solution)/shard_map/all_gather | solution.py:80
  273.4 5.0 %fusion.40 = bf16[4,4,128,128]{3,2,1,0:T(8,128)(2,1)} fusion(bf16[4,4,8,128,128]{3,4,2,1,0:T(8,128)(2,1)} %bitcast.149, pred[4,4,8]{2,1,0:T(4,128)(4,1)S(1)} %get-tuple-element.6, pred[4,4,8]{2,1,0:T(4,128)(4,1)S(1)} %fusion.66, bf16[4,8,128,128]{3,2,1,0:T(8,128)(2,1)} %all-gather.14.cloned.1.call-done, s32[]{:T(128)S(6)} %select_n.63, ...), kind=kOutput, calls=%fused_computation.55 | convolution fusion | flops 543162368 | bytes 6291780 | tf_op jit(solution)/shard_map/itab,istbc->isac/dot_general | solution.py:54
  (18 shorter events, 0.1 us)
Async XLA Ops:
  6.5 85.8 %all-gather.6.cloned.1.call-start = ((), (), s32[]{:S(2)}) async-start(), calls=%async_computation | async-start | bytes 1572864 | tf_op jit(solution)/shard_map/all_gather | solution.py:80
  7.2 22.0 %collective-permute-start = (s32[4,2,8]{2,0,1:T(4,128)S(1)}, s32[4,2,8]{2,0,1:T(4,128)S(1)}, u32[]{:S(2)}, u32[]{:S(2)}) collective-permute-start(s32[4,2,8]{2,0,1:T(4,128)S(1)} %pad_add_fusion.1), channel_id=1, source_target_pairs={{0,2},{2,4},{4,6},{6,8},{8,10},{10,12},{12,14},{14,16},{16,18},{18... | collective-permute-start | bytes 776 | tf_op jit(solution)/shard_map/ppermute | solution.py:15
  11.2 19.3 %collective-permute-start.1 = (s32[4,2,8]{2,0,1:T(4,128)S(1)}, s32[4,2,8]{2,0,1:T(4,128)S(1)}, u32[]{:S(2)}, u32[]{:S(2)}) collective-permute-start(s32[4,2,8]{2,0,1:T(4,128)S(1)} %pad_add_fusion.1), channel_id=1, source_target_pairs={{2,0},{4,2},{6,4},{8,6},{10,8},{12,10},{14,12},{16,14},{18,16},{20... | collective-permute-start | bytes 776 | tf_op jit(solution)/shard_map/ppermute | solution.py:15
  12.5 22.2 %collective-permute-start.4 = (bf16[4,8,128,128]{3,2,1,0:T(8,128)(2,1)}, bf16[4,8,128,128]{3,2,1,0:T(8,128)(2,1)S(1)}, u32[]{:S(2)}, u32[]{:S(2)}) collective-permute-start(bf16[4,8,128,128]{3,2,1,0:T(8,128)(2,1)} %param.6), channel_id=1, source_target_pairs={{0,2},{2,4},{4,6},{6,8},{8,10},{10,12},{12,14},{14,16},{16,18},{18... | collective-permute-start | bytes 3145736 | tf_op jit(solution)/shard_map/ppermute | solution.py:15
  16.5 22.1 %collective-permute-start.5 = (bf16[4,8,128,128]{3,2,1,0:T(8,128)(2,1)}, bf16[4,8,128,128]{3,2,1,0:T(8,128)(2,1)}, u32[]{:S(2)}, u32[]{:S(2)}) collective-permute-start(bf16[4,8,128,128]{3,2,1,0:T(8,128)(2,1)} %param.6), channel_id=1, source_target_pairs={{2,0},{4,2},{6,4},{8,6},{10,8},{12,10},{14,12},{16,14},{18,16},{20... | collective-permute-start | bytes 3145736 | tf_op jit(solution)/shard_map/ppermute | solution.py:15
  21.3 35.9 %collective-permute-start.2 = (bf16[4,8,128,128]{3,2,1,0:T(8,128)(2,1)}, bf16[4,8,128,128]{3,2,1,0:T(8,128)(2,1)}, u32[]{:S(2)}, u32[]{:S(2)}) collective-permute-start(bf16[4,8,128,128]{3,2,1,0:T(8,128)(2,1)} %add_convert_fusion), channel_id=1, source_target_pairs={{0,2},{2,4},{4,6},{6,8},{8,10},{10,12},{12,14},{14,16},{16,18},{18... | collective-permute-start | bytes 3145736 | tf_op jit(solution)/shard_map/ppermute | solution.py:15
  29.2 31.9 %collective-permute-start.3 = (bf16[4,8,128,128]{3,2,1,0:T(8,128)(2,1)}, bf16[4,8,128,128]{3,2,1,0:T(8,128)(2,1)}, u32[]{:S(2)}, u32[]{:S(2)}) collective-permute-start(bf16[4,8,128,128]{3,2,1,0:T(8,128)(2,1)} %add_convert_fusion), channel_id=1, source_target_pairs={{2,0},{4,2},{6,4},{8,6},{10,8},{12,10},{14,12},{16,14},{18,16},{20... | collective-permute-start | bytes 3145736 | tf_op jit(solution)/shard_map/ppermute | solution.py:15
  34.7 1.0 copy-start
  55.0 60.9 %all-gather.8.cloned.1.call-start = ((), (), s32[]{:S(2)}) async-start(), calls=%async_computation.1 | async-start | bytes 1572864 | tf_op jit(solution)/shard_map/all_gather | solution.py:80
  97.3 85.5 %all-gather.10.cloned.1.call-start = ((), (), s32[]{:S(2)}) async-start(), calls=%async_computation.2 | async-start | bytes 1572864 | tf_op jit(solution)/shard_map/all_gather | solution.py:80
  115.9 24.7 %collective-permute-start.6 = (bf16[4,8,128,128]{3,2,1,0:T(8,128)(2,1)}, bf16[4,8,128,128]{3,2,1,0:T(8,128)(2,1)S(1)}, u32[]{:S(2)}, u32[]{:S(2)}) collective-permute-start(bf16[4,8,128,128]{3,2,1,0:T(8,128)(2,1)} %all-gather.8.cloned.1.call-done), channel_id=1, source_target_pairs={{0,2},{2,4},{4,6},{6,8},{8,10},{10,12},{12,14},{14,16},{16,18},{18... | collective-permute-start | bytes 3145736 | tf_op jit(solution)/shard_map/ppermute | solution.py:15
  118.1 26.3 %collective-permute-start.7 = (bf16[4,8,128,128]{3,2,1,0:T(8,128)(2,1)}, bf16[4,8,128,128]{3,2,1,0:T(8,128)(2,1)S(1)}, u32[]{:S(2)}, u32[]{:S(2)}) collective-permute-start(bf16[4,8,128,128]{3,2,1,0:T(8,128)(2,1)} %all-gather.8.cloned.1.call-done), channel_id=1, source_target_pairs={{2,0},{4,2},{6,4},{8,6},{10,8},{12,10},{14,12},{16,14},{18,16},{20... | collective-permute-start | bytes 3145736 | tf_op jit(solution)/shard_map/ppermute | solution.py:15
  149.0 6.4 %copy-start.2 = (bf16[4,8,128,128]{3,2,1,0:T(8,128)(2,1)S(1)}, bf16[4,8,128,128]{3,2,1,0:T(8,128)(2,1)}, u32[]{:S(2)}) copy-start(bf16[4,8,128,128]{3,2,1,0:T(8,128)(2,1)} %all-gather.8.cloned.1.call-done) | copy-start | bytes 3145732
  160.0 46.5 %all-gather.12.cloned.1.call-start = ((), (), s32[]{:S(2)}) async-start(), calls=%async_computation.3 | async-start | bytes 1572864 | tf_op jit(solution)/shard_map/all_gather | solution.py:80
  187.9 85.5 %all-gather.14.cloned.1.call-start = ((), (), s32[]{:S(2)}) async-start(), calls=%async_computation.4 | async-start | bytes 1572864 | tf_op jit(solution)/shard_map/all_gather | solution.py:80
  206.5 24.7 %collective-permute-start.8 = (bf16[4,8,128,128]{3,2,1,0:T(8,128)(2,1)}, bf16[4,8,128,128]{3,2,1,0:T(8,128)(2,1)S(1)}, u32[]{:S(2)}, u32[]{:S(2)}) collective-permute-start(bf16[4,8,128,128]{3,2,1,0:T(8,128)(2,1)} %all-gather.12.cloned.1.call-done), channel_id=1, source_target_pairs={{0,2},{2,4},{4,6},{6,8},{8,10},{10,12},{12,14},{14,16},{16,18},{18... | collective-permute-start | bytes 3145736 | tf_op jit(solution)/shard_map/ppermute | solution.py:15
  208.6 26.3 %collective-permute-start.9 = (bf16[4,8,128,128]{3,2,1,0:T(8,128)(2,1)}, bf16[4,8,128,128]{3,2,1,0:T(8,128)(2,1)S(1)}, u32[]{:S(2)}, u32[]{:S(2)}) collective-permute-start(bf16[4,8,128,128]{3,2,1,0:T(8,128)(2,1)} %all-gather.12.cloned.1.call-done), channel_id=1, source_target_pairs={{2,0},{4,2},{6,4},{8,6},{10,8},{12,10},{14,12},{16,14},{18,16},{20... | collective-permute-start | bytes 3145736 | tf_op jit(solution)/shard_map/ppermute | solution.py:15
  239.5 6.4 %copy-start.1 = (bf16[4,8,128,128]{3,2,1,0:T(8,128)(2,1)S(1)}, bf16[4,8,128,128]{3,2,1,0:T(8,128)(2,1)}, u32[]{:S(2)}) copy-start(bf16[4,8,128,128]{3,2,1,0:T(8,128)(2,1)} %all-gather.12.cloned.1.call-done) | copy-start | bytes 3145732
Sparse Core Ops, SparseCore 0:
  55.1 37.1 all-gather.5
  97.4 18.4 all-gather.7
  160.1 22.6 all-gather.9
  188.0 18.4 all-gather.11
  250.7 22.6 all-gather.13
where the time goes:
time: 286 us; the launch traced here: 285 us
  waiting for transfers between devices  163 us (57%)
  local copies, waits for them, and re-layouts  41.1 us (14%)
  matrix products  29 us (10%)
  starting transfers between devices  24.1 us (8%)
  other arithmetic  14.8 us (5%)
  between operations  13.3 us (5%)
    all_gather x5, waiting for transfers between devices, whole(): return lax.all_gather(part, 'rep', axis=1, tiled=True)  102 us
    ppermute x10, waiting for transfers between devices, passed_along(): return lax.ppermute(x, axis, pairs)  60.1 us
    gather x8, local copies, waits for them, and re-layouts, multiply(): jnp.take(band.reshape(band_rows * slots, size, size), flat_index, axis=0)  38 us
    dot_general x6, matrix products, multiply(): jnp.einsum('itab,istbc->isac', left, picked, preferred_element_type=jnp.f...  29 us
    ppermute x10, starting transfers between devices, passed_along(): return lax.ppermute(x, axis, pairs)  23.9 us
    concatenate x5, other arithmetic, assemble(): joined = jnp.concatenate(pieces[:reach] + [values] + pieces[reach:], axis=0)  7.6 us
  transfers between devices with their start and end apart: 15, of which 13 were waited for; matrix products, arithmetic and copies ran while one was open for 13% of the time, Pallas kernels for 0%

commit v1 on v0

v1 whole, which is shorter than its diff:
```python
import math

import jax
import jax.numpy as jnp
from jax import lax
from jax.experimental import pallas as pl
from jax.experimental.pallas import tpu as pltpu
from jax.sharding import PartitionSpec as P

BAND = 4
STEPS = 2
S = 128
Q = 4 * S
H = 2 * S
TRI = [(p, m) for p in range(4) for m in range(p, 4)]
BF = jnp.bfloat16
F32 = jnp.float32
LEFT, OWN, RIGHT = (0, 1), (2, 3), (4, 5)

VMEM = pl.BlockSpec(memory_space=pltpu.VMEM)
SMEM = pl.BlockSpec(memory_space=pltpu.SMEM)
SQUARE = jax.ShapeDtypeStruct((Q, Q), BF)
CORNER = jax.ShapeDtypeStruct((len(TRI), S, S), BF)
BANDED = jax.ShapeDtypeStruct((Q, 3 * Q), BF)


def call(kernel, outs, out_specs, in_specs, scratch, flops, *args):
    return pl.pallas_call(
        kernel,
        out_shape=outs,
        in_specs=in_specs,
        out_specs=out_specs,
        scratch_shapes=scratch,
        compiler_params=pltpu.CompilerParams(vmem_limit_bytes=24 * 1024 * 1024),
        cost_estimate=pl.CostEstimate(flops=flops, bytes_accessed=4 << 20, transcendentals=0),
    )(*args)


def place(cols_ref, mask_ref, a, s):
    first = lax.axis_index("rows") * 4 - BAND
    core = lax.axis_index("rep")
    k = cols_ref[a, s] - first
    k = jnp.clip(k, 0, 11)
    k = jnp.where(core == 1, 11 - k, k)
    row = jnp.where(core == 1, 3 - a, a)
    t = jnp.where(k < 4, 3 - k, k)
    return mask_ref[a, s] == 1, row, t


def at(index):
    return pl.ds(pl.multiple_of(index * S, S), S)


def corner_index(p, m):
    return ((p * (7 - p)) >> 1) + m


def eye():
    rows = lax.broadcasted_iota(jnp.int32, (S, S), 0)
    cols = lax.broadcasted_iota(jnp.int32, (S, S), 1)
    return (rows == cols).astype(F32)


def send_slots(cols_ref, mask_ref, block_of, a_ref, b_ref):
    a_ref[...] = jnp.zeros_like(a_ref)
    b_ref[...] = jnp.zeros_like(b_ref)
    for a in range(4):
        for s in range(8):
            active, row, t = place(cols_ref, mask_ref, a, s)

            @pl.when(active & (t >= 4) & (t < 8))
            def _():
                b_ref[at(3 - row), at(jnp.clip(7 - t, 0, 3))] = block_of(a, s)

            @pl.when(active & (t >= 8))
            def _():
                index = corner_index(3 - row, 11 - t)
                a_ref[jnp.clip(index, 0, 9)] = block_of(a, s)


def pack_h(cols_ref, mask_ref, h_ref, a_ref, b_ref):
    send_slots(cols_ref, mask_ref, lambda a, s: h_ref[a, s], a_ref, b_ref)


def pack_x(cols_ref, mask_ref, h_ref, x_ref, xa_ref, xb_ref, ho_ref, xo_ref, table_ref):
    diag = eye()

    def x_block(a, s):
        if s == 0:
            return (x_ref[a, s].astype(F32) + diag).astype(BF)
        return x_ref[a, s]

    send_slots(cols_ref, mask_ref, x_block, xa_ref, xb_ref)
    ho_ref[...] = jnp.zeros_like(ho_ref)
    xo_ref[...] = jnp.zeros_like(xo_ref)
    for a in range(4):
        for t in range(12):
            table_ref[a, t] = 0
    for a in range(4):
        for s in range(8):
            active, row, t = place(cols_ref, mask_ref, a, s)

            @pl.when(active)
            def _():
                ho_ref[at(row), at(t)] = h_ref[a, s]
                xo_ref[at(row), at(t)] = x_block(a, s)
                table_ref[row, t] = 1


def spread_mine(corner_ref, square_ref):
    square_ref[H:, :H] = jnp.zeros((H, H), BF)
    square_ref[S : 2 * S, :S] = jnp.zeros((S, S), BF)
    square_ref[3 * S :, H : 3 * S] = jnp.zeros((S, S), BF)
    for index, (p, m) in enumerate(TRI):
        square_ref[p * S : (p + 1) * S, m * S : (m + 1) * S] = corner_ref[index]


def spread_twin(corner_ref, square_ref):
    square_ref[H:, H:] = jnp.zeros((H, H), BF)
    square_ref[S : 2 * S, 3 * S :] = jnp.zeros((S, S), BF)
    square_ref[3 * S :, S:H] = jnp.zeros((S, S), BF)
    for index, (p, m) in enumerate(TRI):
        square_ref[p * S : (p + 1) * S, (3 - m) * S : (4 - m) * S] = corner_ref[index]


def tile(ref, i, j):
    return ref[i * H : (i + 1) * H, j * H : (j + 1) * H]


def right_operand(ll, lc, own, rc, rr):
    def get(t, u):
        if t in OWN:
            if (t, u) in ((3, 1), (2, 5)):
                return None
            return own(t - 2, u)
        if t in LEFT:
            if u in LEFT:
                return tile(ll, t, u)
            if u in OWN and (t, u) != (1, 3):
                return tile(lc, t, u - 2)
            return None
        if u in RIGHT:
            return tile(rr, t - 4, u - 4)
        if u in OWN and (t, u) != (5, 2):
            return tile(rc, t - 4, u - 2)
        return None

    return get


def left_tile(ref, r, t):
    if (r, t) in ((1, 1), (0, 5)):
        return None
    return tile(ref, r, t)


def product(left, right, columns, finish):
    for u in columns:
        for r in range(2):
            if (r, u) in ((1, 1), (0, 5)):
                continue
            total = None
            for t in range(6):
                x = left(r, t)
                y = right(t, u)
                if x is None or y is None:
                    continue
                term = jnp.dot(x, y, preferred_element_type=F32)
                total = term if total is None else total + term
            finish(r, u, total)


def each_block(table_ref, r, u, total, store):
    for i in range(2):
        for j in range(2):
            row, t = 2 * r + i, 2 * u + j
            block = total[i * S : (i + 1) * S, j * S : (j + 1) * S]
            block = jnp.where(table_ref[row, t] == 1, block, 0.0)
            store(row, t, block)


def put(ref, row, t, block):
    ref[row * S : (row + 1) * S, t * S : (t + 1) * S] = block


def put_square(ref, send_ref, row, t, block):
    put(ref, row, t - 4, block)
    put(send_ref, 3 - row, 7 - t, block)


def put_corner(ref, send_ref, row, t, block):
    put(ref, row, t - 8, block)
    p, m = 3 - row, 11 - t
    if m >= p:
        send_ref[TRI.index((p, m))] = block


def half_kernel(factor, table, xo, ho, hb, ha, hb2, ha2, xa, xa2, half_ref, pc_ref, sb_ref, lc, rc, xlc, xrc):
    spread_mine(ha, rc)
    spread_twin(ha2, lc)
    spread_mine(xa, xrc)
    spread_twin(xa2, xlc)
    half_ref[H:, H:Q] = jnp.zeros((H, H), BF)
    half_ref[:H, 2 * Q + H :] = jnp.zeros((H, H), BF)
    right = right_operand(hb2, lc, lambda r, u: tile(ho, r, u), rc, hb)

    def keep(r, u, total):
        each_block(table, r, u, total, lambda row, t, b: put(half_ref, row, t, b.astype(BF)))

    product(lambda r, t: left_tile(xo, r, t), right, range(6), keep)
    right = right_operand(None, xlc, lambda r, u: tile(xo, r, u), xrc, None)
    diag = eye()

    def start(r, u, total):
        def store(row, t, block):
            value = -factor * block
            if t - 4 == row:
                value = value + 0.5 * diag
            put_square(pc_ref, sb_ref, row, t, value.astype(BF))

        each_block(table, r, u, total, store)

    product(lambda r, t: left_tile(half_ref, r, t), right, OWN, start)


def side_kernel(factor, table, half, xo, xb, pr_ref, sa_ref):
    pr_ref[:H, H:] = jnp.zeros((H, H), BF)
    right = right_operand(None, None, lambda r, u: tile(xo, r, u), None, xb)

    def start(r, u, total):
        each_block(
            table,
            r,
            u,
            total,
            lambda row, t, b: put_corner(pr_ref, sa_ref, row, t, (-factor * b).astype(BF)),
        )

    product(lambda r, t: left_tile(half, r, t), right, RIGHT, start)


def squares(table, pc, pr, sa2, hb, ha, hb2, ha2, band, sq, lc, rc):
    spread_mine(ha, rc)
    spread_twin(ha2, lc)
    spread_twin(sa2, band.at[:, :Q])
    band[:, Q : 2 * Q] = pc[...]
    band[:, 2 * Q :] = pr[...]
    right = right_operand(hb2, lc, lambda r, u: tile(band, r, u), rc, hb)

    def keep(r, u, total):
        each_block(table, r, u, total, lambda row, t, b: put(sq, row, t, b.astype(BF)))

    product(lambda r, t: left_tile(band, r, t), right, range(6), keep)
    return right


def blocks_of(sq, row, t):
    return sq[row * S : (row + 1) * S, t * S : (t + 1) * S].astype(F32)


def step_kernel(table, pc, pr, sa2, hb, ha, hb2, ha2, nc_ref, nr_ref, sb_ref, sa_ref, band, sq, lc, rc):
    right = squares(table, pc, pr, sa2, hb, ha, hb2, ha2, band, sq, lc, rc)
    nr_ref[:H, H:] = jnp.zeros((H, H), BF)

    def step(r, u, total):
        def store(row, t, block):
            value = (3.0 * blocks_of(sq, row, t) - 2.0 * block).astype(BF)
            if u in OWN:
                put_square(nc_ref, sb_ref, row, t, value)
            else:
                put_corner(nr_ref, sa_ref, row, t, value)

        each_block(table, r, u, total, store)

    product(lambda r, t: left_tile(sq, r, t), right, RIGHT + OWN, step)


def last_kernel(cols_ref, mask_ref, table, pc, pr, sa2, hb, ha, hb2, ha2, out_ref, band, sq, lc, rc, res):
    right = squares(table, pc, pr, sa2, hb, ha, hb2, ha2, band, sq, lc, rc)

    def step(r, u, total):
        def store(row, t, block):
            put(res, row, t, (3.0 * blocks_of(sq, row, t) - 2.0 * block).astype(BF))

        each_block(table, r, u, total, store)

    product(lambda r, t: left_tile(sq, r, t), right, range(6), step)
    core = lax.axis_index("rep")
    for a in range(4):
        for s in range(4):
            active, row, t = place(cols_ref, mask_ref, a, core * 4 + s)

            @pl.when(active)
            def _():
                out_ref[a, s] = res[at(row), at(t)]

            @pl.when(jnp.logical_not(active))
            def _():
                out_ref[a, s] = jnp.zeros((S, S), BF)


def on_device(hamiltonian, x_correction, cols, mask):
    n = lax.axis_size("rows")
    factor = 0.6 / math.sqrt(cols.shape[1] * hamiltonian.shape[-1])
    outward = [(2 * i, 2 * i + 3) for i in range(n - 1)] + [(2 * i + 1, 2 * i - 2) for i in range(1, n)]

    def link(x):
        return lax.ppermute(x, ("rows", "rep"), outward)

    def swap(x):
        return lax.ppermute(x, "rep", [(0, 1), (1, 0)])

    square = pltpu.VMEM((Q, Q), BF)
    band = pltpu.VMEM((Q, 3 * Q), BF)
    sum_flops = 1 << 30

    ha, hb = call(pack_h, [CORNER, SQUARE], [VMEM] * 2, [SMEM, SMEM, VMEM], [], 0, cols, mask, hamiltonian)
    hb_in = link(hb)
    ha_in = link(ha)
    xa, xb, ho, xo, table = call(
        pack_x,
        [CORNER, SQUARE, BANDED, BANDED, jax.ShapeDtypeStruct((4, 12), jnp.int32)],
        [VMEM] * 4 + [SMEM],
        [SMEM, SMEM, VMEM, VMEM],
        [],
        0,
        cols,
        mask,
        hamiltonian,
        x_correction,
    )
    xa_in = link(xa)
    xb_in = link(xb)
    hb_twin = swap(hb_in)
    ha_twin = swap(ha_in)
    xa_twin = swap(xa_in)
    half, pc, sb = call(
        lambda *refs: half_kernel(factor, *refs),
        [BANDED, SQUARE, SQUARE],
        [VMEM] * 3,
        [SMEM] + [VMEM] * 8,
        [square] * 4,
        sum_flops,
        table, xo, ho, hb_in, ha_in, hb_twin, ha_twin, xa_in, xa_twin,
    )
    b_in = link(sb)
    pr, sa = call(
        lambda *refs: side_kernel(factor, *refs),
        [SQUARE, CORNER],
        [VMEM] * 2,
        [SMEM] + [VMEM] * 3,
        [],
        sum_flops,
        table, half, xo, xb_in,
    )
    a_in = link(sa)
    for step in range(STEPS):
        a_own = swap(sa)
        b_twin = swap(b_in)
        a_twin = swap(a_in)
        halo = (pc, pr, a_own, b_in, a_in, b_twin, a_twin)
        if step + 1 < STEPS:
            pc, pr, sb, sa = call(
                step_kernel,
                [SQUARE, SQUARE, SQUARE, CORNER],
                [VMEM] * 4,
                [SMEM] + [VMEM] * 7,
                [band, band, square, square],
                2 * sum_flops,
                table, *halo,
            )
            b_in = link(sb)
            a_in = link(sa)
        else:
            return call(
                last_kernel,
                jax.ShapeDtypeStruct((4, 4, S, S), BF),
                VMEM,
                [SMEM] * 3 + [VMEM] * 7,
                [band, band, square, square, band],
                2 * sum_flops,
                cols, mask, table, *halo,
            )


def solution(mesh):
    return jax.shard_map(
        on_device,
        mesh=mesh,
        in_specs=(
            P("rows", None, None, None),
            P("rows", None, None, None),
            P("rows", None),
            P("rows", None),
        ),
        out_specs=P("rows", "rep", None, None),
        check_vma=False,
    )
```

time: 286 us -> 107 us (0.37)
  the two profiles are of different devices: /device:TPU:1 before, /device:TPU:33 now
where the time goes in v1:
time: 107 us; the launch traced here: 106 us
  starting transfers between devices  74.2 us (69%)
  Pallas kernels  15.9 us (15%)
  waiting for transfers between devices  13.5 us (13%)
  local copies, waits for them, and re-layouts  2.6 us (2%)
    ppermute x8, starting transfers between devices, link(): return lax.ppermute(x, ('rows', 'rep'), outward)  55.3 us
    ppermute x9, starting transfers between devices, swap(): return lax.ppermute(x, 'rep', [(0, 1), (1, 0)])  18.9 us
    pallas_call x6, Pallas kernels, call(): pl.pallas_call(kernel, out_shape=outs, in_specs=in_specs, out_specs=out_s...  15.9 us
    ppermute x8, waiting for transfers between devices, link(): return lax.ppermute(x, ('rows', 'rep'), outward)  10.5 us
    ppermute x9, waiting for transfers between devices, swap(): return lax.ppermute(x, 'rep', [(0, 1), (1, 0)])  3.01 us
    unnamed x12, local copies, waits for them, and re-layouts  2.6 us
  transfers between devices with their start and end apart: 17, of which 7 were waited for; matrix products, arithmetic and copies ran while one was open for 0% of the time, Pallas kernels for 6%

profile of v1, /device:TPU:33, one launch (start us, length us, event | category | flops | bytes accessed | tf_op | source)
XLA Modules:
  0.0 106.4 jit_solution(1027686270907448815)
XLA Ops:
  0.0 0.0 copy-start
  0.0 1.2 %copy-done = bf16[4,8,128,128]{3,2,1,0:T(8,128)(2,1)S(1)} copy-done((bf16[4,8,128,128]{3,2,1,0:T(8,128)(2,1)S(1)}, bf16[4,8,128,128]{3,2,1,0:T(8,128)(2,1)}, u32[]{:S(2)}) %copy-start) | copy-done | bytes 1048600
  1.2 0.0 copy-start.2
  1.2 0.7 copy-done.2
  1.9 0.0 copy-start.4
  1.9 0.7 copy-done.4
  2.6 0.0 copy-start.1
  2.6 1.5 %shard_map.47 = (bf16[10,128,128]{2,1,0:T(8,128)(2,1)S(1)}, bf16[512,512]{1,0:T(8,128)(2,1)S(1)}) custom-call(s32[4,8]{1,0:T(4,128)S(1)} %copy-done.2, s32[4,8]{1,0:T(4,128)S(1)} %copy-done.4, bf16[4,8,128,128]{3,2,1,0:T(8,128)(2,1)S(1)} %copy-done), custom_call_target="tpu_custom_call" | custom-call | bytes 4194304 | tf_op jit(solution)/shard_map/pallas_call | solution.py:28
  4.1 13.3 %collective-permute-start = (bf16[512,512]{1,0:T(8,128)(2,1)S(1)}, bf16[512,512]{1,0:T(8,128)(2,1)S(1)}, u32[]{:S(2)}, u32[]{:S(2)}) collective-permute-start(bf16[512,512]{1,0:T(8,128)(2,1)S(1)} %get-tuple-element.24), channel_id=1, source_target_pairs={{0,3},{2,5},{4,7},{6,9},{8,11},{10,13},{12,15},{14,17},{16,19},{18... | collective-permute-start | bytes 1572872 | tf_op jit(solution)/shard_map/ppermute | solution.py:308
  17.4 1.9 %collective-permute-start.1 = (bf16[10,128,128]{2,1,0:T(8,128)(2,1)S(1)}, bf16[10,128,128]{2,1,0:T(8,128)(2,1)S(1)}, u32[]{:S(2)}, u32[]{:S(2)}) collective-permute-start(bf16[10,128,128]{2,1,0:T(8,128)(2,1)S(1)} %get-tuple-element.25), channel_id=1, source_target_pairs={{0,3},{2,5},{4,7},{6,9},{8,11},{10,13},{12,15},{14,17},{16,19},{18... | collective-permute-start | bytes 983048 | tf_op jit(solution)/shard_map/ppermute | solution.py:308
  19.3 0.0 copy-done.1
  19.3 2.8 %shard_map.46 = (bf16[10,128,128]{2,1,0:T(8,128)(2,1)S(1)}, bf16[512,512]{1,0:T(8,128)(2,1)S(1)}, bf16[512,1536]{1,0:T(8,128)(2,1)S(1)}, bf16[512,1536]{1,0:T(8,128)(2,1)S(1)}, s32[4,12]{1,0:T(4,128)S(1)}) custom-call(s32[4,8]{1,0:T(4,128)S(1)} %copy-done.2, s32[4,8]{1,0:T(4,128)S(1)} %copy-done.4, bf16[4,8,128,128]{3,2,1,0:T(8,128)(2,1)S(1)} %copy-done, ...), custom_call_target="tpu_custom_call" | custom-call | bytes 4194304 | tf_op jit(solution)/shard_map/pallas_call | solution.py:28
  22.1 9.1 %collective-permute-start.4 = (bf16[10,128,128]{2,1,0:T(8,128)(2,1)S(1)}, bf16[10,128,128]{2,1,0:T(8,128)(2,1)S(1)}, u32[]{:S(2)}, u32[]{:S(2)}) collective-permute-start(bf16[10,128,128]{2,1,0:T(8,128)(2,1)S(1)} %get-tuple-element.26), channel_id=1, source_target_pairs={{0,3},{2,5},{4,7},{6,9},{8,11},{10,13},{12,15},{14,17},{16,19},{18... | collective-permute-start | bytes 983048 | tf_op jit(solution)/shard_map/ppermute | solution.py:308
  31.2 0.0 collective-permute-done.refs_3_
  31.2 1.9 %collective-permute-start.2 = (bf16[512,512]{1,0:T(8,128)(2,1)S(1)}, bf16[512,512]{1,0:T(8,128)(2,1)S(1)}, u32[]{:S(2)}, u32[]{:S(2)}) collective-permute-start(bf16[512,512]{1,0:T(8,128)(2,1)S(1)} %collective-permute-done.refs_3_), channel_id=1, source_target_pairs={{0,1},{1,0},{2,3},{3,2},{4,5},{5,4},{6,7},{7,6},{8,9},{9,8},{10,11... | collective-permute-start | bytes 1572872 | tf_op jit(solution)/shard_map/ppermute | solution.py:311
  33.1 0.0 collective-permute-done.1.refs_4_
  33.1 2.4 %collective-permute-start.3 = (bf16[10,128,128]{2,1,0:T(8,128)(2,1)S(1)}, bf16[10,128,128]{2,1,0:T(8,128)(2,1)S(1)}, u32[]{:S(2)}, u32[]{:S(2)}) collective-permute-start(bf16[10,128,128]{2,1,0:T(8,128)(2,1)S(1)} %collective-permute-done.1.refs_4_), channel_id=1, source_target_pairs={{0,1},{1,0},{2,3},{3,2},{4,5},{5,4},{6,7},{7,6},{8,9},{9,8},{10,11... | collective-permute-start | bytes 983048 | tf_op jit(solution)/shard_map/ppermute | solution.py:311
  35.5 0.4 collective-permute-done.4.refs_7_
  35.9 1.9 %collective-permute-start.5 = (bf16[10,128,128]{2,1,0:T(8,128)(2,1)S(1)}, bf16[10,128,128]{2,1,0:T(8,128)(2,1)S(1)}, u32[]{:S(2)}, u32[]{:S(2)}) collective-permute-start(bf16[10,128,128]{2,1,0:T(8,128)(2,1)S(1)} %collective-permute-done.4.refs_7_), channel_id=1, source_target_pairs={{0,1},{1,0},{2,3},{3,2},{4,5},{5,4},{6,7},{7,6},{8,9},{9,8},{10,11... | collective-permute-start | bytes 983048 | tf_op jit(solution)/shard_map/ppermute | solution.py:311
  37.9 9.1 %collective-permute-start.6 = (bf16[512,512]{1,0:T(8,128)(2,1)S(1)}, bf16[512,512]{1,0:T(8,128)(2,1)S(1)}, u32[]{:S(2)}, u32[]{:S(2)}) collective-permute-start(bf16[512,512]{1,0:T(8,128)(2,1)S(1)} %get-tuple-element.29), channel_id=1, source_target_pairs={{0,3},{2,5},{4,7},{6,9},{8,11},{10,13},{12,15},{14,17},{16,19},{18... | collective-permute-start | bytes 1572872 | tf_op jit(solution)/shard_map/ppermute | solution.py:308
  46.9 0.0 collective-permute-done.3.refs_6_
  46.9 0.0 collective-permute-done.5.refs_8_
  46.9 0.0 collective-permute-done.2.refs_5_
  47.0 2.8 %shard_map.48 = (bf16[512,1536]{1,0:T(8,128)(2,1)S(1)}, bf16[512,512]{1,0:T(8,128)(2,1)S(1)}, bf16[512,512]{1,0:T(8,128)(2,1)S(1)}) custom-call(s32[4,12]{1,0:T(4,128)S(1)} %get-tuple-element.21.refs_0_.table, bf16[512,1536]{1,0:T(8,128)(2,1)S(1)} %get-tuple-element.22.refs_1_.refs_2_, bf16[512,1536]{1,0:T(8,128)(2,1)S(1)} %get-tuple-element.23.refs_2_, ...), custom_call_target="tpu_custom_call" | custom-call | flops 1073741824 | bytes 4194304 | tf_op jit(solution)/shard_map/pallas_call | solution.py:28
  49.7 1.9 %collective-permute-start.8 = (bf16[512,512]{1,0:T(8,128)(2,1)S(1)}, bf16[512,512]{1,0:T(8,128)(2,1)S(1)}, u32[]{:S(2)}, u32[]{:S(2)}) collective-permute-start(bf16[512,512]{1,0:T(8,128)(2,1)S(1)} %get-tuple-element.32), channel_id=1, source_target_pairs={{0,3},{2,5},{4,7},{6,9},{8,11},{10,13},{12,15},{14,17},{16,19},{18... | collective-permute-start | bytes 1572872 | tf_op jit(solution)/shard_map/ppermute | solution.py:308
  51.7 2.1 %collective-permute-done.6.refs_3_ = bf16[512,512]{1,0:T(8,128)(2,1)S(1)} collective-permute-done((bf16[512,512]{1,0:T(8,128)(2,1)S(1)}, bf16[512,512]{1,0:T(8,128)(2,1)S(1)}, u32[]{:S(2)}, u32[]{:S(2)}) %collective-permute-start.6) | collective-permute-done | bytes 524320 | tf_op jit(solution)/shard_map/ppermute | solution.py:308
  53.8 1.1 %shard_map.49 = (bf16[512,512]{1,0:T(8,128)(2,1)S(1)}, bf16[10,128,128]{2,1,0:T(8,128)(2,1)S(1)}) custom-call(s32[4,12]{1,0:T(4,128)S(1)} %get-tuple-element.21.refs_0_.table, bf16[512,1536]{1,0:T(8,128)(2,1)S(1)} %get-tuple-element.28.refs_1_, bf16[512,1536]{1,0:T(8,128)(2,1)S(1)} %get-tuple-element.22.refs_1_.refs_2_, ...), custom_call_target="tpu_custom_call" | custom-call | flops 1073741824 | bytes 4194304 | tf_op jit(solution)/shard_map/pallas_call | solution.py:28
  54.9 9.1 %collective-permute-start.9 = (bf16[10,128,128]{2,1,0:T(8,128)(2,1)S(1)}, bf16[10,128,128]{2,1,0:T(8,128)(2,1)S(1)}, u32[]{:S(2)}, u32[]{:S(2)}) collective-permute-start(bf16[10,128,128]{2,1,0:T(8,128)(2,1)S(1)} %get-tuple-element.31), channel_id=1, source_target_pairs={{0,3},{2,5},{4,7},{6,9},{8,11},{10,13},{12,15},{14,17},{16,19},{18... | collective-permute-start | bytes 983048 | tf_op jit(solution)/shard_map/ppermute | solution.py:308
  63.9 1.7 %collective-permute-done.8.hb = bf16[512,512]{1,0:T(8,128)(2,1)S(1)} collective-permute-done((bf16[512,512]{1,0:T(8,128)(2,1)S(1)}, bf16[512,512]{1,0:T(8,128)(2,1)S(1)}, u32[]{:S(2)}, u32[]{:S(2)}) %collective-permute-start.8) | collective-permute-done | bytes 524320 | tf_op jit(solution)/shard_map/ppermute | solution.py:308
  65.7 1.9 %collective-permute-start.10 = (bf16[512,512]{1,0:T(8,128)(2,1)S(1)}, bf16[512,512]{1,0:T(8,128)(2,1)S(1)}, u32[]{:S(2)}, u32[]{:S(2)}) collective-permute-start(bf16[512,512]{1,0:T(8,128)(2,1)S(1)} %collective-permute-done.8.hb), channel_id=1, source_target_pairs={{0,1},{1,0},{2,3},{3,2},{4,5},{5,4},{6,7},{7,6},{8,9},{9,8},{10,11... | collective-permute-start | bytes 1572872 | tf_op jit(solution)/shard_map/ppermute | solution.py:311
  67.6 2.4 %collective-permute-start.7 = (bf16[10,128,128]{2,1,0:T(8,128)(2,1)S(1)}, bf16[10,128,128]{2,1,0:T(8,128)(2,1)S(1)}, u32[]{:S(2)}, u32[]{:S(2)}) collective-permute-start(bf16[10,128,128]{2,1,0:T(8,128)(2,1)S(1)} %get-tuple-element.31), channel_id=1, source_target_pairs={{0,1},{1,0},{2,3},{3,2},{4,5},{5,4},{6,7},{7,6},{8,9},{9,8},{10,11... | collective-permute-start | bytes 983048 | tf_op jit(solution)/shard_map/ppermute | solution.py:311
  70.0 0.0 collective-permute-done.9.ha
  70.0 1.9 %collective-permute-start.11 = (bf16[10,128,128]{2,1,0:T(8,128)(2,1)S(1)}, bf16[10,128,128]{2,1,0:T(8,128)(2,1)S(1)}, u32[]{:S(2)}, u32[]{:S(2)}) collective-permute-start(bf16[10,128,128]{2,1,0:T(8,128)(2,1)S(1)} %collective-permute-done.9.ha), channel_id=1, source_target_pairs={{0,1},{1,0},{2,3},{3,2},{4,5},{5,4},{6,7},{7,6},{8,9},{9,8},{10,11... | collective-permute-start | bytes 983048 | tf_op jit(solution)/shard_map/ppermute | solution.py:311
  71.9 0.0 collective-permute-done.7.sa2
  71.9 1.6 %collective-permute-done.11.ha2 = bf16[10,128,128]{2,1,0:T(8,128)(2,1)S(1)} collective-permute-done((bf16[10,128,128]{2,1,0:T(8,128)(2,1)S(1)}, bf16[10,128,128]{2,1,0:T(8,128)(2,1)S(1)}, u32[]{:S(2)}, u32[]{:S(2)}) %collective-permute-start.11) | collective-permute-done | bytes 327712 | tf_op jit(solution)/shard_map/ppermute | solution.py:311
  73.5 0.0 collective-permute-done.10.hb2
  73.5 0.0 copy-start.3
  73.5 0.0 copy-start.5
  73.5 3.1 %shard_map.50 = (bf16[512,512]{1,0:T(8,128)(2,1)S(1)}, bf16[512,512]{1,0:T(8,128)(2,1)S(1)}, bf16[512,512]{1,0:T(8,128)(2,1)S(1)}, bf16[10,128,128]{2,1,0:T(8,128)(2,1)S(1)}) custom-call(s32[4,12]{1,0:T(4,128)S(1)} %get-tuple-element.21.refs_0_.table, bf16[512,512]{1,0:T(8,128)(2,1)S(1)} %get-tuple-element.27.pc, bf16[512,512]{1,0:T(8,128)(2,1)S(1)} %get-tuple-element.30.pr, ...), custom_call_target="tpu_custom_call" | custom-call | flops 2147483648 | bytes 4194304 | tf_op jit(solution)/shard_map/pallas_call | solution.py:28
  76.7 7.7 %collective-permute-start.13 = (bf16[512,512]{1,0:T(8,128)(2,1)S(1)}, bf16[512,512]{1,0:T(8,128)(2,1)S(1)}, u32[]{:S(2)}, u32[]{:S(2)}) collective-permute-start(bf16[512,512]{1,0:T(8,128)(2,1)S(1)} %get-tuple-element.36), channel_id=1, source_target_pairs={{0,3},{2,5},{4,7},{6,9},{8,11},{10,13},{12,15},{14,17},{16,19},{18... | collective-permute-start | bytes 1572872 | tf_op jit(solution)/shard_map/ppermute | solution.py:308
  84.4 3.3 %collective-permute-start.14 = (bf16[10,128,128]{2,1,0:T(8,128)(2,1)S(1)}, bf16[10,128,128]{2,1,0:T(8,128)(2,1)S(1)}, u32[]{:S(2)}, u32[]{:S(2)}) collective-permute-start(bf16[10,128,128]{2,1,0:T(8,128)(2,1)S(1)} %get-tuple-element.35), channel_id=1, source_target_pairs={{0,3},{2,5},{4,7},{6,9},{8,11},{10,13},{12,15},{14,17},{16,19},{18... | collective-permute-start | bytes 983048 | tf_op jit(solution)/shard_map/ppermute | solution.py:308
  87.7 4.9 %collective-permute-done.13.hb = bf16[512,512]{1,0:T(8,128)(2,1)S(1)} collective-permute-done((bf16[512,512]{1,0:T(8,128)(2,1)S(1)}, bf16[512,512]{1,0:T(8,128)(2,1)S(1)}, u32[]{:S(2)}, u32[]{:S(2)}) %collective-permute-start.13) | collective-permute-done | bytes 524320 | tf_op jit(solution)/shard_map/ppermute | solution.py:308
  92.6 1.9 %collective-permute-start.15 = (bf16[512,512]{1,0:T(8,128)(2,1)S(1)}, bf16[512,512]{1,0:T(8,128)(2,1)S(1)}, u32[]{:S(2)}, u32[]{:S(2)}) collective-permute-start(bf16[512,512]{1,0:T(8,128)(2,1)S(1)} %collective-permute-done.13.hb), channel_id=1, source_target_pairs={{0,1},{1,0},{2,3},{3,2},{4,5},{5,4},{6,7},{7,6},{8,9},{9,8},{10,11... | collective-permute-start | bytes 1572872 | tf_op jit(solution)/shard_map/ppermute | solution.py:311
  94.5 2.4 %collective-permute-start.12 = (bf16[10,128,128]{2,1,0:T(8,128)(2,1)S(1)}, bf16[10,128,128]{2,1,0:T(8,128)(2,1)S(1)}, u32[]{:S(2)}, u32[]{:S(2)}) collective-permute-start(bf16[10,128,128]{2,1,0:T(8,128)(2,1)S(1)} %get-tuple-element.35), channel_id=1, source_target_pairs={{0,1},{1,0},{2,3},{3,2},{4,5},{5,4},{6,7},{7,6},{8,9},{9,8},{10,11... | collective-permute-start | bytes 983048 | tf_op jit(solution)/shard_map/ppermute | solution.py:311
  96.9 1.3 %collective-permute-done.14.ha = bf16[10,128,128]{2,1,0:T(8,128)(2,1)S(1)} collective-permute-done((bf16[10,128,128]{2,1,0:T(8,128)(2,1)S(1)}, bf16[10,128,128]{2,1,0:T(8,128)(2,1)S(1)}, u32[]{:S(2)}, u32[]{:S(2)}) %collective-permute-start.14) | collective-permute-done | bytes 327712 | tf_op jit(solution)/shard_map/ppermute | solution.py:308
  98.2 2.1 %collective-permute-start.16 = (bf16[10,128,128]{2,1,0:T(8,128)(2,1)S(1)}, bf16[10,128,128]{2,1,0:T(8,128)(2,1)S(1)}, u32[]{:S(2)}, u32[]{:S(2)}) collective-permute-start(bf16[10,128,128]{2,1,0:T(8,128)(2,1)S(1)} %collective-permute-done.14.ha), channel_id=1, source_target_pairs={{0,1},{1,0},{2,3},{3,2},{4,5},{5,4},{6,7},{7,6},{8,9},{9,8},{10,11... | collective-permute-start | bytes 983048 | tf_op jit(solution)/shard_map/ppermute | solution.py:311
  100.3 0.0 collective-permute-done.12.sa2
  100.3 1.4 %collective-permute-done.16.ha2 = bf16[10,128,128]{2,1,0:T(8,128)(2,1)S(1)} collective-permute-done((bf16[10,128,128]{2,1,0:T(8,128)(2,1)S(1)}, bf16[10,128,128]{2,1,0:T(8,128)(2,1)S(1)}, u32[]{:S(2)}, u32[]{:S(2)}) %collective-permute-start.16) | collective-permute-done | bytes 327712 | tf_op jit(solution)/shard_map/ppermute | solution.py:311
  101.7 0.0 collective-permute-done.15.hb2
  101.7 0.0 copy-done.3
  101.7 0.0 copy-done.5
  101.8 4.7 %shard_map.51 = bf16[4,4,128,128]{3,2,1,0:T(8,128)(2,1)} custom-call(s32[4,8]{1,0:T(4,128)S(1)} %copy-done.3, s32[4,8]{1,0:T(4,128)S(1)} %copy-done.5, s32[4,12]{1,0:T(4,128)S(1)} %get-tuple-element.21.refs_0_.table, bf16[512,512]{1,0:T(8,128)(2,1)S(1)} %get-tuple-element.33.pc, bf16[512,512]{1,0:T(8,128)(2,1)S(1)} %get-tuple-element.34.pr, ...), custom_call_target="tpu_custom_call" | custom-call | flops 2147483648 | bytes 4194304 | tf_op jit(solution)/shard_map/pallas_call | solution.py:28
Async XLA Ops:
  0.0 1.2 %copy-start = (bf16[4,8,128,128]{3,2,1,0:T(8,128)(2,1)S(1)}, bf16[4,8,128,128]{3,2,1,0:T(8,128)(2,1)}, u32[]{:S(2)}) copy-start(bf16[4,8,128,128]{3,2,1,0:T(8,128)(2,1)} %h_ref.3) | copy-start | bytes 3145732
  1.2 0.7 copy-start.2
  1.9 0.7 copy-start.4
  2.6 16.7 %copy-start.1 = (bf16[4,8,128,128]{3,2,1,0:T(8,128)(2,1)S(1)}, bf16[4,8,128,128]{3,2,1,0:T(8,128)(2,1)}, u32[]{:S(2)}) copy-start(bf16[4,8,128,128]{3,2,1,0:T(8,128)(2,1)} %x_ref.1) | copy-start | bytes 3145732
  4.1 27.1 %collective-permute-start = (bf16[512,512]{1,0:T(8,128)(2,1)S(1)}, bf16[512,512]{1,0:T(8,128)(2,1)S(1)}, u32[]{:S(2)}, u32[]{:S(2)}) collective-permute-start(bf16[512,512]{1,0:T(8,128)(2,1)S(1)} %get-tuple-element.24), channel_id=1, source_target_pairs={{0,3},{2,5},{4,7},{6,9},{8,11},{10,13},{12,15},{14,17},{16,19},{18... | collective-permute-start | bytes 1572872 | tf_op jit(solution)/shard_map/ppermute | solution.py:308
  17.4 15.8 %collective-permute-start.1 = (bf16[10,128,128]{2,1,0:T(8,128)(2,1)S(1)}, bf16[10,128,128]{2,1,0:T(8,128)(2,1)S(1)}, u32[]{:S(2)}, u32[]{:S(2)}) collective-permute-start(bf16[10,128,128]{2,1,0:T(8,128)(2,1)S(1)} %get-tuple-element.25), channel_id=1, source_target_pairs={{0,3},{2,5},{4,7},{6,9},{8,11},{10,13},{12,15},{14,17},{16,19},{18... | collective-permute-start | bytes 983048 | tf_op jit(solution)/shard_map/ppermute | solution.py:308
  22.1 13.8 %collective-permute-start.4 = (bf16[10,128,128]{2,1,0:T(8,128)(2,1)S(1)}, bf16[10,128,128]{2,1,0:T(8,128)(2,1)S(1)}, u32[]{:S(2)}, u32[]{:S(2)}) collective-permute-start(bf16[10,128,128]{2,1,0:T(8,128)(2,1)S(1)} %get-tuple-element.26), channel_id=1, source_target_pairs={{0,3},{2,5},{4,7},{6,9},{8,11},{10,13},{12,15},{14,17},{16,19},{18... | collective-permute-start | bytes 983048 | tf_op jit(solution)/shard_map/ppermute | solution.py:308
  31.2 15.8 %collective-permute-start.2 = (bf16[512,512]{1,0:T(8,128)(2,1)S(1)}, bf16[512,512]{1,0:T(8,128)(2,1)S(1)}, u32[]{:S(2)}, u32[]{:S(2)}) collective-permute-start(bf16[512,512]{1,0:T(8,128)(2,1)S(1)} %collective-permute-done.refs_3_), channel_id=1, source_target_pairs={{0,1},{1,0},{2,3},{3,2},{4,5},{5,4},{6,7},{7,6},{8,9},{9,8},{10,11... | collective-permute-start | bytes 1572872 | tf_op jit(solution)/shard_map/ppermute | solution.py:311
  33.1 13.8 %collective-permute-start.3 = (bf16[10,128,128]{2,1,0:T(8,128)(2,1)S(1)}, bf16[10,128,128]{2,1,0:T(8,128)(2,1)S(1)}, u32[]{:S(2)}, u32[]{:S(2)}) collective-permute-start(bf16[10,128,128]{2,1,0:T(8,128)(2,1)S(1)} %collective-permute-done.1.refs_4_), channel_id=1, source_target_pairs={{0,1},{1,0},{2,3},{3,2},{4,5},{5,4},{6,7},{7,6},{8,9},{9,8},{10,11... | collective-permute-start | bytes 983048 | tf_op jit(solution)/shard_map/ppermute | solution.py:311
  35.9 11.0 %collective-permute-start.5 = (bf16[10,128,128]{2,1,0:T(8,128)(2,1)S(1)}, bf16[10,128,128]{2,1,0:T(8,128)(2,1)S(1)}, u32[]{:S(2)}, u32[]{:S(2)}) collective-permute-start(bf16[10,128,128]{2,1,0:T(8,128)(2,1)S(1)} %collective-permute-done.4.refs_7_), channel_id=1, source_target_pairs={{0,1},{1,0},{2,3},{3,2},{4,5},{5,4},{6,7},{7,6},{8,9},{9,8},{10,11... | collective-permute-start | bytes 983048 | tf_op jit(solution)/shard_map/ppermute | solution.py:311
  37.9 15.9 %collective-permute-start.6 = (bf16[512,512]{1,0:T(8,128)(2,1)S(1)}, bf16[512,512]{1,0:T(8,128)(2,1)S(1)}, u32[]{:S(2)}, u32[]{:S(2)}) collective-permute-start(bf16[512,512]{1,0:T(8,128)(2,1)S(1)} %get-tuple-element.29), channel_id=1, source_target_pairs={{0,3},{2,5},{4,7},{6,9},{8,11},{10,13},{12,15},{14,17},{16,19},{18... | collective-permute-start | bytes 1572872 | tf_op jit(solution)/shard_map/ppermute | solution.py:308
  49.7 15.9 %collective-permute-start.8 = (bf16[512,512]{1,0:T(8,128)(2,1)S(1)}, bf16[512,512]{1,0:T(8,128)(2,1)S(1)}, u32[]{:S(2)}, u32[]{:S(2)}) collective-permute-start(bf16[512,512]{1,0:T(8,128)(2,1)S(1)} %get-tuple-element.32), channel_id=1, source_target_pairs={{0,3},{2,5},{4,7},{6,9},{8,11},{10,13},{12,15},{14,17},{16,19},{18... | collective-permute-start | bytes 1572872 | tf_op jit(solution)/shard_map/ppermute | solution.py:308
  54.9 15.1 %collective-permute-start.9 = (bf16[10,128,128]{2,1,0:T(8,128)(2,1)S(1)}, bf16[10,128,128]{2,1,0:T(8,128)(2,1)S(1)}, u32[]{:S(2)}, u32[]{:S(2)}) collective-permute-start(bf16[10,128,128]{2,1,0:T(8,128)(2,1)S(1)} %get-tuple-element.31), channel_id=1, source_target_pairs={{0,3},{2,5},{4,7},{6,9},{8,11},{10,13},{12,15},{14,17},{16,19},{18... | collective-permute-start | bytes 983048 | tf_op jit(solution)/shard_map/ppermute | solution.py:308
  65.7 7.9 %collective-permute-start.10 = (bf16[512,512]{1,0:T(8,128)(2,1)S(1)}, bf16[512,512]{1,0:T(8,128)(2,1)S(1)}, u32[]{:S(2)}, u32[]{:S(2)}) collective-permute-start(bf16[512,512]{1,0:T(8,128)(2,1)S(1)} %collective-permute-done.8.hb), channel_id=1, source_target_pairs={{0,1},{1,0},{2,3},{3,2},{4,5},{5,4},{6,7},{7,6},{8,9},{9,8},{10,11... | collective-permute-start | bytes 1572872 | tf_op jit(solution)/shard_map/ppermute | solution.py:311
  67.6 4.4 %collective-permute-start.7 = (bf16[10,128,128]{2,1,0:T(8,128)(2,1)S(1)}, bf16[10,128,128]{2,1,0:T(8,128)(2,1)S(1)}, u32[]{:S(2)}, u32[]{:S(2)}) collective-permute-start(bf16[10,128,128]{2,1,0:T(8,128)(2,1)S(1)} %get-tuple-element.31), channel_id=1, source_target_pairs={{0,1},{1,0},{2,3},{3,2},{4,5},{5,4},{6,7},{7,6},{8,9},{9,8},{10,11... | collective-permute-start | bytes 983048 | tf_op jit(solution)/shard_map/ppermute | solution.py:311
  70.0 3.5 %collective-permute-start.11 = (bf16[10,128,128]{2,1,0:T(8,128)(2,1)S(1)}, bf16[10,128,128]{2,1,0:T(8,128)(2,1)S(1)}, u32[]{:S(2)}, u32[]{:S(2)}) collective-permute-start(bf16[10,128,128]{2,1,0:T(8,128)(2,1)S(1)} %collective-permute-done.9.ha), channel_id=1, source_target_pairs={{0,1},{1,0},{2,3},{3,2},{4,5},{5,4},{6,7},{7,6},{8,9},{9,8},{10,11... | collective-permute-start | bytes 983048 | tf_op jit(solution)/shard_map/ppermute | solution.py:311
  73.5 28.2 %copy-start.3 = (s32[4,8]{1,0:T(4,128)S(1)}, s32[4,8]{1,0:T(4,128)}, u32[]{:S(2)}) copy-start(s32[4,8]{1,0:T(4,128)} %cols_ref.5) | copy-start | bytes 388
  73.5 28.2 %copy-start.5 = (s32[4,8]{1,0:T(4,128)S(1)}, s32[4,8]{1,0:T(4,128)}, u32[]{:S(2)}) copy-start(s32[4,8]{1,0:T(4,128)} %mask_ref.5) | copy-start | bytes 388
  76.7 15.9 %collective-permute-start.13 = (bf16[512,512]{1,0:T(8,128)(2,1)S(1)}, bf16[512,512]{1,0:T(8,128)(2,1)S(1)}, u32[]{:S(2)}, u32[]{:S(2)}) collective-permute-start(bf16[512,512]{1,0:T(8,128)(2,1)S(1)} %get-tuple-element.36), channel_id=1, source_target_pairs={{0,3},{2,5},{4,7},{6,9},{8,11},{10,13},{12,15},{14,17},{16,19},{18... | collective-permute-start | bytes 1572872 | tf_op jit(solution)/shard_map/ppermute | solution.py:308
  84.4 13.8 %collective-permute-start.14 = (bf16[10,128,128]{2,1,0:T(8,128)(2,1)S(1)}, bf16[10,128,128]{2,1,0:T(8,128)(2,1)S(1)}, u32[]{:S(2)}, u32[]{:S(2)}) collective-permute-start(bf16[10,128,128]{2,1,0:T(8,128)(2,1)S(1)} %get-tuple-element.35), channel_id=1, source_target_pairs={{0,3},{2,5},{4,7},{6,9},{8,11},{10,13},{12,15},{14,17},{16,19},{18... | collective-permute-start | bytes 983048 | tf_op jit(solution)/shard_map/ppermute | solution.py:308
  92.6 9.2 %collective-permute-start.15 = (bf16[512,512]{1,0:T(8,128)(2,1)S(1)}, bf16[512,512]{1,0:T(8,128)(2,1)S(1)}, u32[]{:S(2)}, u32[]{:S(2)}) collective-permute-start(bf16[512,512]{1,0:T(8,128)(2,1)S(1)} %collective-permute-done.13.hb), channel_id=1, source_target_pairs={{0,1},{1,0},{2,3},{3,2},{4,5},{5,4},{6,7},{7,6},{8,9},{9,8},{10,11... | collective-permute-start | bytes 1572872 | tf_op jit(solution)/shard_map/ppermute | solution.py:311
  94.5 5.8 %collective-permute-start.12 = (bf16[10,128,128]{2,1,0:T(8,128)(2,1)S(1)}, bf16[10,128,128]{2,1,0:T(8,128)(2,1)S(1)}, u32[]{:S(2)}, u32[]{:S(2)}) collective-permute-start(bf16[10,128,128]{2,1,0:T(8,128)(2,1)S(1)} %get-tuple-element.35), channel_id=1, source_target_pairs={{0,1},{1,0},{2,3},{3,2},{4,5},{5,4},{6,7},{7,6},{8,9},{9,8},{10,11... | collective-permute-start | bytes 983048 | tf_op jit(solution)/shard_map/ppermute | solution.py:311
  98.2 3.5 %collective-permute-start.16 = (bf16[10,128,128]{2,1,0:T(8,128)(2,1)S(1)}, bf16[10,128,128]{2,1,0:T(8,128)(2,1)S(1)}, u32[]{:S(2)}, u32[]{:S(2)}) collective-permute-start(bf16[10,128,128]{2,1,0:T(8,128)(2,1)S(1)} %collective-permute-done.14.ha), channel_id=1, source_target_pairs={{0,1},{1,0},{2,3},{3,2},{4,5},{5,4},{6,7},{7,6},{8,9},{9,8},{10,11... | collective-permute-start | bytes 983048 | tf_op jit(solution)/shard_map/ppermute | solution.py:311

commit v2 on v1

v2 whole, which is shorter than its diff:
```python
import math

import jax
import jax.numpy as jnp
from jax import lax
from jax.experimental import pallas as pl
from jax.experimental.pallas import tpu as pltpu
from jax.sharding import PartitionSpec as P

BAND = 4
STEPS = 2
S = 128
Q = 4 * S
H = 2 * S
TRI = [(p, m) for p in range(4) for m in range(p, 4)]
BF = jnp.bfloat16
F32 = jnp.float32
LEFT, OWN, RIGHT = (0, 1), (2, 3), (4, 5)

VMEM = pl.BlockSpec(memory_space=pltpu.VMEM)
SMEM = pl.BlockSpec(memory_space=pltpu.SMEM)
SQUARE = jax.ShapeDtypeStruct((Q, Q), BF)
CORNER = jax.ShapeDtypeStruct((len(TRI), S, S), BF)
BANDED = jax.ShapeDtypeStruct((Q, 3 * Q), BF)
SEND = jax.ShapeDtypeStruct((6 * S + S // 2, Q), BF)
SUMS = jax.ShapeDtypeStruct((Q, Q), F32)
WIDE = jax.ShapeDtypeStruct((Q, 3 * Q), F32)


def call(kernel, outs, out_specs, in_specs, scratch, flops, *args, room=24):
    return pl.pallas_call(
        kernel,
        out_shape=outs,
        in_specs=in_specs,
        out_specs=out_specs,
        scratch_shapes=scratch,
        compiler_params=pltpu.CompilerParams(vmem_limit_bytes=room << 20),
        cost_estimate=pl.CostEstimate(flops=flops, bytes_accessed=4 << 20, transcendentals=0),
    )(*args)


def place(cols_ref, mask_ref, a, s):
    first = lax.axis_index("rows") * 4 - BAND
    core = lax.axis_index("rep")
    k = cols_ref[a, s] - first
    k = jnp.clip(k, 0, 11)
    k = jnp.where(core == 1, 11 - k, k)
    row = jnp.where(core == 1, 3 - a, a)
    t = jnp.where(k < 4, 3 - k, k)
    return mask_ref[a, s] == 1, row, t


def at(index):
    return pl.ds(pl.multiple_of(index * S, S), S)


def eye():
    rows = lax.broadcasted_iota(jnp.int32, (S, S), 0)
    cols = lax.broadcasted_iota(jnp.int32, (S, S), 1)
    return (rows == cols).astype(F32)


def joint_put(joint, index, block):
    if joint.shape[0] == 6 * S + S // 2 and index >= 24:
        col = (index - 24) * 2 * S
        joint[6 * S :, col : col + S] = block[: S // 2]
        joint[6 * S :, col + S : col + 2 * S] = block[S // 2 :]
    else:
        row, col = index // 4 * S, index % 4 * S
        joint[row : row + S, col : col + S] = block


def joint_block(joint, index):
    if joint.shape[0] == 6 * S + S // 2 and index >= 24:
        col = (index - 24) * 2 * S
        return jnp.concatenate([joint[6 * S :, col : col + S], joint[6 * S :, col + S : col + 2 * S]], axis=0)
    row, col = index // 4 * S, index % 4 * S
    return joint[row : row + S, col : col + S]


def joint_send(joint, row, t, block):
    if 4 <= t < 8:
        joint_put(joint, 4 * (3 - row) + 7 - t, block)
    if t >= 8 and (3 - row, 11 - t) in TRI:
        joint_put(joint, 16 + TRI.index((3 - row, 11 - t)), block)


def fill_table(cols, mask, table):
    for i in range(48):
        table[i] = -1
    for a in range(4):
        for s in range(8):
            active, row, t = place(cols, mask, a, s)
            table[jnp.where(active, 12 * row + t, 48)] = s


def source_row(row):
    return jnp.where(lax.axis_index("rep") == 1, 3 - row, row)


def slot_block(ref, table, row, t):
    slot = table[12 * row + t]
    block = ref[source_row(row), jnp.maximum(slot, 0)]
    return jnp.where(slot >= 0, block, jnp.zeros_like(block))


def x_slot_block(ref, table, diag, row, t):
    block = slot_block(ref, table, row, t)
    return (block.astype(F32) + diag).astype(BF) if t - 4 == row else block


def pack_kernel(cols_hbm, mask_hbm, h_hbm, x_hbm, joint_ref, xb_ref, table_ref, cols, mask, h_ref, x_ref, sems):
    pattern = [
        pltpu.make_async_copy(cols_hbm, cols, sems.at[0]),
        pltpu.make_async_copy(mask_hbm, mask, sems.at[1]),
    ]
    h_copy = pltpu.make_async_copy(h_hbm, h_ref, sems.at[2])
    x_copy = pltpu.make_async_copy(x_hbm, x_ref, sems.at[3])
    for copy in pattern + [h_copy, x_copy]:
        copy.start()
    for copy in pattern:
        copy.wait()
    fill_table(cols, mask, table_ref)
    diag = eye()

    h_copy.wait()
    for row in range(4):
        for t in range(4, 12):
            joint_send(joint_ref, row, t, slot_block(h_ref, table_ref, row, t))
    x_copy.wait()
    for index, (p, m) in enumerate(TRI):
        joint_put(joint_ref, 26 + index, slot_block(x_ref, table_ref, 3 - p, 11 - m))
    for row in range(4):
        for m in range(4):
            put(xb_ref, 3 - row, 3 - m, x_slot_block(x_ref, table_ref, diag, row, 4 + m))


def own_kernel(table, h_ref, x_ref, ho_ref, xo_ref):
    diag = eye()
    for row in range(4):
        for t in range(12):
            put(ho_ref, row, t, slot_block(h_ref, table, row, t))
            put(xo_ref, row, t, x_slot_block(x_ref, table, diag, row, t))


def spread_mine(get, square_ref):
    square_ref[H:, :H] = jnp.zeros((H, H), BF)
    square_ref[S : 2 * S, :S] = jnp.zeros((S, S), BF)
    square_ref[3 * S :, H : 3 * S] = jnp.zeros((S, S), BF)
    for index, (p, m) in enumerate(TRI):
        square_ref[p * S : (p + 1) * S, m * S : (m + 1) * S] = get(index)


def spread_twin(get, square_ref):
    square_ref[H:, H:] = jnp.zeros((H, H), BF)
    square_ref[S : 2 * S, 3 * S :] = jnp.zeros((S, S), BF)
    square_ref[3 * S :, S:H] = jnp.zeros((S, S), BF)
    for index, (p, m) in enumerate(TRI):
        square_ref[p * S : (p + 1) * S, (3 - m) * S : (4 - m) * S] = get(index)


def tile(ref, i, j):
    return ref[i * H : (i + 1) * H, j * H : (j + 1) * H]


def right_operand(ll, lc, own, rc, rr):
    def get(t, u):
        if t in OWN:
            if (t, u) in ((3, 1), (2, 5)):
                return None
            return own(t - 2, u)
        if t in LEFT:
            if u in LEFT:
                return tile(ll, t, u)
            if u in OWN and (t, u) != (1, 3):
                return tile(lc, t, u - 2)
            return None
        if u in RIGHT:
            return tile(rr, t - 4, u - 4)
        if u in OWN and (t, u) != (5, 2):
            return tile(rc, t - 4, u - 2)
        return None

    return get


def left_tile(ref, r, t):
    if (r, t) in ((1, 1), (0, 5)):
        return None
    return tile(ref, r, t)


def product(left, right, columns, finish):
    for u in columns:
        for r in range(2):
            if (r, u) in ((1, 1), (0, 5)):
                continue
            total = None
            for t in range(6):
                x = left(r, t)
                y = None if x is None else right(t, u)
                if y is None:
                    continue
                term = jnp.dot(x, y, preferred_element_type=F32)
                total = term if total is None else total + term
            finish(r, u, total)


def each_block(table_ref, r, u, total, store):
    for i in range(2):
        for j in range(2):
            row, t = 2 * r + i, 2 * u + j
            block = total[i * S : (i + 1) * S, j * S : (j + 1) * S]
            block = jnp.where(table_ref[12 * row + t] >= 0, block, 0.0)
            store(row, t, block)


def put(ref, row, t, block):
    ref[row * S : (row + 1) * S, t * S : (t + 1) * S] = block


def put_tile(ref, i, j, value):
    ref[i * H : (i + 1) * H, j * H : (j + 1) * H] = value


def mine_kernel(xo, ho, joint, part, rc):
    spread_mine(lambda i: joint_block(joint, 16 + i), rc)
    right = right_operand(None, None, lambda r, u: tile(ho, r, u), rc, joint)
    left = lambda r, t: None if t in LEFT else left_tile(xo, r, t)
    product(left, right, range(6), lambda r, u, total: put_tile(part, r, u, total))


def half_kernel(table, xo, twin, part, half_ref, lc):
    spread_twin(lambda i: joint_block(twin, 16 + i), lc)
    half_ref[H:, H:Q] = jnp.zeros((H, H), BF)
    half_ref[:H, 2 * Q + H :] = jnp.zeros((H, H), BF)
    right = right_operand(twin, lc, None, None, None)

    def keep(r, u, total):
        total = tile(part, r, u) if total is None else total + tile(part, r, u)
        each_block(table, r, u, total, lambda row, t, b: put(half_ref, row, t, b.astype(BF)))

    product(lambda r, t: left_tile(xo, r, t) if t in LEFT else None, right, range(6), keep)


def start_kernel(factor, table, half, xo, joint, twin, xb, band, send, side, xlc, xrc):
    spread_twin(lambda i: joint_block(twin, 26 + i), xlc)
    spread_mine(lambda i: joint_block(joint, 26 + i), xrc)
    right = right_operand(None, xlc, lambda r, u: tile(xo, r, u), xrc, xb)
    diag = eye()

    def start(r, u, total):
        def store(row, t, block):
            value = -factor * block
            if t - 4 == row:
                value = value + 0.5 * diag
            value = value.astype(BF)
            put(band, row, t, value)
            joint_send(send, row, t, value)
            if u in RIGHT and (3 - row, 11 - t) in TRI:
                side[TRI.index((3 - row, 11 - t))] = value

        each_block(table, r, u, total, store)

    product(lambda r, t: left_tile(half, r, t), right, OWN + RIGHT, start)


def mine_squares_kernel(table, band, joint, sq_r, part_l, sums, more, rc):
    spread_mine(lambda i: joint_block(joint, 16 + i), rc)
    sq_r[:H, H:] = jnp.zeros((H, H), BF)
    right = right_operand(None, None, lambda r, u: tile(band, r, u), rc, joint)

    def keep(r, u, total):
        if u in LEFT:
            put_tile(part_l, r, u, total)
        elif u in OWN:
            put_tile(sums, r, u - 2, total)
        else:
            each_block(table, r, u, total, lambda row, t, b: put(sq_r, row, t - 8, b.astype(BF)))

    product(lambda r, t: None if t in LEFT else left_tile(band, r, t), right, RIGHT + OWN + LEFT, keep)

    def square(r, t):
        return None if t not in RIGHT or (r, t) == (0, 5) else tile(sq_r, r, t - 4)

    product(square, right, OWN + RIGHT, lambda r, u, total: put_tile(more, r, u - 2, total))


def late_kernel(table, band, sq_r, part_l, sums, more, twin, lc, sq, finish, after=None):
    spread_twin(lambda i: joint_block(twin, 16 + i), lc)
    right = right_operand(twin, lc, lambda r, u: tile(band, r, u), None, None)

    for half in range(2):

        def only(left, *places):
            return lambda r, t: left(r, t) if r == half and t in places else None

        def keep(r, u, total):
            if r != half:
                return
            total = total + (tile(sums, r, u - 2) if u in OWN else tile(part_l, r, u))
            each_block(table, r, u, total, lambda row, t, b: put(sq, row, t, b.astype(BF)))

        def step(r, u, total):
            if r != half:
                return
            if u not in LEFT:
                total = total + tile(more, r, u - 2)

            def store(row, t, block):
                if u in RIGHT:
                    now = sq_r[row * S : (row + 1) * S, (t - 8) * S : (t - 7) * S]
                else:
                    now = sq[row * S : (row + 1) * S, t * S : (t + 1) * S]
                finish(row, t, (3.0 * now.astype(F32) - 2.0 * block).astype(BF))

            each_block(table, r, u, total, store)

        product(only(lambda r, t: left_tile(band, r, t), *LEFT), right, LEFT + OWN, keep)
        product(only(lambda r, t: left_tile(sq, r, t), *LEFT, *OWN), right, OWN + RIGHT + LEFT, step)
        if after:
            after(half)


def step_kernel(table, band, sq_r, part_l, sums, more, twin, new, send, lc, sq):
    new[H:, H:Q] = jnp.zeros((H, H), BF)
    new[:H, 2 * Q + H :] = jnp.zeros((H, H), BF)

    def finish(row, t, value):
        put(new, row, t, value)
        joint_send(send, row, t, value)

    late_kernel(table, band, sq_r, part_l, sums, more, twin, lc, sq, finish)


def last_kernel(cols, mask, table, band, sq_r, part_l, sums, more, twin, out_hbm, lc, sq, res, out, sems):
    core = lax.axis_index("rep")

    def copy(row):
        return pltpu.make_async_copy(out.at[row], out_hbm.at[source_row(row)], sems.at[row])

    def after(half):
        for row in (2 * half, 2 * half + 1):
            for s in range(4):
                active, unused, t = place(cols, mask, source_row(row), core * 4 + s)
                block = res[row * S : (row + 1) * S, at(t)]
                out[row, s] = jnp.where(active, block, jnp.zeros_like(block))
            copy(row).start()

    late_kernel(
        table, band, sq_r, part_l, sums, more, twin, lc, sq, lambda row, t, value: put(res, row, t, value), after
    )
    for row in range(4):
        copy(row).wait()


def join_kernel(band, side, out):
    out[:, Q:] = band[:, Q:]
    out[:H, 2 * Q + H :] = jnp.zeros((H, H), BF)
    spread_twin(lambda i: side[i], out.at[:, :Q])


def on_device(hamiltonian, x_correction, cols, mask):
    n = lax.axis_size("rows")
    factor = 0.6 / math.sqrt(cols.shape[1] * hamiltonian.shape[-1])
    outward = [(2 * i, 2 * i + 3) for i in range(n - 1)] + [(2 * i + 1, 2 * i - 2) for i in range(1, n)]

    def link(x):
        return lax.ppermute(x, ("rows", "rep"), outward)

    def swap(x):
        return lax.ppermute(x, "rep", [(0, 1), (1, 0)])

    square = pltpu.VMEM((Q, Q), BF)
    flops = 1 << 29
    hbm = pl.BlockSpec(memory_space=pltpu.HBM)

    index_table = jax.ShapeDtypeStruct((49,), jnp.int32)
    joint, xb, table = call(
        pack_kernel,
        [jax.ShapeDtypeStruct((9 * S, Q), BF), SQUARE, index_table],
        [VMEM, VMEM, SMEM],
        [hbm] * 4,
        [
            pltpu.SMEM(cols.shape, jnp.int32),
            pltpu.SMEM(mask.shape, jnp.int32),
            pltpu.VMEM(hamiltonian.shape, BF),
            pltpu.VMEM(x_correction.shape, BF),
            pltpu.SemaphoreType.DMA((4,)),
        ],
        flops,
        cols, mask, hamiltonian, x_correction,
        room=56,
    )
    joint_in = link(joint)
    xb_in = link(xb)
    ho, xo = call(
        own_kernel, [BANDED, BANDED], [VMEM] * 2, [SMEM, VMEM, VMEM], [], 0, table, hamiltonian, x_correction
    )
    twin = swap(joint_in)
    part = call(mine_kernel, WIDE, VMEM, [VMEM] * 3, [square], 64 * flops, xo, ho, joint_in)
    half = call(half_kernel, BANDED, VMEM, [SMEM] + [VMEM] * 3, [square], flops, table, xo, twin, part)
    band, send, side = call(
        lambda *refs: start_kernel(factor, *refs),
        [BANDED, SEND, CORNER],
        [VMEM] * 3,
        [SMEM] + [VMEM] * 5,
        [square] * 2,
        flops,
        table, half, xo, joint_in, twin, xb_in,
    )
    halo = link(send)
    band = call(join_kernel, BANDED, VMEM, [VMEM] * 2, [], 0, band, swap(side))
    for step in range(STEPS):
        if step > 0:
            halo = link(send)
        twin = swap(halo)
        sq_r, part_l, sums, more = call(
            mine_squares_kernel,
            [SQUARE, SUMS, SUMS, jax.ShapeDtypeStruct((Q, 2 * Q), F32)],
            [VMEM] * 4,
            [SMEM] + [VMEM] * 2,
            [square],
            64 * flops,
            table, band, halo,
        )
        operands = (table, band, sq_r, part_l, sums, more, twin)
        if step + 1 == STEPS:
            return call(
                last_kernel,
                jax.ShapeDtypeStruct((4, 4, S, S), BF),
                hbm,
                [SMEM] * 3 + [VMEM] * 6,
                [square, pltpu.VMEM((Q, 2 * Q), BF)]
                + [pltpu.VMEM((Q, 3 * Q), BF), pltpu.VMEM((4, 4, S, S), BF), pltpu.SemaphoreType.DMA((4,))],
                flops,
                cols, mask, *operands,
            )
        band, send = call(
            step_kernel,
            [BANDED, SEND],
            [VMEM] * 2,
            [SMEM] + [VMEM] * 6,
            [square, pltpu.VMEM((Q, 2 * Q), BF)],
            flops,
            *operands,
        )


def solution(mesh):
    return jax.shard_map(
        on_device,
        mesh=mesh,
        in_specs=(
            P("rows", None, None, None),
            P("rows", None, None, None),
            P("rows", None),
            P("rows", None),
        ),
        out_specs=P("rows", "rep", None, None),
        check_vma=False,
    )
```

time: 107 us -> 91.9 us (0.86)
  starting transfers between devices: 74.2 us -> 41 us
  waiting for transfers between devices: 13.5 us -> 31.1 us
  Pallas kernels: 15.9 us -> 18.6 us
  local copies, waits for them, and re-layouts: 2.6 us -> 0.68 us
    ppermute x8 -> x4, starting transfers between devices: 55.3 us -> 33.4 us  [link(): return lax.ppermute(x, ('rows', 'rep'), outward)]
    ppermute x8 -> x4, waiting for transfers between devices: 10.5 us -> 27.2 us  [link(): return lax.ppermute(x, ('rows', 'rep'), outward)]
    ppermute x9 -> x4, starting transfers between devices: 18.9 us -> 7.65 us  [swap(): return lax.ppermute(x, 'rep', [(0, 1), (1, 0)])]
    pallas_call x6 -> x10, Pallas kernels: 15.9 us -> 18.6 us  [call(): pl.pallas_call(kernel, out_shape=outs, in_specs=in_specs, out_specs=out_s...]
    unnamed x12, local copies, waits for them, and re-layouts: 2.6 us -> 0.68 us
    ppermute x9 -> x4, waiting for transfers between devices: 3.01 us -> 3.88 us  [swap(): return lax.ppermute(x, 'rep', [(0, 1), (1, 0)])]
  transfers between devices with their start and end apart: 17 -> 8, of which waited for: 7 -> 7; matrix products, arithmetic and copies ran while one was open for 0% -> 0% of each run, Pallas kernels for 6% -> 8%
where the time goes in v2:
time: 91.9 us; the launch traced here: 91.6 us
  starting transfers between devices  41 us (45%)
  waiting for transfers between devices  31.1 us (34%)
  Pallas kernels  18.6 us (20%)
    ppermute x4, starting transfers between devices, link(): return lax.ppermute(x, ('rows', 'rep'), outward)  33.4 us
    ppermute x4, waiting for transfers between devices, link(): return lax.ppermute(x, ('rows', 'rep'), outward)  27.2 us
    pallas_call x10, Pallas kernels, call(): pl.pallas_call(kernel, out_shape=outs, in_specs=in_specs, out_specs=out_s...  18.6 us
    ppermute x4, starting transfers between devices, swap(): return lax.ppermute(x, 'rep', [(0, 1), (1, 0)])  7.65 us
    ppermute x4, waiting for transfers between devices, swap(): return lax.ppermute(x, 'rep', [(0, 1), (1, 0)])  3.88 us
  transfers between devices with their start and end apart: 8, of which 7 were waited for; matrix products, arithmetic and copies ran while one was open for 0% of the time, Pallas kernels for 8%

profile of v2, /device:TPU:33, one launch (start us, length us, event | category | flops | bytes accessed | tf_op | source)
XLA Modules:
  0.0 91.6 jit_solution(2400192900812131587)
XLA Ops:
  0.0 0.0 copy-start.1
  0.0 0.0 copy-start
  0.0 3.1 %shard_map.46 = (bf16[1152,512]{1,0:T(8,128)(2,1)}, bf16[512,512]{1,0:T(8,128)(2,1)}, s32[49]{0:T(128)}) custom-call(s32[4,8]{1,0:T(4,128)} %cols.1, s32[4,8]{1,0:T(4,128)} %mask.1, bf16[4,8,128,128]{3,2,1,0:T(8,128)(2,1)} %h_ref.1, bf16[4,8,128,128]{3,2,1,0:T(8,128)(2,1)} %x_ref.1), custom_call_target="tpu_custom_call" | custom-call | flops 536870912 | bytes 4194304 | tf_op jit(solution)/shard_map/pallas_call | solution.py:31
  3.1 13.3 %collective-permute-start = (bf16[1152,512]{1,0:T(8,128)(2,1)}, bf16[1152,512]{1,0:T(8,128)(2,1)S(1)}, u32[]{:S(2)}, u32[]{:S(2)}) collective-permute-start(bf16[1152,512]{1,0:T(8,128)(2,1)} %get-tuple-element.25), channel_id=1, source_target_pairs={{0,3},{2,5},{4,7},{6,9},{8,11},{10,13},{12,15},{14,17},{16,19},{18... | collective-permute-start | bytes 3538952 | tf_op jit(solution)/shard_map/ppermute | solution.py:369
  16.4 1.9 %collective-permute-start.2 = (bf16[512,512]{1,0:T(8,128)(2,1)}, bf16[512,512]{1,0:T(8,128)(2,1)S(1)}, u32[]{:S(2)}, u32[]{:S(2)}) collective-permute-start(bf16[512,512]{1,0:T(8,128)(2,1)} %get-tuple-element.27), channel_id=1, source_target_pairs={{0,3},{2,5},{4,7},{6,9},{8,11},{10,13},{12,15},{14,17},{16,19},{18... | collective-permute-start | bytes 1572872 | tf_op jit(solution)/shard_map/ppermute | solution.py:369
  18.4 0.0 copy-done.1
  18.4 0.0 copy-done
  18.4 0.0 copy-start.2
  18.4 0.7 copy-done.2
  19.1 1.3 %shard_map.47 = (bf16[512,1536]{1,0:T(8,128)(2,1)S(1)}, bf16[512,1536]{1,0:T(8,128)(2,1)S(1)}) custom-call(s32[49]{0:T(128)S(1)} %copy-done.2, bf16[4,8,128,128]{3,2,1,0:T(8,128)(2,1)S(1)} %copy-done, bf16[4,8,128,128]{3,2,1,0:T(8,128)(2,1)S(1)} %copy-done.1), custom_call_target="tpu_custom_call" | custom-call | bytes 4194304 | tf_op jit(solution)/shard_map/pallas_call | solution.py:31
  20.4 10.2 %collective-permute-done.joint.refs_3_ = bf16[1152,512]{1,0:T(8,128)(2,1)S(1)} collective-permute-done((bf16[1152,512]{1,0:T(8,128)(2,1)}, bf16[1152,512]{1,0:T(8,128)(2,1)S(1)}, u32[]{:S(2)}, u32[]{:S(2)}) %collective-permute-start) | collective-permute-done | bytes 1179680 | tf_op jit(solution)/shard_map/ppermute | solution.py:369
  30.5 1.9 %collective-permute-start.1 = (bf16[1152,512]{1,0:T(8,128)(2,1)S(1)}, bf16[1152,512]{1,0:T(8,128)(2,1)S(1)}, u32[]{:S(2)}, u32[]{:S(2)}) collective-permute-start(bf16[1152,512]{1,0:T(8,128)(2,1)S(1)} %collective-permute-done.joint.refs_3_), channel_id=1, source_target_pairs={{0,1},{1,0},{2,3},{3,2},{4,5},{5,4},{6,7},{7,6},{8,9},{9,8},{10,11... | collective-permute-start | bytes 3538952 | tf_op jit(solution)/shard_map/ppermute | solution.py:372
  32.5 0.0 copy-start.3
  32.5 1.1 %shard_map.48.part = f32[512,1536]{1,0:T(8,128)S(1)} custom-call(bf16[512,1536]{1,0:T(8,128)(2,1)S(1)} %get-tuple-element.24.xo.refs_2_, bf16[512,1536]{1,0:T(8,128)(2,1)S(1)} %get-tuple-element.26.ho, bf16[1152,512]{1,0:T(8,128)(2,1)S(1)} %collective-permute-done.joint.refs_3_), custom_call_target="tpu_custom_call" | custom-call | flops 34359738368 | bytes 4194304 | tf_op jit(solution)/shard_map/pallas_call | solution.py:31
  33.6 1.7 %collective-permute-done.1.twin.refs_4_ = bf16[1152,512]{1,0:T(8,128)(2,1)S(1)} collective-permute-done((bf16[1152,512]{1,0:T(8,128)(2,1)S(1)}, bf16[1152,512]{1,0:T(8,128)(2,1)S(1)}, u32[]{:S(2)}, u32[]{:S(2)}) %collective-permute-start.1) | collective-permute-done | bytes 1179680 | tf_op jit(solution)/shard_map/ppermute | solution.py:372
  35.3 0.0 copy-done.3
  35.3 1.2 %shard_map.49.refs_1_ = bf16[512,1536]{1,0:T(8,128)(2,1)S(1)} custom-call(s32[49]{0:T(128)S(1)} %copy-done.3, bf16[512,1536]{1,0:T(8,128)(2,1)S(1)} %get-tuple-element.24.xo.refs_2_, bf16[1152,512]{1,0:T(8,128)(2,1)S(1)} %collective-permute-done.1.twin.refs_4_, f32[512,1536]{1,0:T(8,128)S(1)} %shard_map.48.part), custom_call_target="tpu_custom_call" | custom-call | flops 536870912 | bytes 4194304 | tf_op jit(solution)/shard_map/pallas_call | solution.py:31
  36.4 0.0 collective-permute-done.2.refs_5_
  36.4 1.7 %shard_map.50 = (bf16[512,1536]{1,0:T(8,128)(2,1)S(1)}, bf16[832,512]{1,0:T(8,128)(2,1)S(1)}, bf16[10,128,128]{2,1,0:T(8,128)(2,1)S(1)}) custom-call(s32[49]{0:T(128)S(1)} %copy-done.3, bf16[512,1536]{1,0:T(8,128)(2,1)S(1)} %shard_map.49.refs_1_, bf16[512,1536]{1,0:T(8,128)(2,1)S(1)} %get-tuple-element.24.xo.refs_2_, ...), custom_call_target="tpu_custom_call" | custom-call | flops 536870912 | bytes 4194304 | tf_op jit(solution)/shard_map/pallas_call | solution.py:31
  38.2 9.1 %collective-permute-start.4 = (bf16[832,512]{1,0:T(8,128)(2,1)S(1)}, bf16[832,512]{1,0:T(8,128)(2,1)S(1)}, u32[]{:S(2)}, u32[]{:S(2)}) collective-permute-start(bf16[832,512]{1,0:T(8,128)(2,1)S(1)} %get-tuple-element.30), channel_id=1, source_target_pairs={{0,3},{2,5},{4,7},{6,9},{8,11},{10,13},{12,15},{14,17},{16,19},{18... | collective-permute-start | bytes 2555912 | tf_op jit(solution)/shard_map/ppermute | solution.py:369
  47.3 1.9 %collective-permute-start.3 = (bf16[10,128,128]{2,1,0:T(8,128)(2,1)S(1)}, bf16[10,128,128]{2,1,0:T(8,128)(2,1)S(1)}, u32[]{:S(2)}, u32[]{:S(2)}) collective-permute-start(bf16[10,128,128]{2,1,0:T(8,128)(2,1)S(1)} %get-tuple-element.29), channel_id=1, source_target_pairs={{0,1},{1,0},{2,3},{3,2},{4,5},{5,4},{6,7},{7,6},{8,9},{9,8},{10,11... | collective-permute-start | bytes 983048 | tf_op jit(solution)/shard_map/ppermute | solution.py:372
  49.2 1.6 %collective-permute-done.3.side = bf16[10,128,128]{2,1,0:T(8,128)(2,1)S(1)} collective-permute-done((bf16[10,128,128]{2,1,0:T(8,128)(2,1)S(1)}, bf16[10,128,128]{2,1,0:T(8,128)(2,1)S(1)}, u32[]{:S(2)}, u32[]{:S(2)}) %collective-permute-start.3) | collective-permute-done | bytes 327712 | tf_op jit(solution)/shard_map/ppermute | solution.py:372
  50.8 0.1 shard_map.51.band
  50.9 6.7 %collective-permute-done.4.joint = bf16[832,512]{1,0:T(8,128)(2,1)S(1)} collective-permute-done((bf16[832,512]{1,0:T(8,128)(2,1)S(1)}, bf16[832,512]{1,0:T(8,128)(2,1)S(1)}, u32[]{:S(2)}, u32[]{:S(2)}) %collective-permute-start.4) | collective-permute-done | bytes 852000 | tf_op jit(solution)/shard_map/ppermute | solution.py:369
  57.6 1.9 %collective-permute-start.5 = (bf16[832,512]{1,0:T(8,128)(2,1)S(1)}, bf16[832,512]{1,0:T(8,128)(2,1)S(1)}, u32[]{:S(2)}, u32[]{:S(2)}) collective-permute-start(bf16[832,512]{1,0:T(8,128)(2,1)S(1)} %collective-permute-done.4.joint), channel_id=1, source_target_pairs={{0,1},{1,0},{2,3},{3,2},{4,5},{5,4},{6,7},{7,6},{8,9},{9,8},{10,11... | collective-permute-start | bytes 2555912 | tf_op jit(solution)/shard_map/ppermute | solution.py:372
  59.5 2.0 %shard_map.52 = (bf16[512,512]{1,0:T(8,128)(2,1)S(1)}, f32[512,512]{1,0:T(8,128)S(1)}, f32[512,512]{1,0:T(8,128)S(1)}, f32[512,1024]{1,0:T(8,128)S(1)}) custom-call(s32[49]{0:T(128)S(1)} %copy-done.3, bf16[512,1536]{1,0:T(8,128)(2,1)S(1)} %shard_map.51.band, bf16[832,512]{1,0:T(8,128)(2,1)S(1)} %collective-permute-done.4.joint), custom_call_target="tpu_custom_call" | custom-call | flops 34359738368 | bytes 4194304 | tf_op jit(solution)/shard_map/pallas_call | solution.py:31
  61.6 0.3 collective-permute-done.5.twin
  61.9 2.5 %shard_map.53 = (bf16[512,1536]{1,0:T(8,128)(2,1)S(1)}, bf16[832,512]{1,0:T(8,128)(2,1)S(1)}) custom-call(s32[49]{0:T(128)S(1)} %copy-done.3, bf16[512,1536]{1,0:T(8,128)(2,1)S(1)} %shard_map.51.band, bf16[512,512]{1,0:T(8,128)(2,1)S(1)} %get-tuple-element.31.sq_r, f32[512,512]{1,0:T(8,128)S(1)} %get-tuple-element.32.part_l, ...), custom_call_target="tpu_custom_call" | custom-call | flops 536870912 | bytes 4194304 | tf_op jit(solution)/shard_map/pallas_call | solution.py:31
  64.4 9.1 %collective-permute-start.6 = (bf16[832,512]{1,0:T(8,128)(2,1)S(1)}, bf16[832,512]{1,0:T(8,128)(2,1)S(1)}, u32[]{:S(2)}, u32[]{:S(2)}) collective-permute-start(bf16[832,512]{1,0:T(8,128)(2,1)S(1)} %get-tuple-element.36), channel_id=1, source_target_pairs={{0,3},{2,5},{4,7},{6,9},{8,11},{10,13},{12,15},{14,17},{16,19},{18... | collective-permute-start | bytes 2555912 | tf_op jit(solution)/shard_map/ppermute | solution.py:369
  73.5 10.4 %collective-permute-done.6.joint = bf16[832,512]{1,0:T(8,128)(2,1)S(1)} collective-permute-done((bf16[832,512]{1,0:T(8,128)(2,1)S(1)}, bf16[832,512]{1,0:T(8,128)(2,1)S(1)}, u32[]{:S(2)}, u32[]{:S(2)}) %collective-permute-start.6) | collective-permute-done | bytes 852000 | tf_op jit(solution)/shard_map/ppermute | solution.py:369
  83.9 1.9 %collective-permute-start.7 = (bf16[832,512]{1,0:T(8,128)(2,1)S(1)}, bf16[832,512]{1,0:T(8,128)(2,1)S(1)}, u32[]{:S(2)}, u32[]{:S(2)}) collective-permute-start(bf16[832,512]{1,0:T(8,128)(2,1)S(1)} %collective-permute-done.6.joint), channel_id=1, source_target_pairs={{0,1},{1,0},{2,3},{3,2},{4,5},{5,4},{6,7},{7,6},{8,9},{9,8},{10,11... | collective-permute-start | bytes 2555912 | tf_op jit(solution)/shard_map/ppermute | solution.py:372
  85.8 0.0 copy-start.4
  85.8 0.0 copy-start.5
  85.8 2.0 %shard_map.54 = (bf16[512,512]{1,0:T(8,128)(2,1)S(1)}, f32[512,512]{1,0:T(8,128)S(1)}, f32[512,512]{1,0:T(8,128)S(1)}, f32[512,1024]{1,0:T(8,128)S(1)}) custom-call(s32[49]{0:T(128)S(1)} %copy-done.3, bf16[512,1536]{1,0:T(8,128)(2,1)S(1)} %get-tuple-element.35.band, bf16[832,512]{1,0:T(8,128)(2,1)S(1)} %collective-permute-done.6.joint), custom_call_target="tpu_custom_call" | custom-call | flops 34359738368 | bytes 4194304 | tf_op jit(solution)/shard_map/pallas_call | solution.py:31
  87.8 0.3 collective-permute-done.7.twin
  88.1 0.0 copy-done.4
  88.1 0.0 copy-done.5
  88.1 3.5 %shard_map.55 = bf16[4,4,128,128]{3,2,1,0:T(8,128)(2,1)} custom-call(s32[4,8]{1,0:T(4,128)S(1)} %copy-done.4, s32[4,8]{1,0:T(4,128)S(1)} %copy-done.5, s32[49]{0:T(128)S(1)} %copy-done.3, bf16[512,1536]{1,0:T(8,128)(2,1)S(1)} %get-tuple-element.35.band, bf16[512,512]{1,0:T(8,128)(2,1)S(1)} %get-tuple-element.37.sq_r, ...), custom_call_target="tpu_custom_call" | custom-call | flops 536870912 | bytes 4194304 | tf_op jit(solution)/shard_map/pallas_call | solution.py:31
Async XLA Ops:
  0.0 18.4 %copy-start.1 = (bf16[4,8,128,128]{3,2,1,0:T(8,128)(2,1)S(1)}, bf16[4,8,128,128]{3,2,1,0:T(8,128)(2,1)}, u32[]{:S(2)}) copy-start(bf16[4,8,128,128]{3,2,1,0:T(8,128)(2,1)} %x_ref.1) | copy-start | bytes 3145732
  0.0 18.4 %copy-start = (bf16[4,8,128,128]{3,2,1,0:T(8,128)(2,1)S(1)}, bf16[4,8,128,128]{3,2,1,0:T(8,128)(2,1)}, u32[]{:S(2)}) copy-start(bf16[4,8,128,128]{3,2,1,0:T(8,128)(2,1)} %h_ref.1) | copy-start | bytes 3145732
  3.1 27.4 %collective-permute-start = (bf16[1152,512]{1,0:T(8,128)(2,1)}, bf16[1152,512]{1,0:T(8,128)(2,1)S(1)}, u32[]{:S(2)}, u32[]{:S(2)}) collective-permute-start(bf16[1152,512]{1,0:T(8,128)(2,1)} %get-tuple-element.25), channel_id=1, source_target_pairs={{0,3},{2,5},{4,7},{6,9},{8,11},{10,13},{12,15},{14,17},{16,19},{18... | collective-permute-start | bytes 3538952 | tf_op jit(solution)/shard_map/ppermute | solution.py:369
  16.4 20.0 %collective-permute-start.2 = (bf16[512,512]{1,0:T(8,128)(2,1)}, bf16[512,512]{1,0:T(8,128)(2,1)S(1)}, u32[]{:S(2)}, u32[]{:S(2)}) collective-permute-start(bf16[512,512]{1,0:T(8,128)(2,1)} %get-tuple-element.27), channel_id=1, source_target_pairs={{0,3},{2,5},{4,7},{6,9},{8,11},{10,13},{12,15},{14,17},{16,19},{18... | collective-permute-start | bytes 1572872 | tf_op jit(solution)/shard_map/ppermute | solution.py:369
  18.4 0.7 copy-start.2
  30.5 4.7 %collective-permute-start.1 = (bf16[1152,512]{1,0:T(8,128)(2,1)S(1)}, bf16[1152,512]{1,0:T(8,128)(2,1)S(1)}, u32[]{:S(2)}, u32[]{:S(2)}) collective-permute-start(bf16[1152,512]{1,0:T(8,128)(2,1)S(1)} %collective-permute-done.joint.refs_3_), channel_id=1, source_target_pairs={{0,1},{1,0},{2,3},{3,2},{4,5},{5,4},{6,7},{7,6},{8,9},{9,8},{10,11... | collective-permute-start | bytes 3538952 | tf_op jit(solution)/shard_map/ppermute | solution.py:372
  32.5 2.8 %copy-start.3 = (s32[49]{0:T(128)S(1)}, s32[49]{0:T(128)}, u32[]{:S(2)}) copy-start(s32[49]{0:T(128)} %get-tuple-element.23.table.refs_0_) | copy-start | bytes 592
  38.2 19.4 %collective-permute-start.4 = (bf16[832,512]{1,0:T(8,128)(2,1)S(1)}, bf16[832,512]{1,0:T(8,128)(2,1)S(1)}, u32[]{:S(2)}, u32[]{:S(2)}) collective-permute-start(bf16[832,512]{1,0:T(8,128)(2,1)S(1)} %get-tuple-element.30), channel_id=1, source_target_pairs={{0,3},{2,5},{4,7},{6,9},{8,11},{10,13},{12,15},{14,17},{16,19},{18... | collective-permute-start | bytes 2555912 | tf_op jit(solution)/shard_map/ppermute | solution.py:369
  47.3 3.5 %collective-permute-start.3 = (bf16[10,128,128]{2,1,0:T(8,128)(2,1)S(1)}, bf16[10,128,128]{2,1,0:T(8,128)(2,1)S(1)}, u32[]{:S(2)}, u32[]{:S(2)}) collective-permute-start(bf16[10,128,128]{2,1,0:T(8,128)(2,1)S(1)} %get-tuple-element.29), channel_id=1, source_target_pairs={{0,1},{1,0},{2,3},{3,2},{4,5},{5,4},{6,7},{7,6},{8,9},{9,8},{10,11... | collective-permute-start | bytes 983048 | tf_op jit(solution)/shard_map/ppermute | solution.py:372
  57.6 4.3 %collective-permute-start.5 = (bf16[832,512]{1,0:T(8,128)(2,1)S(1)}, bf16[832,512]{1,0:T(8,128)(2,1)S(1)}, u32[]{:S(2)}, u32[]{:S(2)}) collective-permute-start(bf16[832,512]{1,0:T(8,128)(2,1)S(1)} %collective-permute-done.4.joint), channel_id=1, source_target_pairs={{0,1},{1,0},{2,3},{3,2},{4,5},{5,4},{6,7},{7,6},{8,9},{9,8},{10,11... | collective-permute-start | bytes 2555912 | tf_op jit(solution)/shard_map/ppermute | solution.py:372
  64.4 19.4 %collective-permute-start.6 = (bf16[832,512]{1,0:T(8,128)(2,1)S(1)}, bf16[832,512]{1,0:T(8,128)(2,1)S(1)}, u32[]{:S(2)}, u32[]{:S(2)}) collective-permute-start(bf16[832,512]{1,0:T(8,128)(2,1)S(1)} %get-tuple-element.36), channel_id=1, source_target_pairs={{0,3},{2,5},{4,7},{6,9},{8,11},{10,13},{12,15},{14,17},{16,19},{18... | collective-permute-start | bytes 2555912 | tf_op jit(solution)/shard_map/ppermute | solution.py:369
  83.9 4.3 %collective-permute-start.7 = (bf16[832,512]{1,0:T(8,128)(2,1)S(1)}, bf16[832,512]{1,0:T(8,128)(2,1)S(1)}, u32[]{:S(2)}, u32[]{:S(2)}) collective-permute-start(bf16[832,512]{1,0:T(8,128)(2,1)S(1)} %collective-permute-done.6.joint), channel_id=1, source_target_pairs={{0,1},{1,0},{2,3},{3,2},{4,5},{5,4},{6,7},{7,6},{8,9},{9,8},{10,11... | collective-permute-start | bytes 2555912 | tf_op jit(solution)/shard_map/ppermute | solution.py:372
  85.8 2.3 %copy-start.4 = (s32[4,8]{1,0:T(4,128)S(1)}, s32[4,8]{1,0:T(4,128)}, u32[]{:S(2)}) copy-start(s32[4,8]{1,0:T(4,128)} %cols.1) | copy-start | bytes 388
  85.8 2.3 %copy-start.5 = (s32[4,8]{1,0:T(4,128)S(1)}, s32[4,8]{1,0:T(4,128)}, u32[]{:S(2)}) copy-start(s32[4,8]{1,0:T(4,128)} %mask.1) | copy-start | bytes 388

commit v3 on v2

--- a/solution.py
+++ b/solution.py
@@ -27,13 +27,14 @@
 WIDE = jax.ShapeDtypeStruct((Q, 3 * Q), F32)
 
 
-def call(kernel, outs, out_specs, in_specs, scratch, flops, *args, room=24):
+def call(kernel, outs, out_specs, in_specs, scratch, flops, *args, room=24, alias=None):
     return pl.pallas_call(
         kernel,
         out_shape=outs,
         in_specs=in_specs,
         out_specs=out_specs,
         scratch_shapes=scratch,
+        input_output_aliases=alias or {},
         compiler_params=pltpu.CompilerParams(vmem_limit_bytes=room << 20),
         cost_estimate=pl.CostEstimate(flops=flops, bytes_accessed=4 << 20, transcendentals=0),
     )(*args)
@@ -61,7 +62,7 @@
 
 
 def joint_put(joint, index, block):
-    if joint.shape[0] == 6 * S + S // 2 and index >= 24:
+    if index >= 24:
         col = (index - 24) * 2 * S
         joint[6 * S :, col : col + S] = block[: S // 2]
         joint[6 * S :, col + S : col + 2 * S] = block[S // 2 :]
@@ -71,7 +72,7 @@
 
 
 def joint_block(joint, index):
-    if joint.shape[0] == 6 * S + S // 2 and index >= 24:
+    if index >= 24:
         col = (index - 24) * 2 * S
         return jnp.concatenate([joint[6 * S :, col : col + S], joint[6 * S :, col + S : col + 2 * S]], axis=0)
     row, col = index // 4 * S, index % 4 * S
@@ -109,34 +110,38 @@
     return (block.astype(F32) + diag).astype(BF) if t - 4 == row else block
 
 
-def pack_kernel(cols_hbm, mask_hbm, h_hbm, x_hbm, joint_ref, xb_ref, table_ref, cols, mask, h_ref, x_ref, sems):
+def pack_h_kernel(cols_hbm, mask_hbm, h_hbm, send, table, cols, mask, h_ref, sems):
     pattern = [
         pltpu.make_async_copy(cols_hbm, cols, sems.at[0]),
         pltpu.make_async_copy(mask_hbm, mask, sems.at[1]),
     ]
-    h_copy = pltpu.make_async_copy(h_hbm, h_ref, sems.at[2])
-    x_copy = pltpu.make_async_copy(x_hbm, x_ref, sems.at[3])
-    for copy in pattern + [h_copy, x_copy]:
+    rows = [pltpu.make_async_copy(h_hbm.at[source_row(row)], h_ref.at[row], sems.at[2 + row]) for row in range(4)]
+    for copy in pattern + rows:
         copy.start()
     for copy in pattern:
         copy.wait()
-    fill_table(cols, mask, table_ref)
+    fill_table(cols, mask, table)
+    for row in range(4):
+        rows[row].wait()
+        for t in range(4, 12):
+            slot = table[12 * row + t]
+            block = h_ref[row, jnp.maximum(slot, 0)]
+            joint_send(send, row, t, jnp.where(slot >= 0, block, jnp.zeros_like(block)))
+
+
+def pack_x_kernel(table, x_ref, xa, xb):
     diag = eye()
-
-    h_copy.wait()
-    for row in range(4):
-        for t in range(4, 12):
-            joint_send(joint_ref, row, t, slot_block(h_ref, table_ref, row, t))
-    x_copy.wait()
     for index, (p, m) in enumerate(TRI):
-        joint_put(joint_ref, 26 + index, slot_block(x_ref, table_ref, 3 - p, 11 - m))
+        xa[index] = slot_block(x_ref, table, 3 - p, 11 - m)
     for row in range(4):
         for m in range(4):
-            put(xb_ref, 3 - row, 3 - m, x_slot_block(x_ref, table_ref, diag, row, 4 + m))
-
-
-def own_kernel(table, h_ref, x_ref, ho_ref, xo_ref):
+            put(xb, 3 - row, 3 - m, x_slot_block(x_ref, table, diag, row, 4 + m))
+
+
+def own_kernel(table, h_ref, x_ref, ho_ref, xo_ref, marks):
     diag = eye()
+    for i in range(48):
+        marks[i : i + 1, :] = jnp.full((1, S), jnp.where(table[i] >= 0, 1.0, 0.0), F32)
     for row in range(4):
         for t in range(12):
             put(ho_ref, row, t, slot_block(h_ref, table, row, t))
@@ -195,14 +200,17 @@
         for r in range(2):
             if (r, u) in ((1, 1), (0, 5)):
                 continue
-            total = None
+            xs, ys = [], []
             for t in range(6):
                 x = left(r, t)
                 y = None if x is None else right(t, u)
-                if y is None:
-                    continue
-                term = jnp.dot(x, y, preferred_element_type=F32)
-                total = term if total is None else total + term
+                if y is not None:
+                    xs.append(x)
+                    ys.append(y)
+            total = None
+            if xs:
+                x, y = jnp.concatenate(xs, axis=1), jnp.concatenate(ys, axis=0)
+                total = jnp.dot(x, y, preferred_element_type=F32)
             finish(r, u, total)
 
 
@@ -211,7 +219,7 @@
         for j in range(2):
             row, t = 2 * r + i, 2 * u + j
             block = total[i * S : (i + 1) * S, j * S : (j + 1) * S]
-            block = jnp.where(table_ref[12 * row + t] >= 0, block, 0.0)
+            block = jnp.where(table_ref[12 * row + t : 12 * row + t + 1, :] > 0.0, block, 0.0)
             store(row, t, block)
 
 
@@ -230,6 +238,11 @@
     product(left, right, range(6), lambda r, u, total: put_tile(part, r, u, total))
 
 
+def spread_kernel(xa, part, copy, square):
+    copy[...] = xa[...]
+    spread_mine(lambda i: xa[i], square)
+
+
 def half_kernel(table, xo, twin, part, half_ref, lc):
     spread_twin(lambda i: joint_block(twin, 16 + i), lc)
     half_ref[H:, H:Q] = jnp.zeros((H, H), BF)
@@ -243,10 +256,9 @@
     product(lambda r, t: left_tile(xo, r, t) if t in LEFT else None, right, range(6), keep)
 
 
-def start_kernel(factor, table, half, xo, joint, twin, xb, band, send, side, xlc, xrc):
-    spread_twin(lambda i: joint_block(twin, 26 + i), xlc)
-    spread_mine(lambda i: joint_block(joint, 26 + i), xrc)
-    right = right_operand(None, xlc, lambda r, u: tile(xo, r, u), xrc, xb)
+def center_kernel(factor, table, half, xo, xrc, xa2, band, send, xlc):
+    spread_twin(lambda i: xa2[i], xlc)
+    right = right_operand(None, xlc, lambda r, u: tile(xo, r, u), xrc, None)
     diag = eye()
 
     def start(r, u, total):
@@ -257,12 +269,26 @@
             value = value.astype(BF)
             put(band, row, t, value)
             joint_send(send, row, t, value)
-            if u in RIGHT and (3 - row, 11 - t) in TRI:
+
+        each_block(table, r, u, total, store)
+
+    product(lambda r, t: left_tile(half, r, t), right, OWN, start)
+
+
+def side_kernel(factor, table, half, xo, xb, band_in, send_in, band, send, side):
+    right = right_operand(None, None, lambda r, u: tile(xo, r, u), None, xb)
+
+    def start(r, u, total):
+        def store(row, t, block):
+            value = (-factor * block).astype(BF)
+            put(band, row, t, value)
+            joint_send(send, row, t, value)
+            if (3 - row, 11 - t) in TRI:
                 side[TRI.index((3 - row, 11 - t))] = value
 
         each_block(table, r, u, total, store)
 
-    product(lambda r, t: left_tile(half, r, t), right, OWN + RIGHT, start)
+    product(lambda r, t: left_tile(half, r, t), right, RIGHT, start)
 
 
 def mine_squares_kernel(table, band, joint, sq_r, part_l, sums, more, rc):
@@ -286,7 +312,7 @@
     product(square, right, OWN + RIGHT, lambda r, u, total: put_tile(more, r, u - 2, total))
 
 
-def late_kernel(table, band, sq_r, part_l, sums, more, twin, lc, sq, finish, after=None):
+def late_kernel(columns, table, band, sq_r, part_l, sums, more, twin, lc, sq, finish, after=None):
     spread_twin(lambda i: joint_block(twin, 16 + i), lc)
     right = right_operand(twin, lc, lambda r, u: tile(band, r, u), None, None)
 
@@ -317,29 +343,51 @@
             each_block(table, r, u, total, store)
 
         product(only(lambda r, t: left_tile(band, r, t), *LEFT), right, LEFT + OWN, keep)
-        product(only(lambda r, t: left_tile(sq, r, t), *LEFT, *OWN), right, OWN + RIGHT + LEFT, step)
+        product(only(lambda r, t: left_tile(sq, r, t), *LEFT, *OWN), right, columns, step)
         if after:
             after(half)
 
 
-def step_kernel(table, band, sq_r, part_l, sums, more, twin, new, send, lc, sq):
-    new[H:, H:Q] = jnp.zeros((H, H), BF)
-    new[:H, 2 * Q + H :] = jnp.zeros((H, H), BF)
-
+def step_kernel(table, band, sq_r, part_l, sums, more, twin, new, send, sq, lc):
     def finish(row, t, value):
         put(new, row, t, value)
         joint_send(send, row, t, value)
 
-    late_kernel(table, band, sq_r, part_l, sums, more, twin, lc, sq, finish)
-
-
-def last_kernel(cols, mask, table, band, sq_r, part_l, sums, more, twin, out_hbm, lc, sq, res, out, sems):
+    late_kernel(OWN + RIGHT, table, band, sq_r, part_l, sums, more, twin, lc, sq, finish)
+
+
+def step_left_kernel(table, band, sq, twin, new_in, new):
+    new[H:, H:Q] = jnp.zeros((H, H), BF)
+    new[:H, 2 * Q + H :] = jnp.zeros((H, H), BF)
+    right = right_operand(twin, None, lambda r, u: tile(band, r, u), None, None)
+
+    def step(r, u, total):
+        def store(row, t, block):
+            now = sq[row * S : (row + 1) * S, t * S : (t + 1) * S]
+            put(new, row, t, (3.0 * now.astype(F32) - 2.0 * block).astype(BF))
+
+        each_block(table, r, u, total, store)
+
+    product(lambda r, t: None if t in RIGHT else left_tile(sq, r, t), right, LEFT, step)
+
+
+def last_kernel(cols_hbm, mask_hbm, table, band, sq_r, part_l, sums, more, twin, out_hbm, *scratch):
+    lc, sq, res, out, sems, cols, mask = scratch
     core = lax.axis_index("rep")
+    pattern = [
+        pltpu.make_async_copy(cols_hbm, cols, sems.at[4]),
+        pltpu.make_async_copy(mask_hbm, mask, sems.at[5]),
+    ]
+    for one in pattern:
+        one.start()
 
     def copy(row):
         return pltpu.make_async_copy(out.at[row], out_hbm.at[source_row(row)], sems.at[row])
 
     def after(half):
+        if half == 0:
+            for one in pattern:
+                one.wait()
         for row in (2 * half, 2 * half + 1):
             for s in range(4):
                 active, unused, t = place(cols, mask, source_row(row), core * 4 + s)
@@ -348,7 +396,7 @@
             copy(row).start()
 
     late_kernel(
-        table, band, sq_r, part_l, sums, more, twin, lc, sq, lambda row, t, value: put(res, row, t, value), after
+        LEFT + OWN + RIGHT, table, band, sq_r, part_l, sums, more, twin, lc, sq, lambda row, t, value: put(res, row, t, value), after
     )
     for row in range(4):
         copy(row).wait()
@@ -376,38 +424,57 @@
     hbm = pl.BlockSpec(memory_space=pltpu.HBM)
 
     index_table = jax.ShapeDtypeStruct((49,), jnp.int32)
-    joint, xb, table = call(
-        pack_kernel,
-        [jax.ShapeDtypeStruct((9 * S, Q), BF), SQUARE, index_table],
-        [VMEM, VMEM, SMEM],
-        [hbm] * 4,
+    h_send, table = call(
+        pack_h_kernel,
+        [SEND, index_table],
+        [VMEM, SMEM],
+        [hbm] * 3,
         [
             pltpu.SMEM(cols.shape, jnp.int32),
             pltpu.SMEM(mask.shape, jnp.int32),
             pltpu.VMEM(hamiltonian.shape, BF),
-            pltpu.VMEM(x_correction.shape, BF),
-            pltpu.SemaphoreType.DMA((4,)),
+            pltpu.SemaphoreType.DMA((6,)),
         ],
         flops,
-        cols, mask, hamiltonian, x_correction,
+        cols, mask, hamiltonian,
         room=56,
     )
-    joint_in = link(joint)
-    xb_in = link(xb)
-    ho, xo = call(
-        own_kernel, [BANDED, BANDED], [VMEM] * 2, [SMEM, VMEM, VMEM], [], 0, table, hamiltonian, x_correction
+    h_halo = link(h_send)
+    xa, xb = call(pack_x_kernel, [CORNER, SQUARE], [VMEM] * 2, [SMEM, VMEM], [], 0, table, x_correction)
+    xa_halo = link(xa)
+    xb_halo = link(xb)
+    ho, xo, marks = call(
+        own_kernel,
+        [BANDED, BANDED, jax.ShapeDtypeStruct((48, S), F32)],
+        [VMEM] * 3,
+        [SMEM, VMEM, VMEM],
+        [],
+        0,
+        table, hamiltonian, x_correction,
     )
-    twin = swap(joint_in)
-    part = call(mine_kernel, WIDE, VMEM, [VMEM] * 3, [square], 64 * flops, xo, ho, joint_in)
-    half = call(half_kernel, BANDED, VMEM, [SMEM] + [VMEM] * 3, [square], flops, table, xo, twin, part)
+    h_twin = swap(h_halo)
+    part = call(mine_kernel, WIDE, VMEM, [VMEM] * 3, [square], 64 * flops, xo, ho, h_halo)
+    xa_copy, x_corner = call(spread_kernel, [CORNER, SQUARE], [VMEM] * 2, [VMEM] * 2, [], 0, xa_halo, part)
+    xa_twin = swap(xa_copy)
+    half = call(half_kernel, BANDED, VMEM, [VMEM] + [VMEM] * 3, [square], 16 * flops, marks, xo, h_twin, part)
+    band, send = call(
+        lambda *refs: center_kernel(factor, *refs),
+        [BANDED, SEND],
+        [VMEM] * 2,
+        [VMEM] * 5,
+        [square],
+        flops,
+        marks, half, xo, x_corner, xa_twin,
+    )
     band, send, side = call(
-        lambda *refs: start_kernel(factor, *refs),
+        lambda *refs: side_kernel(factor, *refs),
         [BANDED, SEND, CORNER],
         [VMEM] * 3,
-        [SMEM] + [VMEM] * 5,
-        [square] * 2,
+        [VMEM] * 6,
+        [],
         flops,
-        table, half, xo, joint_in, twin, xb_in,
+        marks, half, xo, xb_halo, band, send,
+        alias={4: 0, 5: 1},
     )
     halo = link(send)
     band = call(join_kernel, BANDED, VMEM, [VMEM] * 2, [], 0, band, swap(side))
@@ -419,31 +486,35 @@
             mine_squares_kernel,
             [SQUARE, SUMS, SUMS, jax.ShapeDtypeStruct((Q, 2 * Q), F32)],
             [VMEM] * 4,
-            [SMEM] + [VMEM] * 2,
+            [VMEM] + [VMEM] * 2,
             [square],
             64 * flops,
-            table, band, halo,
+            marks, band, halo,
         )
-        operands = (table, band, sq_r, part_l, sums, more, twin)
+        operands = (marks, band, sq_r, part_l, sums, more, twin)
         if step + 1 == STEPS:
             return call(
                 last_kernel,
                 jax.ShapeDtypeStruct((4, 4, S, S), BF),
                 hbm,
-                [SMEM] * 3 + [VMEM] * 6,
+                [hbm] * 2 + [VMEM] * 7,
                 [square, pltpu.VMEM((Q, 2 * Q), BF)]
-                + [pltpu.VMEM((Q, 3 * Q), BF), pltpu.VMEM((4, 4, S, S), BF), pltpu.SemaphoreType.DMA((4,))],
+                + [pltpu.VMEM((Q, 3 * Q), BF), pltpu.VMEM((4, 4, S, S), BF), pltpu.SemaphoreType.DMA((6,))]
+                + [pltpu.SMEM(cols.shape, jnp.int32), pltpu.SMEM(mask.shape, jnp.int32)],
                 flops,
                 cols, mask, *operands,
             )
-        band, send = call(
+        new, send, sq = call(
             step_kernel,
-            [BANDED, SEND],
-            [VMEM] * 2,
-            [SMEM] + [VMEM] * 6,
-            [square, pltpu.VMEM((Q, 2 * Q), BF)],
+            [BANDED, SEND, jax.ShapeDtypeStruct((Q, 2 * Q), BF)],
+            [VMEM] * 3,
+            [VMEM] * 7,
+            [square],
             flops,
             *operands,
+        )
+        band = call(
+            step_left_kernel, BANDED, VMEM, [VMEM] * 5, [], 0, marks, band, sq, twin, new, alias={4: 0}
         )
 
 

time: 91.9 us -> 89.7 us (0.976)
  starting transfers between devices: 41 us -> 48.9 us
  waiting for transfers between devices: 31.1 us -> 24.1 us
  Pallas kernels: 18.6 us -> 15.4 us
    ppermute x4 -> x5, waiting for transfers between devices: 27.2 us -> 20.1 us  [link(): return lax.ppermute(x, ('rows', 'rep'), outward)]
    ppermute x4 -> x5, starting transfers between devices: 33.4 us -> 38.8 us  [link(): return lax.ppermute(x, ('rows', 'rep'), outward)]
    pallas_call x10 -> x14, Pallas kernels: 18.6 us -> 15.4 us  [call(): pl.pallas_call(kernel, out_shape=outs, in_specs=in_specs, out_specs=out_s...]
    ppermute x4 -> x5, starting transfers between devices: 7.65 us -> 10.1 us  [swap(): return lax.ppermute(x, 'rep', [(0, 1), (1, 0)])]
    ppermute x4 -> x5, waiting for transfers between devices: 3.88 us -> 3.96 us  [swap(): return lax.ppermute(x, 'rep', [(0, 1), (1, 0)])]
  transfers between devices with their start and end apart: 8 -> 10, of which waited for: 7 -> 6; matrix products, arithmetic and copies ran while one was open for 0% -> 0% of each run, Pallas kernels for 8% -> 9%
where the time goes in v3:
time: 89.7 us; the launch traced here: 89.3 us
  starting transfers between devices  48.9 us (55%)
  waiting for transfers between devices  24.1 us (27%)
  Pallas kernels  15.4 us (17%)
    ppermute x5, starting transfers between devices, link(): return lax.ppermute(x, ('rows', 'rep'), outward)  38.8 us
    ppermute x5, waiting for transfers between devices, link(): return lax.ppermute(x, ('rows', 'rep'), outward)  20.1 us
    pallas_call x14, Pallas kernels, call(): pl.pallas_call(kernel, out_shape=outs, in_specs=in_specs, out_specs=out_s...  15.4 us
    ppermute x5, starting transfers between devices, swap(): return lax.ppermute(x, 'rep', [(0, 1), (1, 0)])  10.1 us
    ppermute x5, waiting for transfers between devices, swap(): return lax.ppermute(x, 'rep', [(0, 1), (1, 0)])  3.96 us
  transfers between devices with their start and end apart: 10, of which 6 were waited for; matrix products, arithmetic and copies ran while one was open for 0% of the time, Pallas kernels for 9%

profile of v3, /device:TPU:33, one launch (start us, length us, event | category | flops | bytes accessed | tf_op | source)
XLA Modules:
  0.0 89.3 jit_solution(1920995494037191106)
XLA Ops:
  0.0 0.0 copy-start
  0.0 0.0 copy-start.1
  0.0 2.4 %shard_map.46 = (bf16[832,512]{1,0:T(8,128)(2,1)}, s32[49]{0:T(128)}) custom-call(s32[4,8]{1,0:T(4,128)} %cols_hbm.3, s32[4,8]{1,0:T(4,128)} %mask_hbm.3, bf16[4,8,128,128]{3,2,1,0:T(8,128)(2,1)} %h_ref.1), custom_call_target="tpu_custom_call" | custom-call | flops 536870912 | bytes 4194304 | tf_op jit(solution)/shard_map/pallas_call | solution.py:31
  2.4 13.3 %collective-permute-start = (bf16[832,512]{1,0:T(8,128)(2,1)}, bf16[832,512]{1,0:T(8,128)(2,1)S(1)}, u32[]{:S(2)}, u32[]{:S(2)}) collective-permute-start(bf16[832,512]{1,0:T(8,128)(2,1)} %get-tuple-element.33), channel_id=1, source_target_pairs={{0,3},{2,5},{4,7},{6,9},{8,11},{10,13},{12,15},{14,17},{16,19},{18... | collective-permute-start | bytes 2555912 | tf_op jit(solution)/shard_map/ppermute | solution.py:417
  15.7 0.0 copy-done
  15.7 0.0 copy-start.2
  15.7 0.6 copy-done.2
  16.4 0.8 shard_map.50
  17.1 1.9 %collective-permute-start.3 = (bf16[10,128,128]{2,1,0:T(8,128)(2,1)S(1)}, bf16[10,128,128]{2,1,0:T(8,128)(2,1)S(1)}, u32[]{:S(2)}, u32[]{:S(2)}) collective-permute-start(bf16[10,128,128]{2,1,0:T(8,128)(2,1)S(1)} %get-tuple-element.36), channel_id=1, source_target_pairs={{0,3},{2,5},{4,7},{6,9},{8,11},{10,13},{12,15},{14,17},{16,19},{18... | collective-permute-start | bytes 983048 | tf_op jit(solution)/shard_map/ppermute | solution.py:417
  19.1 9.1 %collective-permute-start.2 = (bf16[512,512]{1,0:T(8,128)(2,1)S(1)}, bf16[512,512]{1,0:T(8,128)(2,1)S(1)}, u32[]{:S(2)}, u32[]{:S(2)}) collective-permute-start(bf16[512,512]{1,0:T(8,128)(2,1)S(1)} %get-tuple-element.35), channel_id=1, source_target_pairs={{0,3},{2,5},{4,7},{6,9},{8,11},{10,13},{12,15},{14,17},{16,19},{18... | collective-permute-start | bytes 1572872 | tf_op jit(solution)/shard_map/ppermute | solution.py:417
  28.1 0.0 copy-done.1
  28.2 1.3 %shard_map.47 = (bf16[512,1536]{1,0:T(8,128)(2,1)S(1)}, bf16[512,1536]{1,0:T(8,128)(2,1)S(1)}, f32[48,128]{1,0:T(8,128)S(1)}) custom-call(s32[49]{0:T(128)S(1)} %copy-done.2, bf16[4,8,128,128]{3,2,1,0:T(8,128)(2,1)S(1)} %copy-done.1, bf16[4,8,128,128]{3,2,1,0:T(8,128)(2,1)S(1)} %copy-done), custom_call_target="tpu_custom_call" | custom-call | bytes 4194304 | tf_op jit(solution)/shard_map/pallas_call | solution.py:31
  29.5 0.0 collective-permute-done.joint
  29.5 1.9 %collective-permute-start.1 = (bf16[832,512]{1,0:T(8,128)(2,1)S(1)}, bf16[832,512]{1,0:T(8,128)(2,1)S(1)}, u32[]{:S(2)}, u32[]{:S(2)}) collective-permute-start(bf16[832,512]{1,0:T(8,128)(2,1)S(1)} %collective-permute-done.joint), channel_id=1, source_target_pairs={{0,1},{1,0},{2,3},{3,2},{4,5},{5,4},{6,7},{7,6},{8,9},{9,8},{10,11... | collective-permute-start | bytes 2555912 | tf_op jit(solution)/shard_map/ppermute | solution.py:420
  31.4 1.1 %shard_map.48.part = f32[512,1536]{1,0:T(8,128)S(1)} custom-call(bf16[512,1536]{1,0:T(8,128)(2,1)S(1)} %get-tuple-element.32.xo.refs_2_, bf16[512,1536]{1,0:T(8,128)(2,1)S(1)} %get-tuple-element.34.ho, bf16[832,512]{1,0:T(8,128)(2,1)S(1)} %collective-permute-done.joint), custom_call_target="tpu_custom_call" | custom-call | flops 34359738368 | bytes 4194304 | tf_op jit(solution)/shard_map/pallas_call | solution.py:31
  32.6 0.0 collective-permute-done.3.xa
  32.6 0.1 shard_map.51
  32.7 2.4 %collective-permute-start.4 = (bf16[10,128,128]{2,1,0:T(8,128)(2,1)S(1)}, bf16[10,128,128]{2,1,0:T(8,128)(2,1)S(1)}, u32[]{:S(2)}, u32[]{:S(2)}) collective-permute-start(bf16[10,128,128]{2,1,0:T(8,128)(2,1)S(1)} %get-tuple-element.38), channel_id=1, source_target_pairs={{0,1},{1,0},{2,3},{3,2},{4,5},{5,4},{6,7},{7,6},{8,9},{9,8},{10,11... | collective-permute-start | bytes 983048 | tf_op jit(solution)/shard_map/ppermute | solution.py:420
  35.1 0.0 collective-permute-done.1.twin
  35.1 0.6 shard_map.49.refs_1_
  35.7 0.6 collective-permute-done.4.refs_4_
  36.3 0.8 shard_map.52
  37.2 0.0 collective-permute-done.2.refs_3_
  37.2 0.5 shard_map.53
  37.8 7.3 %collective-permute-start.6 = (bf16[832,512]{1,0:T(8,128)(2,1)S(1)}, bf16[832,512]{1,0:T(8,128)(2,1)S(1)}, u32[]{:S(2)}, u32[]{:S(2)}) collective-permute-start(bf16[832,512]{1,0:T(8,128)(2,1)S(1)} %get-tuple-element.43), channel_id=1, source_target_pairs={{0,3},{2,5},{4,7},{6,9},{8,11},{10,13},{12,15},{14,17},{16,19},{18... | collective-permute-start | bytes 2555912 | tf_op jit(solution)/shard_map/ppermute | solution.py:417
  45.0 1.9 %collective-permute-start.5 = (bf16[10,128,128]{2,1,0:T(8,128)(2,1)S(1)}, bf16[10,128,128]{2,1,0:T(8,128)(2,1)S(1)}, u32[]{:S(2)}, u32[]{:S(2)}) collective-permute-start(bf16[10,128,128]{2,1,0:T(8,128)(2,1)S(1)} %get-tuple-element.42), channel_id=1, source_target_pairs={{0,1},{1,0},{2,3},{3,2},{4,5},{5,4},{6,7},{7,6},{8,9},{9,8},{10,11... | collective-permute-start | bytes 983048 | tf_op jit(solution)/shard_map/ppermute | solution.py:420
  46.9 1.6 %collective-permute-done.5.side = bf16[10,128,128]{2,1,0:T(8,128)(2,1)S(1)} collective-permute-done((bf16[10,128,128]{2,1,0:T(8,128)(2,1)S(1)}, bf16[10,128,128]{2,1,0:T(8,128)(2,1)S(1)}, u32[]{:S(2)}, u32[]{:S(2)}) %collective-permute-start.5) | collective-permute-done | bytes 327712 | tf_op jit(solution)/shard_map/ppermute | solution.py:420
  48.5 0.1 shard_map.54.band
  48.7 8.5 %collective-permute-done.6.joint = bf16[832,512]{1,0:T(8,128)(2,1)S(1)} collective-permute-done((bf16[832,512]{1,0:T(8,128)(2,1)S(1)}, bf16[832,512]{1,0:T(8,128)(2,1)S(1)}, u32[]{:S(2)}, u32[]{:S(2)}) %collective-permute-start.6) | collective-permute-done | bytes 852000 | tf_op jit(solution)/shard_map/ppermute | solution.py:417
  57.2 1.9 %collective-permute-start.7 = (bf16[832,512]{1,0:T(8,128)(2,1)S(1)}, bf16[832,512]{1,0:T(8,128)(2,1)S(1)}, u32[]{:S(2)}, u32[]{:S(2)}) collective-permute-start(bf16[832,512]{1,0:T(8,128)(2,1)S(1)} %collective-permute-done.6.joint), channel_id=1, source_target_pairs={{0,1},{1,0},{2,3},{3,2},{4,5},{5,4},{6,7},{7,6},{8,9},{9,8},{10,11... | collective-permute-start | bytes 2555912 | tf_op jit(solution)/shard_map/ppermute | solution.py:420
  59.1 1.5 %shard_map.55 = (bf16[512,512]{1,0:T(8,128)(2,1)S(1)}, f32[512,512]{1,0:T(8,128)S(1)}, f32[512,512]{1,0:T(8,128)S(1)}, f32[512,1024]{1,0:T(8,128)S(1)}) custom-call(f32[48,128]{1,0:T(8,128)S(1)} %get-tuple-element.31.table.refs_0_, bf16[512,1536]{1,0:T(8,128)(2,1)S(1)} %shard_map.54.band, bf16[832,512]{1,0:T(8,128)(2,1)S(1)} %collective-permute-done.6.joint), custom_call_target="tpu_custom_call" | custom-call | flops 34359738368 | bytes 4194304 | tf_op jit(solution)/shard_map/pallas_call | solution.py:31
  60.6 0.9 collective-permute-done.7.twin
  61.5 1.3 %shard_map.56 = (bf16[512,1536]{1,0:T(8,128)(2,1)S(1)}, bf16[832,512]{1,0:T(8,128)(2,1)S(1)}, bf16[512,1024]{1,0:T(8,128)(2,1)S(1)}) custom-call(f32[48,128]{1,0:T(8,128)S(1)} %get-tuple-element.31.table.refs_0_, bf16[512,1536]{1,0:T(8,128)(2,1)S(1)} %shard_map.54.band, bf16[512,512]{1,0:T(8,128)(2,1)S(1)} %get-tuple-element.44.sq_r, ...), custom_call_target="tpu_custom_call" | custom-call | flops 536870912 | bytes 4194304 | tf_op jit(solution)/shard_map/pallas_call | solution.py:31
  62.8 7.3 %collective-permute-start.8 = (bf16[832,512]{1,0:T(8,128)(2,1)S(1)}, bf16[832,512]{1,0:T(8,128)(2,1)S(1)}, u32[]{:S(2)}, u32[]{:S(2)}) collective-permute-start(bf16[832,512]{1,0:T(8,128)(2,1)S(1)} %get-tuple-element.50), channel_id=1, source_target_pairs={{0,3},{2,5},{4,7},{6,9},{8,11},{10,13},{12,15},{14,17},{16,19},{18... | collective-permute-start | bytes 2555912 | tf_op jit(solution)/shard_map/ppermute | solution.py:417
  70.1 0.5 shard_map.57.band
  70.6 0.0 copy-start.3
  70.6 0.0 copy-start.4
  70.6 11.6 %collective-permute-done.8.joint = bf16[832,512]{1,0:T(8,128)(2,1)S(1)} collective-permute-done((bf16[832,512]{1,0:T(8,128)(2,1)S(1)}, bf16[832,512]{1,0:T(8,128)(2,1)S(1)}, u32[]{:S(2)}, u32[]{:S(2)}) %collective-permute-start.8) | collective-permute-done | bytes 852000 | tf_op jit(solution)/shard_map/ppermute | solution.py:417
  82.2 1.9 %collective-permute-start.9 = (bf16[832,512]{1,0:T(8,128)(2,1)S(1)}, bf16[832,512]{1,0:T(8,128)(2,1)S(1)}, u32[]{:S(2)}, u32[]{:S(2)}) collective-permute-start(bf16[832,512]{1,0:T(8,128)(2,1)S(1)} %collective-permute-done.8.joint), channel_id=1, source_target_pairs={{0,1},{1,0},{2,3},{3,2},{4,5},{5,4},{6,7},{7,6},{8,9},{9,8},{10,11... | collective-permute-start | bytes 2555912 | tf_op jit(solution)/shard_map/ppermute | solution.py:420
  84.2 1.5 %shard_map.58 = (bf16[512,512]{1,0:T(8,128)(2,1)S(1)}, f32[512,512]{1,0:T(8,128)S(1)}, f32[512,512]{1,0:T(8,128)S(1)}, f32[512,1024]{1,0:T(8,128)S(1)}) custom-call(f32[48,128]{1,0:T(8,128)S(1)} %get-tuple-element.31.table.refs_0_, bf16[512,1536]{1,0:T(8,128)(2,1)S(1)} %shard_map.57.band, bf16[832,512]{1,0:T(8,128)(2,1)S(1)} %collective-permute-done.8.joint), custom_call_target="tpu_custom_call" | custom-call | flops 34359738368 | bytes 4194304 | tf_op jit(solution)/shard_map/pallas_call | solution.py:31
  85.6 0.9 collective-permute-done.9.twin
  86.5 0.0 copy-done.3
  86.5 0.0 copy-done.4
  86.5 2.8 %shard_map.59 = bf16[4,4,128,128]{3,2,1,0:T(8,128)(2,1)} custom-call(s32[4,8]{1,0:T(4,128)S(1)} %copy-done.3, s32[4,8]{1,0:T(4,128)S(1)} %copy-done.4, f32[48,128]{1,0:T(8,128)S(1)} %get-tuple-element.31.table.refs_0_, bf16[512,1536]{1,0:T(8,128)(2,1)S(1)} %shard_map.57.band, bf16[512,512]{1,0:T(8,128)(2,1)S(1)} %get-tuple-element.51.sq_r, ...), custom_call_target="tpu_custom_call" | custom-call | flops 536870912 | bytes 4194304 | tf_op jit(solution)/shard_map/pallas_call | solution.py:31
Async XLA Ops:
  0.0 15.7 %copy-start = (bf16[4,8,128,128]{3,2,1,0:T(8,128)(2,1)S(1)}, bf16[4,8,128,128]{3,2,1,0:T(8,128)(2,1)}, u32[]{:S(2)}) copy-start(bf16[4,8,128,128]{3,2,1,0:T(8,128)(2,1)} %x_ref.3) | copy-start | bytes 3145732
  0.0 28.1 %copy-start.1 = (bf16[4,8,128,128]{3,2,1,0:T(8,128)(2,1)S(1)}, bf16[4,8,128,128]{3,2,1,0:T(8,128)(2,1)}, u32[]{:S(2)}) copy-start(bf16[4,8,128,128]{3,2,1,0:T(8,128)(2,1)} %h_ref.1) | copy-start | bytes 3145732
  2.4 27.1 %collective-permute-start = (bf16[832,512]{1,0:T(8,128)(2,1)}, bf16[832,512]{1,0:T(8,128)(2,1)S(1)}, u32[]{:S(2)}, u32[]{:S(2)}) collective-permute-start(bf16[832,512]{1,0:T(8,128)(2,1)} %get-tuple-element.33), channel_id=1, source_target_pairs={{0,3},{2,5},{4,7},{6,9},{8,11},{10,13},{12,15},{14,17},{16,19},{18... | collective-permute-start | bytes 2555912 | tf_op jit(solution)/shard_map/ppermute | solution.py:417
  15.7 0.7 copy-start.2
  17.1 15.4 %collective-permute-start.3 = (bf16[10,128,128]{2,1,0:T(8,128)(2,1)S(1)}, bf16[10,128,128]{2,1,0:T(8,128)(2,1)S(1)}, u32[]{:S(2)}, u32[]{:S(2)}) collective-permute-start(bf16[10,128,128]{2,1,0:T(8,128)(2,1)S(1)} %get-tuple-element.36), channel_id=1, source_target_pairs={{0,3},{2,5},{4,7},{6,9},{8,11},{10,13},{12,15},{14,17},{16,19},{18... | collective-permute-start | bytes 983048 | tf_op jit(solution)/shard_map/ppermute | solution.py:417
  19.1 18.1 %collective-permute-start.2 = (bf16[512,512]{1,0:T(8,128)(2,1)S(1)}, bf16[512,512]{1,0:T(8,128)(2,1)S(1)}, u32[]{:S(2)}, u32[]{:S(2)}) collective-permute-start(bf16[512,512]{1,0:T(8,128)(2,1)S(1)} %get-tuple-element.35), channel_id=1, source_target_pairs={{0,3},{2,5},{4,7},{6,9},{8,11},{10,13},{12,15},{14,17},{16,19},{18... | collective-permute-start | bytes 1572872 | tf_op jit(solution)/shard_map/ppermute | solution.py:417
  29.5 5.6 %collective-permute-start.1 = (bf16[832,512]{1,0:T(8,128)(2,1)S(1)}, bf16[832,512]{1,0:T(8,128)(2,1)S(1)}, u32[]{:S(2)}, u32[]{:S(2)}) collective-permute-start(bf16[832,512]{1,0:T(8,128)(2,1)S(1)} %collective-permute-done.joint), channel_id=1, source_target_pairs={{0,1},{1,0},{2,3},{3,2},{4,5},{5,4},{6,7},{7,6},{8,9},{9,8},{10,11... | collective-permute-start | bytes 2555912 | tf_op jit(solution)/shard_map/ppermute | solution.py:420
  32.7 3.6 %collective-permute-start.4 = (bf16[10,128,128]{2,1,0:T(8,128)(2,1)S(1)}, bf16[10,128,128]{2,1,0:T(8,128)(2,1)S(1)}, u32[]{:S(2)}, u32[]{:S(2)}) collective-permute-start(bf16[10,128,128]{2,1,0:T(8,128)(2,1)S(1)} %get-tuple-element.38), channel_id=1, source_target_pairs={{0,1},{1,0},{2,3},{3,2},{4,5},{5,4},{6,7},{7,6},{8,9},{9,8},{10,11... | collective-permute-start | bytes 983048 | tf_op jit(solution)/shard_map/ppermute | solution.py:420
  37.8 19.4 %collective-permute-start.6 = (bf16[832,512]{1,0:T(8,128)(2,1)S(1)}, bf16[832,512]{1,0:T(8,128)(2,1)S(1)}, u32[]{:S(2)}, u32[]{:S(2)}) collective-permute-start(bf16[832,512]{1,0:T(8,128)(2,1)S(1)} %get-tuple-element.43), channel_id=1, source_target_pairs={{0,3},{2,5},{4,7},{6,9},{8,11},{10,13},{12,15},{14,17},{16,19},{18... | collective-permute-start | bytes 2555912 | tf_op jit(solution)/shard_map/ppermute | solution.py:417
  45.0 3.5 %collective-permute-start.5 = (bf16[10,128,128]{2,1,0:T(8,128)(2,1)S(1)}, bf16[10,128,128]{2,1,0:T(8,128)(2,1)S(1)}, u32[]{:S(2)}, u32[]{:S(2)}) collective-permute-start(bf16[10,128,128]{2,1,0:T(8,128)(2,1)S(1)} %get-tuple-element.42), channel_id=1, source_target_pairs={{0,1},{1,0},{2,3},{3,2},{4,5},{5,4},{6,7},{7,6},{8,9},{9,8},{10,11... | collective-permute-start | bytes 983048 | tf_op jit(solution)/shard_map/ppermute | solution.py:420
  57.2 4.3 %collective-permute-start.7 = (bf16[832,512]{1,0:T(8,128)(2,1)S(1)}, bf16[832,512]{1,0:T(8,128)(2,1)S(1)}, u32[]{:S(2)}, u32[]{:S(2)}) collective-permute-start(bf16[832,512]{1,0:T(8,128)(2,1)S(1)} %collective-permute-done.6.joint), channel_id=1, source_target_pairs={{0,1},{1,0},{2,3},{3,2},{4,5},{5,4},{6,7},{7,6},{8,9},{9,8},{10,11... | collective-permute-start | bytes 2555912 | tf_op jit(solution)/shard_map/ppermute | solution.py:420
  62.8 19.4 %collective-permute-start.8 = (bf16[832,512]{1,0:T(8,128)(2,1)S(1)}, bf16[832,512]{1,0:T(8,128)(2,1)S(1)}, u32[]{:S(2)}, u32[]{:S(2)}) collective-permute-start(bf16[832,512]{1,0:T(8,128)(2,1)S(1)} %get-tuple-element.50), channel_id=1, source_target_pairs={{0,3},{2,5},{4,7},{6,9},{8,11},{10,13},{12,15},{14,17},{16,19},{18... | collective-permute-start | bytes 2555912 | tf_op jit(solution)/shard_map/ppermute | solution.py:417
  70.6 15.9 %copy-start.3 = (s32[4,8]{1,0:T(4,128)S(1)}, s32[4,8]{1,0:T(4,128)}, u32[]{:S(2)}) copy-start(s32[4,8]{1,0:T(4,128)} %cols_hbm.3) | copy-start | bytes 388
  70.6 15.9 %copy-start.4 = (s32[4,8]{1,0:T(4,128)S(1)}, s32[4,8]{1,0:T(4,128)}, u32[]{:S(2)}) copy-start(s32[4,8]{1,0:T(4,128)} %mask_hbm.3) | copy-start | bytes 388
  82.2 4.3 %collective-permute-start.9 = (bf16[832,512]{1,0:T(8,128)(2,1)S(1)}, bf16[832,512]{1,0:T(8,128)(2,1)S(1)}, u32[]{:S(2)}, u32[]{:S(2)}) collective-permute-start(bf16[832,512]{1,0:T(8,128)(2,1)S(1)} %collective-permute-done.8.joint), channel_id=1, source_target_pairs={{0,1},{1,0},{2,3},{3,2},{4,5},{5,4},{6,7},{7,6},{8,9},{9,8},{10,11... | collective-permute-start | bytes 2555912 | tf_op jit(solution)/shard_map/ppermute | solution.py:420

commit v4 on v3

--- a/solution.py
+++ b/solution.py
@@ -99,10 +99,14 @@
     return jnp.where(lax.axis_index("rep") == 1, 3 - row, row)
 
 
+def row_block(ref, table, row, t, source=None):
+    slot = table[12 * row + t]
+    block = ref[row if source is None else source, jnp.maximum(slot, 0)]
+    return jnp.where(slot >= 0, block, jnp.zeros_like(block))
+
+
 def slot_block(ref, table, row, t):
-    slot = table[12 * row + t]
-    block = ref[source_row(row), jnp.maximum(slot, 0)]
-    return jnp.where(slot >= 0, block, jnp.zeros_like(block))
+    return row_block(ref, table, row, t, source_row(row))
 
 
 def x_slot_block(ref, table, diag, row, t):
@@ -110,7 +114,7 @@
     return (block.astype(F32) + diag).astype(BF) if t - 4 == row else block
 
 
-def pack_h_kernel(cols_hbm, mask_hbm, h_hbm, send, table, cols, mask, h_ref, sems):
+def pack_h_kernel(cols_hbm, mask_hbm, h_hbm, send, table, h_ref, cols, mask, sems):
     pattern = [
         pltpu.make_async_copy(cols_hbm, cols, sems.at[0]),
         pltpu.make_async_copy(mask_hbm, mask, sems.at[1]),
@@ -124,28 +128,18 @@
     for row in range(4):
         rows[row].wait()
         for t in range(4, 12):
-            slot = table[12 * row + t]
-            block = h_ref[row, jnp.maximum(slot, 0)]
-            joint_send(send, row, t, jnp.where(slot >= 0, block, jnp.zeros_like(block)))
-
-
-def pack_x_kernel(table, x_ref, xa, xb):
+            joint_send(send, row, t, row_block(h_ref, table, row, t))
+
+
+def pack_x_kernel(table, x_ref, xa, xb, marks):
     diag = eye()
     for index, (p, m) in enumerate(TRI):
         xa[index] = slot_block(x_ref, table, 3 - p, 11 - m)
     for row in range(4):
         for m in range(4):
             put(xb, 3 - row, 3 - m, x_slot_block(x_ref, table, diag, row, 4 + m))
-
-
-def own_kernel(table, h_ref, x_ref, ho_ref, xo_ref, marks):
-    diag = eye()
     for i in range(48):
         marks[i : i + 1, :] = jnp.full((1, S), jnp.where(table[i] >= 0, 1.0, 0.0), F32)
-    for row in range(4):
-        for t in range(12):
-            put(ho_ref, row, t, slot_block(h_ref, table, row, t))
-            put(xo_ref, row, t, x_slot_block(x_ref, table, diag, row, t))
 
 
 def spread_mine(get, square_ref):
@@ -231,7 +225,12 @@
     ref[i * H : (i + 1) * H, j * H : (j + 1) * H] = value
 
 
-def mine_kernel(xo, ho, joint, part, rc):
+def mine_kernel(table, h_ref, x_ref, joint, xo, part, ho, rc):
+    diag = eye()
+    for row in range(4):
+        for t in range(12):
+            put(ho, row, t, row_block(h_ref, table, row, t))
+            put(xo, row, t, x_slot_block(x_ref, table, diag, row, t))
     spread_mine(lambda i: joint_block(joint, 16 + i), rc)
     right = right_operand(None, None, lambda r, u: tile(ho, r, u), rc, joint)
     left = lambda r, t: None if t in LEFT else left_tile(xo, r, t)
@@ -424,36 +423,41 @@
     hbm = pl.BlockSpec(memory_space=pltpu.HBM)
 
     index_table = jax.ShapeDtypeStruct((49,), jnp.int32)
-    h_send, table = call(
+    h_send, table, h_rows = call(
         pack_h_kernel,
-        [SEND, index_table],
-        [VMEM, SMEM],
+        [SEND, index_table, jax.ShapeDtypeStruct(hamiltonian.shape, BF)],
+        [VMEM, SMEM, VMEM],
         [hbm] * 3,
         [
             pltpu.SMEM(cols.shape, jnp.int32),
             pltpu.SMEM(mask.shape, jnp.int32),
-            pltpu.VMEM(hamiltonian.shape, BF),
             pltpu.SemaphoreType.DMA((6,)),
         ],
         flops,
-        cols, mask, hamiltonian,
-        room=56,
+        *(pltpu.with_memory_space_constraint(x, pltpu.HBM) for x in (cols, mask, hamiltonian)),
     )
     h_halo = link(h_send)
-    xa, xb = call(pack_x_kernel, [CORNER, SQUARE], [VMEM] * 2, [SMEM, VMEM], [], 0, table, x_correction)
+    xa, xb, marks = call(
+        pack_x_kernel,
+        [CORNER, SQUARE, jax.ShapeDtypeStruct((48, S), F32)],
+        [VMEM] * 3,
+        [SMEM, VMEM],
+        [],
+        0,
+        table, x_correction,
+    )
     xa_halo = link(xa)
     xb_halo = link(xb)
-    ho, xo, marks = call(
-        own_kernel,
-        [BANDED, BANDED, jax.ShapeDtypeStruct((48, S), F32)],
-        [VMEM] * 3,
-        [SMEM, VMEM, VMEM],
-        [],
-        0,
-        table, hamiltonian, x_correction,
-    )
     h_twin = swap(h_halo)
-    part = call(mine_kernel, WIDE, VMEM, [VMEM] * 3, [square], 64 * flops, xo, ho, h_halo)
+    xo, part = call(
+        mine_kernel,
+        [BANDED, WIDE],
+        [VMEM] * 2,
+        [SMEM] + [VMEM] * 3,
+        [pltpu.VMEM((Q, 3 * Q), BF), square],
+        64 * flops,
+        table, h_rows, x_correction, h_halo,
+    )
     xa_copy, x_corner = call(spread_kernel, [CORNER, SQUARE], [VMEM] * 2, [VMEM] * 2, [], 0, xa_halo, part)
     xa_twin = swap(xa_copy)
     half = call(half_kernel, BANDED, VMEM, [VMEM] + [VMEM] * 3, [square], 16 * flops, marks, xo, h_twin, part)

time: 89.7 us -> 88.3 us (0.984)
  starting transfers between devices: 48.9 us -> 50.6 us
  waiting for transfers between devices: 24.1 us -> 22.4 us
    ppermute x5, starting transfers between devices: 38.8 us -> 40.5 us  [link(): return lax.ppermute(x, ('rows', 'rep'), outward)]
    ppermute x5, waiting for transfers between devices: 20.1 us -> 18.5 us  [link(): return lax.ppermute(x, ('rows', 'rep'), outward)]
    pallas_call x14 -> x13, Pallas kernels: 15.4 us -> 14.6 us  [call(): pl.pallas_call(kernel, out_shape=outs, in_specs=in_specs, out_specs=out_s...]
where the time goes in v4:
time: 88.3 us; the launch traced here: 87.8 us
  starting transfers between devices  50.6 us (57%)
  waiting for transfers between devices  22.4 us (25%)
  Pallas kernels  14.6 us (17%)
    ppermute x5, starting transfers between devices, link(): return lax.ppermute(x, ('rows', 'rep'), outward)  40.5 us
    ppermute x5, waiting for transfers between devices, link(): return lax.ppermute(x, ('rows', 'rep'), outward)  18.5 us
    pallas_call x13, Pallas kernels, call(): pl.pallas_call(kernel, out_shape=outs, in_specs=in_specs, out_specs=out_s...  14.6 us
    ppermute x5, starting transfers between devices, swap(): return lax.ppermute(x, 'rep', [(0, 1), (1, 0)])  10.1 us
    ppermute x5, waiting for transfers between devices, swap(): return lax.ppermute(x, 'rep', [(0, 1), (1, 0)])  3.99 us
  transfers between devices with their start and end apart: 10, of which 6 were waited for; matrix products, arithmetic and copies ran while one was open for 0% of the time, Pallas kernels for 9%

profile of v4, /device:TPU:33, one launch (start us, length us, event | category | flops | bytes accessed | tf_op | source)
XLA Modules:
  0.0 87.8 jit_solution(9490814086009542741)
XLA Ops:
  0.0 0.0 copy-start
  0.0 1.9 %shard_map.46 = (bf16[832,512]{1,0:T(8,128)(2,1)S(1)}, s32[49]{0:T(128)S(1)}, bf16[4,8,128,128]{3,2,1,0:T(8,128)(2,1)S(1)}) custom-call(s32[4,8]{1,0:T(4,128)} %cols_hbm.3, s32[4,8]{1,0:T(4,128)} %mask_hbm.3, bf16[4,8,128,128]{3,2,1,0:T(8,128)(2,1)} %h_hbm.1), custom_call_target="tpu_custom_call" | custom-call | flops 536870912 | bytes 4194304 | tf_op jit(solution)/shard_map/pallas_call | solution.py:31
  1.9 13.3 %collective-permute-start = (bf16[832,512]{1,0:T(8,128)(2,1)S(1)}, bf16[832,512]{1,0:T(8,128)(2,1)S(1)}, u32[]{:S(2)}, u32[]{:S(2)}) collective-permute-start(bf16[832,512]{1,0:T(8,128)(2,1)S(1)} %get-tuple-element.34), channel_id=1, source_target_pairs={{0,3},{2,5},{4,7},{6,9},{8,11},{10,13},{12,15},{14,17},{16,19},{18... | collective-permute-start | bytes 2555912 | tf_op jit(solution)/shard_map/ppermute | solution.py:416
  15.2 0.0 copy-done
  15.3 0.8 shard_map.47
  16.1 1.9 %collective-permute-start.3 = (bf16[10,128,128]{2,1,0:T(8,128)(2,1)S(1)}, bf16[10,128,128]{2,1,0:T(8,128)(2,1)S(1)}, u32[]{:S(2)}, u32[]{:S(2)}) collective-permute-start(bf16[10,128,128]{2,1,0:T(8,128)(2,1)S(1)} %get-tuple-element.38), channel_id=1, source_target_pairs={{0,3},{2,5},{4,7},{6,9},{8,11},{10,13},{12,15},{14,17},{16,19},{18... | collective-permute-start | bytes 983048 | tf_op jit(solution)/shard_map/ppermute | solution.py:416
  18.0 9.1 %collective-permute-start.2 = (bf16[512,512]{1,0:T(8,128)(2,1)S(1)}, bf16[512,512]{1,0:T(8,128)(2,1)S(1)}, u32[]{:S(2)}, u32[]{:S(2)}) collective-permute-start(bf16[512,512]{1,0:T(8,128)(2,1)S(1)} %get-tuple-element.37), channel_id=1, source_target_pairs={{0,3},{2,5},{4,7},{6,9},{8,11},{10,13},{12,15},{14,17},{16,19},{18... | collective-permute-start | bytes 1572872 | tf_op jit(solution)/shard_map/ppermute | solution.py:416
  27.1 0.0 collective-permute-done.joint
  27.1 1.9 %collective-permute-start.1 = (bf16[832,512]{1,0:T(8,128)(2,1)S(1)}, bf16[832,512]{1,0:T(8,128)(2,1)S(1)}, u32[]{:S(2)}, u32[]{:S(2)}) collective-permute-start(bf16[832,512]{1,0:T(8,128)(2,1)S(1)} %collective-permute-done.joint), channel_id=1, source_target_pairs={{0,1},{1,0},{2,3},{3,2},{4,5},{5,4},{6,7},{7,6},{8,9},{9,8},{10,11... | collective-permute-start | bytes 2555912 | tf_op jit(solution)/shard_map/ppermute | solution.py:419
  29.0 2.0 %shard_map.48 = (bf16[512,1536]{1,0:T(8,128)(2,1)S(1)}, f32[512,1536]{1,0:T(8,128)S(1)}) custom-call(s32[49]{0:T(128)S(1)} %get-tuple-element.31.table, bf16[4,8,128,128]{3,2,1,0:T(8,128)(2,1)S(1)} %get-tuple-element.33.h_ref, bf16[4,8,128,128]{3,2,1,0:T(8,128)(2,1)S(1)} %copy-done, bf16[832,512]{1,0:T(8,128)(2,1)S(1)} %collective-permute-done.joint), custom_call_target="tpu_custom_call" | custom-call | flops 34359738368 | bytes 4194304 | tf_op jit(solution)/shard_map/pallas_call | solution.py:31
  31.1 0.0 collective-permute-done.3.xa
  31.1 0.1 shard_map.50
  31.2 2.4 %collective-permute-start.4 = (bf16[10,128,128]{2,1,0:T(8,128)(2,1)S(1)}, bf16[10,128,128]{2,1,0:T(8,128)(2,1)S(1)}, u32[]{:S(2)}, u32[]{:S(2)}) collective-permute-start(bf16[10,128,128]{2,1,0:T(8,128)(2,1)S(1)} %get-tuple-element.40), channel_id=1, source_target_pairs={{0,1},{1,0},{2,3},{3,2},{4,5},{5,4},{6,7},{7,6},{8,9},{9,8},{10,11... | collective-permute-start | bytes 983048 | tf_op jit(solution)/shard_map/ppermute | solution.py:419
  33.6 0.0 collective-permute-done.1.twin
  33.6 0.6 shard_map.49.refs_1_
  34.2 0.6 collective-permute-done.4.refs_4_
  34.8 0.8 shard_map.51
  35.7 0.0 collective-permute-done.2.refs_3_
  35.7 0.5 shard_map.52
  36.3 8.1 %collective-permute-start.6 = (bf16[832,512]{1,0:T(8,128)(2,1)S(1)}, bf16[832,512]{1,0:T(8,128)(2,1)S(1)}, u32[]{:S(2)}, u32[]{:S(2)}) collective-permute-start(bf16[832,512]{1,0:T(8,128)(2,1)S(1)} %get-tuple-element.45), channel_id=1, source_target_pairs={{0,3},{2,5},{4,7},{6,9},{8,11},{10,13},{12,15},{14,17},{16,19},{18... | collective-permute-start | bytes 2555912 | tf_op jit(solution)/shard_map/ppermute | solution.py:416
  44.4 1.9 %collective-permute-start.5 = (bf16[10,128,128]{2,1,0:T(8,128)(2,1)S(1)}, bf16[10,128,128]{2,1,0:T(8,128)(2,1)S(1)}, u32[]{:S(2)}, u32[]{:S(2)}) collective-permute-start(bf16[10,128,128]{2,1,0:T(8,128)(2,1)S(1)} %get-tuple-element.44), channel_id=1, source_target_pairs={{0,1},{1,0},{2,3},{3,2},{4,5},{5,4},{6,7},{7,6},{8,9},{9,8},{10,11... | collective-permute-start | bytes 983048 | tf_op jit(solution)/shard_map/ppermute | solution.py:419
  46.3 1.6 %collective-permute-done.5.side = bf16[10,128,128]{2,1,0:T(8,128)(2,1)S(1)} collective-permute-done((bf16[10,128,128]{2,1,0:T(8,128)(2,1)S(1)}, bf16[10,128,128]{2,1,0:T(8,128)(2,1)S(1)}, u32[]{:S(2)}, u32[]{:S(2)}) %collective-permute-start.5) | collective-permute-done | bytes 327712 | tf_op jit(solution)/shard_map/ppermute | solution.py:419
  47.9 0.1 shard_map.53.band
  48.0 7.7 %collective-permute-done.6.joint = bf16[832,512]{1,0:T(8,128)(2,1)S(1)} collective-permute-done((bf16[832,512]{1,0:T(8,128)(2,1)S(1)}, bf16[832,512]{1,0:T(8,128)(2,1)S(1)}, u32[]{:S(2)}, u32[]{:S(2)}) %collective-permute-start.6) | collective-permute-done | bytes 852000 | tf_op jit(solution)/shard_map/ppermute | solution.py:416
  55.7 1.9 %collective-permute-start.7 = (bf16[832,512]{1,0:T(8,128)(2,1)S(1)}, bf16[832,512]{1,0:T(8,128)(2,1)S(1)}, u32[]{:S(2)}, u32[]{:S(2)}) collective-permute-start(bf16[832,512]{1,0:T(8,128)(2,1)S(1)} %collective-permute-done.6.joint), channel_id=1, source_target_pairs={{0,1},{1,0},{2,3},{3,2},{4,5},{5,4},{6,7},{7,6},{8,9},{9,8},{10,11... | collective-permute-start | bytes 2555912 | tf_op jit(solution)/shard_map/ppermute | solution.py:419
  57.6 1.5 %shard_map.54 = (bf16[512,512]{1,0:T(8,128)(2,1)S(1)}, f32[512,512]{1,0:T(8,128)S(1)}, f32[512,512]{1,0:T(8,128)S(1)}, f32[512,1024]{1,0:T(8,128)S(1)}) custom-call(f32[48,128]{1,0:T(8,128)S(1)} %get-tuple-element.32.table.refs_0_, bf16[512,1536]{1,0:T(8,128)(2,1)S(1)} %shard_map.53.band, bf16[832,512]{1,0:T(8,128)(2,1)S(1)} %collective-permute-done.6.joint), custom_call_target="tpu_custom_call" | custom-call | flops 34359738368 | bytes 4194304 | tf_op jit(solution)/shard_map/pallas_call | solution.py:31
  59.1 0.9 %collective-permute-done.7.twin = bf16[832,512]{1,0:T(8,128)(2,1)S(1)} collective-permute-done((bf16[832,512]{1,0:T(8,128)(2,1)S(1)}, bf16[832,512]{1,0:T(8,128)(2,1)S(1)}, u32[]{:S(2)}, u32[]{:S(2)}) %collective-permute-start.7) | collective-permute-done | bytes 852000 | tf_op jit(solution)/shard_map/ppermute | solution.py:419
  60.0 1.3 %shard_map.55 = (bf16[512,1536]{1,0:T(8,128)(2,1)S(1)}, bf16[832,512]{1,0:T(8,128)(2,1)S(1)}, bf16[512,1024]{1,0:T(8,128)(2,1)S(1)}) custom-call(f32[48,128]{1,0:T(8,128)S(1)} %get-tuple-element.32.table.refs_0_, bf16[512,1536]{1,0:T(8,128)(2,1)S(1)} %shard_map.53.band, bf16[512,512]{1,0:T(8,128)(2,1)S(1)} %get-tuple-element.46.sq_r, ...), custom_call_target="tpu_custom_call" | custom-call | flops 536870912 | bytes 4194304 | tf_op jit(solution)/shard_map/pallas_call | solution.py:31
  61.3 8.1 %collective-permute-start.8 = (bf16[832,512]{1,0:T(8,128)(2,1)S(1)}, bf16[832,512]{1,0:T(8,128)(2,1)S(1)}, u32[]{:S(2)}, u32[]{:S(2)}) collective-permute-start(bf16[832,512]{1,0:T(8,128)(2,1)S(1)} %get-tuple-element.52), channel_id=1, source_target_pairs={{0,3},{2,5},{4,7},{6,9},{8,11},{10,13},{12,15},{14,17},{16,19},{18... | collective-permute-start | bytes 2555912 | tf_op jit(solution)/shard_map/ppermute | solution.py:416
  69.4 0.5 shard_map.56.band
  70.0 0.0 copy-start.1
  70.0 0.0 copy-start.2
  70.0 10.8 %collective-permute-done.8.joint = bf16[832,512]{1,0:T(8,128)(2,1)S(1)} collective-permute-done((bf16[832,512]{1,0:T(8,128)(2,1)S(1)}, bf16[832,512]{1,0:T(8,128)(2,1)S(1)}, u32[]{:S(2)}, u32[]{:S(2)}) %collective-permute-start.8) | collective-permute-done | bytes 852000 | tf_op jit(solution)/shard_map/ppermute | solution.py:416
  80.7 1.9 %collective-permute-start.9 = (bf16[832,512]{1,0:T(8,128)(2,1)S(1)}, bf16[832,512]{1,0:T(8,128)(2,1)S(1)}, u32[]{:S(2)}, u32[]{:S(2)}) collective-permute-start(bf16[832,512]{1,0:T(8,128)(2,1)S(1)} %collective-permute-done.8.joint), channel_id=1, source_target_pairs={{0,1},{1,0},{2,3},{3,2},{4,5},{5,4},{6,7},{7,6},{8,9},{9,8},{10,11... | collective-permute-start | bytes 2555912 | tf_op jit(solution)/shard_map/ppermute | solution.py:419
  82.7 1.5 %shard_map.57 = (bf16[512,512]{1,0:T(8,128)(2,1)S(1)}, f32[512,512]{1,0:T(8,128)S(1)}, f32[512,512]{1,0:T(8,128)S(1)}, f32[512,1024]{1,0:T(8,128)S(1)}) custom-call(f32[48,128]{1,0:T(8,128)S(1)} %get-tuple-element.32.table.refs_0_, bf16[512,1536]{1,0:T(8,128)(2,1)S(1)} %shard_map.56.band, bf16[832,512]{1,0:T(8,128)(2,1)S(1)} %collective-permute-done.8.joint), custom_call_target="tpu_custom_call" | custom-call | flops 34359738368 | bytes 4194304 | tf_op jit(solution)/shard_map/pallas_call | solution.py:31
  84.1 0.9 %collective-permute-done.9.twin = bf16[832,512]{1,0:T(8,128)(2,1)S(1)} collective-permute-done((bf16[832,512]{1,0:T(8,128)(2,1)S(1)}, bf16[832,512]{1,0:T(8,128)(2,1)S(1)}, u32[]{:S(2)}, u32[]{:S(2)}) %collective-permute-start.9) | collective-permute-done | bytes 852000 | tf_op jit(solution)/shard_map/ppermute | solution.py:419
  85.0 0.0 copy-done.1
  85.0 0.0 copy-done.2
  85.0 2.8 %shard_map.58 = bf16[4,4,128,128]{3,2,1,0:T(8,128)(2,1)} custom-call(s32[4,8]{1,0:T(4,128)S(1)} %copy-done.1, s32[4,8]{1,0:T(4,128)S(1)} %copy-done.2, f32[48,128]{1,0:T(8,128)S(1)} %get-tuple-element.32.table.refs_0_, bf16[512,1536]{1,0:T(8,128)(2,1)S(1)} %shard_map.56.band, bf16[512,512]{1,0:T(8,128)(2,1)S(1)} %get-tuple-element.53.sq_r, ...), custom_call_target="tpu_custom_call" | custom-call | flops 536870912 | bytes 4194304 | tf_op jit(solution)/shard_map/pallas_call | solution.py:31
Async XLA Ops:
  0.0 15.2 %copy-start = (bf16[4,8,128,128]{3,2,1,0:T(8,128)(2,1)S(1)}, bf16[4,8,128,128]{3,2,1,0:T(8,128)(2,1)}, u32[]{:S(2)}) copy-start(bf16[4,8,128,128]{3,2,1,0:T(8,128)(2,1)} %x_ref.3) | copy-start | bytes 3145732
  1.9 25.2 %collective-permute-start = (bf16[832,512]{1,0:T(8,128)(2,1)S(1)}, bf16[832,512]{1,0:T(8,128)(2,1)S(1)}, u32[]{:S(2)}, u32[]{:S(2)}) collective-permute-start(bf16[832,512]{1,0:T(8,128)(2,1)S(1)} %get-tuple-element.34), channel_id=1, source_target_pairs={{0,3},{2,5},{4,7},{6,9},{8,11},{10,13},{12,15},{14,17},{16,19},{18... | collective-permute-start | bytes 2555912 | tf_op jit(solution)/shard_map/ppermute | solution.py:416
  16.1 15.0 %collective-permute-start.3 = (bf16[10,128,128]{2,1,0:T(8,128)(2,1)S(1)}, bf16[10,128,128]{2,1,0:T(8,128)(2,1)S(1)}, u32[]{:S(2)}, u32[]{:S(2)}) collective-permute-start(bf16[10,128,128]{2,1,0:T(8,128)(2,1)S(1)} %get-tuple-element.38), channel_id=1, source_target_pairs={{0,3},{2,5},{4,7},{6,9},{8,11},{10,13},{12,15},{14,17},{16,19},{18... | collective-permute-start | bytes 983048 | tf_op jit(solution)/shard_map/ppermute | solution.py:416
  18.0 17.7 %collective-permute-start.2 = (bf16[512,512]{1,0:T(8,128)(2,1)S(1)}, bf16[512,512]{1,0:T(8,128)(2,1)S(1)}, u32[]{:S(2)}, u32[]{:S(2)}) collective-permute-start(bf16[512,512]{1,0:T(8,128)(2,1)S(1)} %get-tuple-element.37), channel_id=1, source_target_pairs={{0,3},{2,5},{4,7},{6,9},{8,11},{10,13},{12,15},{14,17},{16,19},{18... | collective-permute-start | bytes 1572872 | tf_op jit(solution)/shard_map/ppermute | solution.py:416
  27.1 6.5 %collective-permute-start.1 = (bf16[832,512]{1,0:T(8,128)(2,1)S(1)}, bf16[832,512]{1,0:T(8,128)(2,1)S(1)}, u32[]{:S(2)}, u32[]{:S(2)}) collective-permute-start(bf16[832,512]{1,0:T(8,128)(2,1)S(1)} %collective-permute-done.joint), channel_id=1, source_target_pairs={{0,1},{1,0},{2,3},{3,2},{4,5},{5,4},{6,7},{7,6},{8,9},{9,8},{10,11... | collective-permute-start | bytes 2555912 | tf_op jit(solution)/shard_map/ppermute | solution.py:419
  31.2 3.6 %collective-permute-start.4 = (bf16[10,128,128]{2,1,0:T(8,128)(2,1)S(1)}, bf16[10,128,128]{2,1,0:T(8,128)(2,1)S(1)}, u32[]{:S(2)}, u32[]{:S(2)}) collective-permute-start(bf16[10,128,128]{2,1,0:T(8,128)(2,1)S(1)} %get-tuple-element.40), channel_id=1, source_target_pairs={{0,1},{1,0},{2,3},{3,2},{4,5},{5,4},{6,7},{7,6},{8,9},{9,8},{10,11... | collective-permute-start | bytes 983048 | tf_op jit(solution)/shard_map/ppermute | solution.py:419
  36.3 19.4 %collective-permute-start.6 = (bf16[832,512]{1,0:T(8,128)(2,1)S(1)}, bf16[832,512]{1,0:T(8,128)(2,1)S(1)}, u32[]{:S(2)}, u32[]{:S(2)}) collective-permute-start(bf16[832,512]{1,0:T(8,128)(2,1)S(1)} %get-tuple-element.45), channel_id=1, source_target_pairs={{0,3},{2,5},{4,7},{6,9},{8,11},{10,13},{12,15},{14,17},{16,19},{18... | collective-permute-start | bytes 2555912 | tf_op jit(solution)/shard_map/ppermute | solution.py:416
  44.4 3.5 %collective-permute-start.5 = (bf16[10,128,128]{2,1,0:T(8,128)(2,1)S(1)}, bf16[10,128,128]{2,1,0:T(8,128)(2,1)S(1)}, u32[]{:S(2)}, u32[]{:S(2)}) collective-permute-start(bf16[10,128,128]{2,1,0:T(8,128)(2,1)S(1)} %get-tuple-element.44), channel_id=1, source_target_pairs={{0,1},{1,0},{2,3},{3,2},{4,5},{5,4},{6,7},{7,6},{8,9},{9,8},{10,11... | collective-permute-start | bytes 983048 | tf_op jit(solution)/shard_map/ppermute | solution.py:419
  55.7 4.3 %collective-permute-start.7 = (bf16[832,512]{1,0:T(8,128)(2,1)S(1)}, bf16[832,512]{1,0:T(8,128)(2,1)S(1)}, u32[]{:S(2)}, u32[]{:S(2)}) collective-permute-start(bf16[832,512]{1,0:T(8,128)(2,1)S(1)} %collective-permute-done.6.joint), channel_id=1, source_target_pairs={{0,1},{1,0},{2,3},{3,2},{4,5},{5,4},{6,7},{7,6},{8,9},{9,8},{10,11... | collective-permute-start | bytes 2555912 | tf_op jit(solution)/shard_map/ppermute | solution.py:419
  61.3 19.4 %collective-permute-start.8 = (bf16[832,512]{1,0:T(8,128)(2,1)S(1)}, bf16[832,512]{1,0:T(8,128)(2,1)S(1)}, u32[]{:S(2)}, u32[]{:S(2)}) collective-permute-start(bf16[832,512]{1,0:T(8,128)(2,1)S(1)} %get-tuple-element.52), channel_id=1, source_target_pairs={{0,3},{2,5},{4,7},{6,9},{8,11},{10,13},{12,15},{14,17},{16,19},{18... | collective-permute-start | bytes 2555912 | tf_op jit(solution)/shard_map/ppermute | solution.py:416
  70.0 15.1 %copy-start.1 = (s32[4,8]{1,0:T(4,128)S(1)}, s32[4,8]{1,0:T(4,128)}, u32[]{:S(2)}) copy-start(s32[4,8]{1,0:T(4,128)} %cols_hbm.3) | copy-start | bytes 388
  70.0 15.0 %copy-start.2 = (s32[4,8]{1,0:T(4,128)S(1)}, s32[4,8]{1,0:T(4,128)}, u32[]{:S(2)}) copy-start(s32[4,8]{1,0:T(4,128)} %mask_hbm.3) | copy-start | bytes 388
  80.7 4.3 %collective-permute-start.9 = (bf16[832,512]{1,0:T(8,128)(2,1)S(1)}, bf16[832,512]{1,0:T(8,128)(2,1)S(1)}, u32[]{:S(2)}, u32[]{:S(2)}) collective-permute-start(bf16[832,512]{1,0:T(8,128)(2,1)S(1)} %collective-permute-done.8.joint), channel_id=1, source_target_pairs={{0,1},{1,0},{2,3},{3,2},{4,5},{5,4},{6,7},{7,6},{8,9},{9,8},{10,11... | collective-permute-start | bytes 2555912 | tf_op jit(solution)/shard_map/ppermute | solution.py:419

commit v5 on v4

--- a/solution.py
+++ b/solution.py
@@ -422,7 +422,7 @@
     flops = 1 << 29
     hbm = pl.BlockSpec(memory_space=pltpu.HBM)
 
-    index_table = jax.ShapeDtypeStruct((49,), jnp.int32)
+    index_table = pltpu.SMEM((49,), jnp.int32)
     h_send, table, h_rows = call(
         pack_h_kernel,
         [SEND, index_table, jax.ShapeDtypeStruct(hamiltonian.shape, BF)],

time: 88.3 us -> 87 us (0.985)
  Pallas kernels: 14.6 us -> 13 us
  starting transfers between devices: 50.6 us -> 52 us
  waiting for transfers between devices: 22.4 us -> 21.4 us
    pallas_call x13, Pallas kernels: 14.6 us -> 13 us  [call(): pl.pallas_call(kernel, out_shape=outs, in_specs=in_specs, out_specs=out_s...]
    ppermute x5, starting transfers between devices: 40.5 us -> 41.9 us  [link(): return lax.ppermute(x, ('rows', 'rep'), outward)]
    ppermute x5, waiting for transfers between devices: 18.5 us -> 17.4 us  [link(): return lax.ppermute(x, ('rows', 'rep'), outward)]
  transfers between devices with their start and end apart: 10 -> 10, of which waited for: 6 -> 7; matrix products, arithmetic and copies ran while one was open for 0% -> 0% of each run, Pallas kernels for 9% -> 8%
where the time goes in v5:
time: 87 us; the launch traced here: 86.6 us
  starting transfers between devices  52 us (60%)
  waiting for transfers between devices  21.4 us (25%)
  Pallas kernels  13 us (15%)
    ppermute x5, starting transfers between devices, link(): return lax.ppermute(x, ('rows', 'rep'), outward)  41.9 us
    ppermute x5, waiting for transfers between devices, link(): return lax.ppermute(x, ('rows', 'rep'), outward)  17.4 us
    pallas_call x13, Pallas kernels, call(): pl.pallas_call(kernel, out_shape=outs, in_specs=in_specs, out_specs=out_s...  13 us
    ppermute x5, starting transfers between devices, swap(): return lax.ppermute(x, 'rep', [(0, 1), (1, 0)])  10.1 us
    ppermute x5, waiting for transfers between devices, swap(): return lax.ppermute(x, 'rep', [(0, 1), (1, 0)])  3.99 us
  transfers between devices with their start and end apart: 10, of which 7 were waited for; matrix products, arithmetic and copies ran while one was open for 0% of the time, Pallas kernels for 8%

profile of v5, /device:TPU:33, one launch (start us, length us, event | category | flops | bytes accessed | tf_op | source)
XLA Modules:
  0.0 86.6 jit_solution(13308431946935308632)
XLA Ops:
  0.0 0.0 copy-start
  0.0 1.4 %shard_map.46 = (bf16[832,512]{1,0:T(8,128)(2,1)S(1)}, s32[49]{0:T(128)S(4)}, bf16[4,8,128,128]{3,2,1,0:T(8,128)(2,1)S(1)}) custom-call(s32[4,8]{1,0:T(4,128)} %cols_hbm.3, s32[4,8]{1,0:T(4,128)} %mask_hbm.3, bf16[4,8,128,128]{3,2,1,0:T(8,128)(2,1)} %h_hbm.1), custom_call_target="tpu_custom_call" | custom-call | flops 536870912 | bytes 4194304 | tf_op jit(solution)/shard_map/pallas_call | solution.py:31
  1.4 13.3 %collective-permute-start = (bf16[832,512]{1,0:T(8,128)(2,1)S(1)}, bf16[832,512]{1,0:T(8,128)(2,1)S(1)}, u32[]{:S(2)}, u32[]{:S(2)}) collective-permute-start(bf16[832,512]{1,0:T(8,128)(2,1)S(1)} %get-tuple-element.34), channel_id=1, source_target_pairs={{0,3},{2,5},{4,7},{6,9},{8,11},{10,13},{12,15},{14,17},{16,19},{18... | collective-permute-start | bytes 2555912 | tf_op jit(solution)/shard_map/ppermute | solution.py:416
  14.7 0.0 copy-done
  14.7 0.3 shard_map.47
  15.0 1.9 %collective-permute-start.3 = (bf16[10,128,128]{2,1,0:T(8,128)(2,1)S(1)}, bf16[10,128,128]{2,1,0:T(8,128)(2,1)S(1)}, u32[]{:S(2)}, u32[]{:S(2)}) collective-permute-start(bf16[10,128,128]{2,1,0:T(8,128)(2,1)S(1)} %get-tuple-element.38), channel_id=1, source_target_pairs={{0,3},{2,5},{4,7},{6,9},{8,11},{10,13},{12,15},{14,17},{16,19},{18... | collective-permute-start | bytes 983048 | tf_op jit(solution)/shard_map/ppermute | solution.py:416
  16.9 9.1 %collective-permute-start.2 = (bf16[512,512]{1,0:T(8,128)(2,1)S(1)}, bf16[512,512]{1,0:T(8,128)(2,1)S(1)}, u32[]{:S(2)}, u32[]{:S(2)}) collective-permute-start(bf16[512,512]{1,0:T(8,128)(2,1)S(1)} %get-tuple-element.37), channel_id=1, source_target_pairs={{0,3},{2,5},{4,7},{6,9},{8,11},{10,13},{12,15},{14,17},{16,19},{18... | collective-permute-start | bytes 1572872 | tf_op jit(solution)/shard_map/ppermute | solution.py:416
  26.0 0.0 collective-permute-done.joint
  26.0 1.9 %collective-permute-start.1 = (bf16[832,512]{1,0:T(8,128)(2,1)S(1)}, bf16[832,512]{1,0:T(8,128)(2,1)S(1)}, u32[]{:S(2)}, u32[]{:S(2)}) collective-permute-start(bf16[832,512]{1,0:T(8,128)(2,1)S(1)} %collective-permute-done.joint), channel_id=1, source_target_pairs={{0,1},{1,0},{2,3},{3,2},{4,5},{5,4},{6,7},{7,6},{8,9},{9,8},{10,11... | collective-permute-start | bytes 2555912 | tf_op jit(solution)/shard_map/ppermute | solution.py:419
  28.0 1.5 %shard_map.48 = (bf16[512,1536]{1,0:T(8,128)(2,1)S(1)}, f32[512,1536]{1,0:T(8,128)S(1)}) custom-call(s32[49]{0:T(128)S(4)} %get-tuple-element.31.table, bf16[4,8,128,128]{3,2,1,0:T(8,128)(2,1)S(1)} %get-tuple-element.33.h_ref, bf16[4,8,128,128]{3,2,1,0:T(8,128)(2,1)S(1)} %copy-done, bf16[832,512]{1,0:T(8,128)(2,1)S(1)} %collective-permute-done.joint), custom_call_target="tpu_custom_call" | custom-call | flops 34359738368 | bytes 4194304 | tf_op jit(solution)/shard_map/pallas_call | solution.py:31
  29.5 0.0 collective-permute-done.3.xa
  29.5 0.1 shard_map.50
  29.6 2.4 %collective-permute-start.4 = (bf16[10,128,128]{2,1,0:T(8,128)(2,1)S(1)}, bf16[10,128,128]{2,1,0:T(8,128)(2,1)S(1)}, u32[]{:S(2)}, u32[]{:S(2)}) collective-permute-start(bf16[10,128,128]{2,1,0:T(8,128)(2,1)S(1)} %get-tuple-element.40), channel_id=1, source_target_pairs={{0,1},{1,0},{2,3},{3,2},{4,5},{5,4},{6,7},{7,6},{8,9},{9,8},{10,11... | collective-permute-start | bytes 983048 | tf_op jit(solution)/shard_map/ppermute | solution.py:419
  32.0 0.0 collective-permute-done.1.twin
  32.0 0.6 shard_map.49.refs_1_
  32.6 0.6 collective-permute-done.4.refs_4_
  33.2 0.8 shard_map.51
  34.1 0.4 collective-permute-done.2.refs_3_
  34.5 0.5 shard_map.52
  35.0 8.8 %collective-permute-start.6 = (bf16[832,512]{1,0:T(8,128)(2,1)S(1)}, bf16[832,512]{1,0:T(8,128)(2,1)S(1)}, u32[]{:S(2)}, u32[]{:S(2)}) collective-permute-start(bf16[832,512]{1,0:T(8,128)(2,1)S(1)} %get-tuple-element.45), channel_id=1, source_target_pairs={{0,3},{2,5},{4,7},{6,9},{8,11},{10,13},{12,15},{14,17},{16,19},{18... | collective-permute-start | bytes 2555912 | tf_op jit(solution)/shard_map/ppermute | solution.py:416
  43.8 1.9 %collective-permute-start.5 = (bf16[10,128,128]{2,1,0:T(8,128)(2,1)S(1)}, bf16[10,128,128]{2,1,0:T(8,128)(2,1)S(1)}, u32[]{:S(2)}, u32[]{:S(2)}) collective-permute-start(bf16[10,128,128]{2,1,0:T(8,128)(2,1)S(1)} %get-tuple-element.44), channel_id=1, source_target_pairs={{0,1},{1,0},{2,3},{3,2},{4,5},{5,4},{6,7},{7,6},{8,9},{9,8},{10,11... | collective-permute-start | bytes 983048 | tf_op jit(solution)/shard_map/ppermute | solution.py:419
  45.8 1.6 %collective-permute-done.5.side = bf16[10,128,128]{2,1,0:T(8,128)(2,1)S(1)} collective-permute-done((bf16[10,128,128]{2,1,0:T(8,128)(2,1)S(1)}, bf16[10,128,128]{2,1,0:T(8,128)(2,1)S(1)}, u32[]{:S(2)}, u32[]{:S(2)}) %collective-permute-start.5) | collective-permute-done | bytes 327712 | tf_op jit(solution)/shard_map/ppermute | solution.py:419
  47.4 0.1 shard_map.53.band
  47.5 7.0 %collective-permute-done.6.joint = bf16[832,512]{1,0:T(8,128)(2,1)S(1)} collective-permute-done((bf16[832,512]{1,0:T(8,128)(2,1)S(1)}, bf16[832,512]{1,0:T(8,128)(2,1)S(1)}, u32[]{:S(2)}, u32[]{:S(2)}) %collective-permute-start.6) | collective-permute-done | bytes 852000 | tf_op jit(solution)/shard_map/ppermute | solution.py:416
  54.4 1.9 %collective-permute-start.7 = (bf16[832,512]{1,0:T(8,128)(2,1)S(1)}, bf16[832,512]{1,0:T(8,128)(2,1)S(1)}, u32[]{:S(2)}, u32[]{:S(2)}) collective-permute-start(bf16[832,512]{1,0:T(8,128)(2,1)S(1)} %collective-permute-done.6.joint), channel_id=1, source_target_pairs={{0,1},{1,0},{2,3},{3,2},{4,5},{5,4},{6,7},{7,6},{8,9},{9,8},{10,11... | collective-permute-start | bytes 2555912 | tf_op jit(solution)/shard_map/ppermute | solution.py:419
  56.4 1.5 %shard_map.54 = (bf16[512,512]{1,0:T(8,128)(2,1)S(1)}, f32[512,512]{1,0:T(8,128)S(1)}, f32[512,512]{1,0:T(8,128)S(1)}, f32[512,1024]{1,0:T(8,128)S(1)}) custom-call(f32[48,128]{1,0:T(8,128)S(1)} %get-tuple-element.32.table.refs_0_, bf16[512,1536]{1,0:T(8,128)(2,1)S(1)} %shard_map.53.band, bf16[832,512]{1,0:T(8,128)(2,1)S(1)} %collective-permute-done.6.joint), custom_call_target="tpu_custom_call" | custom-call | flops 34359738368 | bytes 4194304 | tf_op jit(solution)/shard_map/pallas_call | solution.py:31
  57.8 0.9 %collective-permute-done.7.twin = bf16[832,512]{1,0:T(8,128)(2,1)S(1)} collective-permute-done((bf16[832,512]{1,0:T(8,128)(2,1)S(1)}, bf16[832,512]{1,0:T(8,128)(2,1)S(1)}, u32[]{:S(2)}, u32[]{:S(2)}) %collective-permute-start.7) | collective-permute-done | bytes 852000 | tf_op jit(solution)/shard_map/ppermute | solution.py:419
  58.7 1.3 %shard_map.55 = (bf16[512,1536]{1,0:T(8,128)(2,1)S(1)}, bf16[832,512]{1,0:T(8,128)(2,1)S(1)}, bf16[512,1024]{1,0:T(8,128)(2,1)S(1)}) custom-call(f32[48,128]{1,0:T(8,128)S(1)} %get-tuple-element.32.table.refs_0_, bf16[512,1536]{1,0:T(8,128)(2,1)S(1)} %shard_map.53.band, bf16[512,512]{1,0:T(8,128)(2,1)S(1)} %get-tuple-element.46.sq_r, ...), custom_call_target="tpu_custom_call" | custom-call | flops 536870912 | bytes 4194304 | tf_op jit(solution)/shard_map/pallas_call | solution.py:31
  60.1 8.8 %collective-permute-start.8 = (bf16[832,512]{1,0:T(8,128)(2,1)S(1)}, bf16[832,512]{1,0:T(8,128)(2,1)S(1)}, u32[]{:S(2)}, u32[]{:S(2)}) collective-permute-start(bf16[832,512]{1,0:T(8,128)(2,1)S(1)} %get-tuple-element.52), channel_id=1, source_target_pairs={{0,3},{2,5},{4,7},{6,9},{8,11},{10,13},{12,15},{14,17},{16,19},{18... | collective-permute-start | bytes 2555912 | tf_op jit(solution)/shard_map/ppermute | solution.py:416
  68.9 0.5 shard_map.56.band
  69.4 0.0 copy-start.1
  69.4 0.0 copy-start.2
  69.4 10.1 %collective-permute-done.8.joint = bf16[832,512]{1,0:T(8,128)(2,1)S(1)} collective-permute-done((bf16[832,512]{1,0:T(8,128)(2,1)S(1)}, bf16[832,512]{1,0:T(8,128)(2,1)S(1)}, u32[]{:S(2)}, u32[]{:S(2)}) %collective-permute-start.8) | collective-permute-done | bytes 852000 | tf_op jit(solution)/shard_map/ppermute | solution.py:416
  79.5 1.9 %collective-permute-start.9 = (bf16[832,512]{1,0:T(8,128)(2,1)S(1)}, bf16[832,512]{1,0:T(8,128)(2,1)S(1)}, u32[]{:S(2)}, u32[]{:S(2)}) collective-permute-start(bf16[832,512]{1,0:T(8,128)(2,1)S(1)} %collective-permute-done.8.joint), channel_id=1, source_target_pairs={{0,1},{1,0},{2,3},{3,2},{4,5},{5,4},{6,7},{7,6},{8,9},{9,8},{10,11... | collective-permute-start | bytes 2555912 | tf_op jit(solution)/shard_map/ppermute | solution.py:419
  81.4 1.5 %shard_map.57 = (bf16[512,512]{1,0:T(8,128)(2,1)S(1)}, f32[512,512]{1,0:T(8,128)S(1)}, f32[512,512]{1,0:T(8,128)S(1)}, f32[512,1024]{1,0:T(8,128)S(1)}) custom-call(f32[48,128]{1,0:T(8,128)S(1)} %get-tuple-element.32.table.refs_0_, bf16[512,1536]{1,0:T(8,128)(2,1)S(1)} %shard_map.56.band, bf16[832,512]{1,0:T(8,128)(2,1)S(1)} %collective-permute-done.8.joint), custom_call_target="tpu_custom_call" | custom-call | flops 34359738368 | bytes 4194304 | tf_op jit(solution)/shard_map/pallas_call | solution.py:31
  82.9 0.9 %collective-permute-done.9.twin = bf16[832,512]{1,0:T(8,128)(2,1)S(1)} collective-permute-done((bf16[832,512]{1,0:T(8,128)(2,1)S(1)}, bf16[832,512]{1,0:T(8,128)(2,1)S(1)}, u32[]{:S(2)}, u32[]{:S(2)}) %collective-permute-start.9) | collective-permute-done | bytes 852000 | tf_op jit(solution)/shard_map/ppermute | solution.py:419
  83.8 0.0 copy-done.1
  83.8 0.0 copy-done.2
  83.8 2.8 %shard_map.58 = bf16[4,4,128,128]{3,2,1,0:T(8,128)(2,1)} custom-call(s32[4,8]{1,0:T(4,128)S(1)} %copy-done.1, s32[4,8]{1,0:T(4,128)S(1)} %copy-done.2, f32[48,128]{1,0:T(8,128)S(1)} %get-tuple-element.32.table.refs_0_, bf16[512,1536]{1,0:T(8,128)(2,1)S(1)} %shard_map.56.band, bf16[512,512]{1,0:T(8,128)(2,1)S(1)} %get-tuple-element.53.sq_r, ...), custom_call_target="tpu_custom_call" | custom-call | flops 536870912 | bytes 4194304 | tf_op jit(solution)/shard_map/pallas_call | solution.py:31
Async XLA Ops:
  0.0 14.7 %copy-start = (bf16[4,8,128,128]{3,2,1,0:T(8,128)(2,1)S(1)}, bf16[4,8,128,128]{3,2,1,0:T(8,128)(2,1)}, u32[]{:S(2)}) copy-start(bf16[4,8,128,128]{3,2,1,0:T(8,128)(2,1)} %x_ref.3) | copy-start | bytes 3145732
  1.4 24.6 %collective-permute-start = (bf16[832,512]{1,0:T(8,128)(2,1)S(1)}, bf16[832,512]{1,0:T(8,128)(2,1)S(1)}, u32[]{:S(2)}, u32[]{:S(2)}) collective-permute-start(bf16[832,512]{1,0:T(8,128)(2,1)S(1)} %get-tuple-element.34), channel_id=1, source_target_pairs={{0,3},{2,5},{4,7},{6,9},{8,11},{10,13},{12,15},{14,17},{16,19},{18... | collective-permute-start | bytes 2555912 | tf_op jit(solution)/shard_map/ppermute | solution.py:416
  15.0 14.5 %collective-permute-start.3 = (bf16[10,128,128]{2,1,0:T(8,128)(2,1)S(1)}, bf16[10,128,128]{2,1,0:T(8,128)(2,1)S(1)}, u32[]{:S(2)}, u32[]{:S(2)}) collective-permute-start(bf16[10,128,128]{2,1,0:T(8,128)(2,1)S(1)} %get-tuple-element.38), channel_id=1, source_target_pairs={{0,3},{2,5},{4,7},{6,9},{8,11},{10,13},{12,15},{14,17},{16,19},{18... | collective-permute-start | bytes 983048 | tf_op jit(solution)/shard_map/ppermute | solution.py:416
  16.9 17.5 %collective-permute-start.2 = (bf16[512,512]{1,0:T(8,128)(2,1)S(1)}, bf16[512,512]{1,0:T(8,128)(2,1)S(1)}, u32[]{:S(2)}, u32[]{:S(2)}) collective-permute-start(bf16[512,512]{1,0:T(8,128)(2,1)S(1)} %get-tuple-element.37), channel_id=1, source_target_pairs={{0,3},{2,5},{4,7},{6,9},{8,11},{10,13},{12,15},{14,17},{16,19},{18... | collective-permute-start | bytes 1572872 | tf_op jit(solution)/shard_map/ppermute | solution.py:416
  26.0 6.0 %collective-permute-start.1 = (bf16[832,512]{1,0:T(8,128)(2,1)S(1)}, bf16[832,512]{1,0:T(8,128)(2,1)S(1)}, u32[]{:S(2)}, u32[]{:S(2)}) collective-permute-start(bf16[832,512]{1,0:T(8,128)(2,1)S(1)} %collective-permute-done.joint), channel_id=1, source_target_pairs={{0,1},{1,0},{2,3},{3,2},{4,5},{5,4},{6,7},{7,6},{8,9},{9,8},{10,11... | collective-permute-start | bytes 2555912 | tf_op jit(solution)/shard_map/ppermute | solution.py:419
  29.6 3.6 %collective-permute-start.4 = (bf16[10,128,128]{2,1,0:T(8,128)(2,1)S(1)}, bf16[10,128,128]{2,1,0:T(8,128)(2,1)S(1)}, u32[]{:S(2)}, u32[]{:S(2)}) collective-permute-start(bf16[10,128,128]{2,1,0:T(8,128)(2,1)S(1)} %get-tuple-element.40), channel_id=1, source_target_pairs={{0,1},{1,0},{2,3},{3,2},{4,5},{5,4},{6,7},{7,6},{8,9},{9,8},{10,11... | collective-permute-start | bytes 983048 | tf_op jit(solution)/shard_map/ppermute | solution.py:419
  35.0 19.4 %collective-permute-start.6 = (bf16[832,512]{1,0:T(8,128)(2,1)S(1)}, bf16[832,512]{1,0:T(8,128)(2,1)S(1)}, u32[]{:S(2)}, u32[]{:S(2)}) collective-permute-start(bf16[832,512]{1,0:T(8,128)(2,1)S(1)} %get-tuple-element.45), channel_id=1, source_target_pairs={{0,3},{2,5},{4,7},{6,9},{8,11},{10,13},{12,15},{14,17},{16,19},{18... | collective-permute-start | bytes 2555912 | tf_op jit(solution)/shard_map/ppermute | solution.py:416
  43.8 3.5 %collective-permute-start.5 = (bf16[10,128,128]{2,1,0:T(8,128)(2,1)S(1)}, bf16[10,128,128]{2,1,0:T(8,128)(2,1)S(1)}, u32[]{:S(2)}, u32[]{:S(2)}) collective-permute-start(bf16[10,128,128]{2,1,0:T(8,128)(2,1)S(1)} %get-tuple-element.44), channel_id=1, source_target_pairs={{0,1},{1,0},{2,3},{3,2},{4,5},{5,4},{6,7},{7,6},{8,9},{9,8},{10,11... | collective-permute-start | bytes 983048 | tf_op jit(solution)/shard_map/ppermute | solution.py:419
  54.4 4.3 %collective-permute-start.7 = (bf16[832,512]{1,0:T(8,128)(2,1)S(1)}, bf16[832,512]{1,0:T(8,128)(2,1)S(1)}, u32[]{:S(2)}, u32[]{:S(2)}) collective-permute-start(bf16[832,512]{1,0:T(8,128)(2,1)S(1)} %collective-permute-done.6.joint), channel_id=1, source_target_pairs={{0,1},{1,0},{2,3},{3,2},{4,5},{5,4},{6,7},{7,6},{8,9},{9,8},{10,11... | collective-permute-start | bytes 2555912 | tf_op jit(solution)/shard_map/ppermute | solution.py:419
  60.1 19.4 %collective-permute-start.8 = (bf16[832,512]{1,0:T(8,128)(2,1)S(1)}, bf16[832,512]{1,0:T(8,128)(2,1)S(1)}, u32[]{:S(2)}, u32[]{:S(2)}) collective-permute-start(bf16[832,512]{1,0:T(8,128)(2,1)S(1)} %get-tuple-element.52), channel_id=1, source_target_pairs={{0,3},{2,5},{4,7},{6,9},{8,11},{10,13},{12,15},{14,17},{16,19},{18... | collective-permute-start | bytes 2555912 | tf_op jit(solution)/shard_map/ppermute | solution.py:416
  69.4 14.3 %copy-start.1 = (s32[4,8]{1,0:T(4,128)S(1)}, s32[4,8]{1,0:T(4,128)}, u32[]{:S(2)}) copy-start(s32[4,8]{1,0:T(4,128)} %cols_hbm.3) | copy-start | bytes 388
  69.4 14.3 %copy-start.2 = (s32[4,8]{1,0:T(4,128)S(1)}, s32[4,8]{1,0:T(4,128)}, u32[]{:S(2)}) copy-start(s32[4,8]{1,0:T(4,128)} %mask_hbm.3) | copy-start | bytes 388
  79.5 4.3 %collective-permute-start.9 = (bf16[832,512]{1,0:T(8,128)(2,1)S(1)}, bf16[832,512]{1,0:T(8,128)(2,1)S(1)}, u32[]{:S(2)}, u32[]{:S(2)}) collective-permute-start(bf16[832,512]{1,0:T(8,128)(2,1)S(1)} %collective-permute-done.8.joint), channel_id=1, source_target_pairs={{0,1},{1,0},{2,3},{3,2},{4,5},{5,4},{6,7},{7,6},{8,9},{9,8},{10,11... | collective-permute-start | bytes 2555912 | tf_op jit(solution)/shard_map/ppermute | solution.py:419

commit v6 on v5

--- a/solution.py
+++ b/solution.py
@@ -93,6 +93,7 @@
         for s in range(8):
             active, row, t = place(cols, mask, a, s)
             table[jnp.where(active, 12 * row + t, 48)] = s
+            table[49 + 8 * row + s] = jnp.where(active, t, -1)
 
 
 def source_row(row):
@@ -315,36 +316,28 @@
     spread_twin(lambda i: joint_block(twin, 16 + i), lc)
     right = right_operand(twin, lc, lambda r, u: tile(band, r, u), None, None)
 
-    for half in range(2):
-
-        def only(left, *places):
-            return lambda r, t: left(r, t) if r == half and t in places else None
-
-        def keep(r, u, total):
-            if r != half:
-                return
-            total = total + (tile(sums, r, u - 2) if u in OWN else tile(part_l, r, u))
-            each_block(table, r, u, total, lambda row, t, b: put(sq, row, t, b.astype(BF)))
-
-        def step(r, u, total):
-            if r != half:
-                return
-            if u not in LEFT:
-                total = total + tile(more, r, u - 2)
-
-            def store(row, t, block):
-                if u in RIGHT:
-                    now = sq_r[row * S : (row + 1) * S, (t - 8) * S : (t - 7) * S]
-                else:
-                    now = sq[row * S : (row + 1) * S, t * S : (t + 1) * S]
-                finish(row, t, (3.0 * now.astype(F32) - 2.0 * block).astype(BF))
-
-            each_block(table, r, u, total, store)
-
-        product(only(lambda r, t: left_tile(band, r, t), *LEFT), right, LEFT + OWN, keep)
-        product(only(lambda r, t: left_tile(sq, r, t), *LEFT, *OWN), right, columns, step)
-        if after:
-            after(half)
+    def keep(r, u, total):
+        total = total + (tile(sums, r, u - 2) if u in OWN else tile(part_l, r, u))
+        each_block(table, r, u, total, lambda row, t, b: put(sq, row, t, b.astype(BF)))
+
+    def step(r, u, total):
+        if u not in LEFT:
+            total = total + tile(more, r, u - 2)
+
+        def store(row, t, block):
+            if u in RIGHT:
+                now = sq_r[row * S : (row + 1) * S, (t - 8) * S : (t - 7) * S]
+            else:
+                now = sq[row * S : (row + 1) * S, t * S : (t + 1) * S]
+            finish(row, t, (3.0 * now.astype(F32) - 2.0 * block).astype(BF))
+
+        each_block(table, r, u, total, store)
+
+    product(lambda r, t: left_tile(band, r, t) if t in LEFT else None, right, LEFT + OWN, keep)
+    product(lambda r, t: None if t in RIGHT else left_tile(sq, r, t), right, columns, step)
+    if after:
+        after(0)
+        after(1)
 
 
 def step_kernel(table, band, sq_r, part_l, sums, more, twin, new, send, sq, lc):
@@ -370,32 +363,24 @@
     product(lambda r, t: None if t in RIGHT else left_tile(sq, r, t), right, LEFT, step)
 
 
-def last_kernel(cols_hbm, mask_hbm, table, band, sq_r, part_l, sums, more, twin, out_hbm, *scratch):
-    lc, sq, res, out, sems, cols, mask = scratch
+def last_kernel(index, table, band, sq_r, part_l, sums, more, twin, out_hbm, *scratch):
+    lc, sq, res, out, sems = scratch
     core = lax.axis_index("rep")
-    pattern = [
-        pltpu.make_async_copy(cols_hbm, cols, sems.at[4]),
-        pltpu.make_async_copy(mask_hbm, mask, sems.at[5]),
-    ]
-    for one in pattern:
-        one.start()
 
     def copy(row):
         return pltpu.make_async_copy(out.at[row], out_hbm.at[source_row(row)], sems.at[row])
 
     def after(half):
-        if half == 0:
-            for one in pattern:
-                one.wait()
         for row in (2 * half, 2 * half + 1):
             for s in range(4):
-                active, unused, t = place(cols, mask, source_row(row), core * 4 + s)
-                block = res[row * S : (row + 1) * S, at(t)]
-                out[row, s] = jnp.where(active, block, jnp.zeros_like(block))
+                t = index[49 + 8 * row + core * 4 + s]
+                block = res[row * S : (row + 1) * S, at(jnp.maximum(t, 0))]
+                out[row, s] = jnp.where(t >= 0, block, jnp.zeros_like(block))
             copy(row).start()
 
     late_kernel(
-        LEFT + OWN + RIGHT, table, band, sq_r, part_l, sums, more, twin, lc, sq, lambda row, t, value: put(res, row, t, value), after
+        LEFT + OWN + RIGHT, table, band, sq_r, part_l, sums, more, twin, lc, sq,
+        lambda row, t, value: put(res, row, t, value), after,
     )
     for row in range(4):
         copy(row).wait()
@@ -422,7 +407,7 @@
     flops = 1 << 29
     hbm = pl.BlockSpec(memory_space=pltpu.HBM)
 
-    index_table = pltpu.SMEM((49,), jnp.int32)
+    index_table = pltpu.SMEM((81,), jnp.int32)
     h_send, table, h_rows = call(
         pack_h_kernel,
         [SEND, index_table, jax.ShapeDtypeStruct(hamiltonian.shape, BF)],
@@ -501,12 +486,11 @@
                 last_kernel,
                 jax.ShapeDtypeStruct((4, 4, S, S), BF),
                 hbm,
-                [hbm] * 2 + [VMEM] * 7,
+                [SMEM] + [VMEM] * 7,
                 [square, pltpu.VMEM((Q, 2 * Q), BF)]
-                + [pltpu.VMEM((Q, 3 * Q), BF), pltpu.VMEM((4, 4, S, S), BF), pltpu.SemaphoreType.DMA((6,))]
-                + [pltpu.SMEM(cols.shape, jnp.int32), pltpu.SMEM(mask.shape, jnp.int32)],
+                + [pltpu.VMEM((Q, 3 * Q), BF), pltpu.VMEM((4, 4, S, S), BF), pltpu.SemaphoreType.DMA((4,))],
                 flops,
-                cols, mask, *operands,
+                table, *operands,
             )
         new, send, sq = call(
             step_kernel,

time: 87 us -> 86.5 us (level)
  no operation moved by 1% of the time
where the time goes in v6:
time: 86.5 us; the launch traced here: 86.2 us
  starting transfers between devices  52 us (60%)
  waiting for transfers between devices  21.4 us (25%)
  Pallas kernels  12.5 us (14%)
    ppermute x5, starting transfers between devices, link(): return lax.ppermute(x, ('rows', 'rep'), outward)  41.9 us
    ppermute x5, waiting for transfers between devices, link(): return lax.ppermute(x, ('rows', 'rep'), outward)  17.4 us
    pallas_call x13, Pallas kernels, call(): pl.pallas_call(kernel, out_shape=outs, in_specs=in_specs, out_specs=out_s...  12.5 us
    ppermute x5, starting transfers between devices, swap(): return lax.ppermute(x, 'rep', [(0, 1), (1, 0)])  10.1 us
    ppermute x5, waiting for transfers between devices, swap(): return lax.ppermute(x, 'rep', [(0, 1), (1, 0)])  3.99 us
  transfers between devices with their start and end apart: 10, of which 7 were waited for; matrix products, arithmetic and copies ran while one was open for 0% of the time, Pallas kernels for 8%

profile of v6, /device:TPU:33, one launch (start us, length us, event | category | flops | bytes accessed | tf_op | source)
XLA Modules:
  0.0 86.2 jit_solution(592993396070481960)
XLA Ops:
  0.0 0.0 copy-start
  0.0 1.4 %shard_map.46 = (bf16[832,512]{1,0:T(8,128)(2,1)S(1)}, s32[81]{0:T(128)S(4)}, bf16[4,8,128,128]{3,2,1,0:T(8,128)(2,1)S(1)}) custom-call(s32[4,8]{1,0:T(4,128)} %cols_hbm.1, s32[4,8]{1,0:T(4,128)} %mask_hbm.1, bf16[4,8,128,128]{3,2,1,0:T(8,128)(2,1)} %h_hbm.1), custom_call_target="tpu_custom_call" | custom-call | flops 536870912 | bytes 4194304 | tf_op jit(solution)/shard_map/pallas_call | solution.py:31
  1.4 13.3 %collective-permute-start = (bf16[832,512]{1,0:T(8,128)(2,1)S(1)}, bf16[832,512]{1,0:T(8,128)(2,1)S(1)}, u32[]{:S(2)}, u32[]{:S(2)}) collective-permute-start(bf16[832,512]{1,0:T(8,128)(2,1)S(1)} %get-tuple-element.34), channel_id=1, source_target_pairs={{0,3},{2,5},{4,7},{6,9},{8,11},{10,13},{12,15},{14,17},{16,19},{18... | collective-permute-start | bytes 2555912 | tf_op jit(solution)/shard_map/ppermute | solution.py:401
  14.7 0.0 copy-done
  14.7 0.3 shard_map.47
  15.0 1.9 %collective-permute-start.3 = (bf16[10,128,128]{2,1,0:T(8,128)(2,1)S(1)}, bf16[10,128,128]{2,1,0:T(8,128)(2,1)S(1)}, u32[]{:S(2)}, u32[]{:S(2)}) collective-permute-start(bf16[10,128,128]{2,1,0:T(8,128)(2,1)S(1)} %get-tuple-element.38), channel_id=1, source_target_pairs={{0,3},{2,5},{4,7},{6,9},{8,11},{10,13},{12,15},{14,17},{16,19},{18... | collective-permute-start | bytes 983048 | tf_op jit(solution)/shard_map/ppermute | solution.py:401
  16.9 9.1 %collective-permute-start.2 = (bf16[512,512]{1,0:T(8,128)(2,1)S(1)}, bf16[512,512]{1,0:T(8,128)(2,1)S(1)}, u32[]{:S(2)}, u32[]{:S(2)}) collective-permute-start(bf16[512,512]{1,0:T(8,128)(2,1)S(1)} %get-tuple-element.37), channel_id=1, source_target_pairs={{0,3},{2,5},{4,7},{6,9},{8,11},{10,13},{12,15},{14,17},{16,19},{18... | collective-permute-start | bytes 1572872 | tf_op jit(solution)/shard_map/ppermute | solution.py:401
  26.0 0.0 collective-permute-done.joint
  26.0 1.9 %collective-permute-start.1 = (bf16[832,512]{1,0:T(8,128)(2,1)S(1)}, bf16[832,512]{1,0:T(8,128)(2,1)S(1)}, u32[]{:S(2)}, u32[]{:S(2)}) collective-permute-start(bf16[832,512]{1,0:T(8,128)(2,1)S(1)} %collective-permute-done.joint), channel_id=1, source_target_pairs={{0,1},{1,0},{2,3},{3,2},{4,5},{5,4},{6,7},{7,6},{8,9},{9,8},{10,11... | collective-permute-start | bytes 2555912 | tf_op jit(solution)/shard_map/ppermute | solution.py:404
  28.0 1.5 %shard_map.48 = (bf16[512,1536]{1,0:T(8,128)(2,1)S(1)}, f32[512,1536]{1,0:T(8,128)S(1)}) custom-call(s32[81]{0:T(128)S(4)} %get-tuple-element.31.table.index, bf16[4,8,128,128]{3,2,1,0:T(8,128)(2,1)S(1)} %get-tuple-element.33.h_ref, bf16[4,8,128,128]{3,2,1,0:T(8,128)(2,1)S(1)} %copy-done, bf16[832,512]{1,0:T(8,128)(2,1)S(1)} %collective-permute-done.joint), custom_call_target="tpu_custom_call" | custom-call | flops 34359738368 | bytes 4194304 | tf_op jit(solution)/shard_map/pallas_call | solution.py:31
  29.5 0.0 collective-permute-done.3.xa
  29.5 0.1 shard_map.50
  29.6 2.4 %collective-permute-start.4 = (bf16[10,128,128]{2,1,0:T(8,128)(2,1)S(1)}, bf16[10,128,128]{2,1,0:T(8,128)(2,1)S(1)}, u32[]{:S(2)}, u32[]{:S(2)}) collective-permute-start(bf16[10,128,128]{2,1,0:T(8,128)(2,1)S(1)} %get-tuple-element.40), channel_id=1, source_target_pairs={{0,1},{1,0},{2,3},{3,2},{4,5},{5,4},{6,7},{7,6},{8,9},{9,8},{10,11... | collective-permute-start | bytes 983048 | tf_op jit(solution)/shard_map/ppermute | solution.py:404
  32.0 0.0 collective-permute-done.1.twin
  32.0 0.6 shard_map.49.refs_1_
  32.6 0.6 collective-permute-done.4.refs_4_
  33.2 0.8 shard_map.51
  34.1 0.4 collective-permute-done.2.refs_3_
  34.5 0.5 shard_map.52
  35.0 8.8 %collective-permute-start.6 = (bf16[832,512]{1,0:T(8,128)(2,1)S(1)}, bf16[832,512]{1,0:T(8,128)(2,1)S(1)}, u32[]{:S(2)}, u32[]{:S(2)}) collective-permute-start(bf16[832,512]{1,0:T(8,128)(2,1)S(1)} %get-tuple-element.45), channel_id=1, source_target_pairs={{0,3},{2,5},{4,7},{6,9},{8,11},{10,13},{12,15},{14,17},{16,19},{18... | collective-permute-start | bytes 2555912 | tf_op jit(solution)/shard_map/ppermute | solution.py:401
  43.8 1.9 %collective-permute-start.5 = (bf16[10,128,128]{2,1,0:T(8,128)(2,1)S(1)}, bf16[10,128,128]{2,1,0:T(8,128)(2,1)S(1)}, u32[]{:S(2)}, u32[]{:S(2)}) collective-permute-start(bf16[10,128,128]{2,1,0:T(8,128)(2,1)S(1)} %get-tuple-element.44), channel_id=1, source_target_pairs={{0,1},{1,0},{2,3},{3,2},{4,5},{5,4},{6,7},{7,6},{8,9},{9,8},{10,11... | collective-permute-start | bytes 983048 | tf_op jit(solution)/shard_map/ppermute | solution.py:404
  45.8 1.6 %collective-permute-done.5.side = bf16[10,128,128]{2,1,0:T(8,128)(2,1)S(1)} collective-permute-done((bf16[10,128,128]{2,1,0:T(8,128)(2,1)S(1)}, bf16[10,128,128]{2,1,0:T(8,128)(2,1)S(1)}, u32[]{:S(2)}, u32[]{:S(2)}) %collective-permute-start.5) | collective-permute-done | bytes 327712 | tf_op jit(solution)/shard_map/ppermute | solution.py:404
  47.4 0.1 shard_map.53.band
  47.5 7.0 %collective-permute-done.6.joint = bf16[832,512]{1,0:T(8,128)(2,1)S(1)} collective-permute-done((bf16[832,512]{1,0:T(8,128)(2,1)S(1)}, bf16[832,512]{1,0:T(8,128)(2,1)S(1)}, u32[]{:S(2)}, u32[]{:S(2)}) %collective-permute-start.6) | collective-permute-done | bytes 852000 | tf_op jit(solution)/shard_map/ppermute | solution.py:401
  54.4 1.9 %collective-permute-start.7 = (bf16[832,512]{1,0:T(8,128)(2,1)S(1)}, bf16[832,512]{1,0:T(8,128)(2,1)S(1)}, u32[]{:S(2)}, u32[]{:S(2)}) collective-permute-start(bf16[832,512]{1,0:T(8,128)(2,1)S(1)} %collective-permute-done.6.joint), channel_id=1, source_target_pairs={{0,1},{1,0},{2,3},{3,2},{4,5},{5,4},{6,7},{7,6},{8,9},{9,8},{10,11... | collective-permute-start | bytes 2555912 | tf_op jit(solution)/shard_map/ppermute | solution.py:404
  56.4 1.5 %shard_map.54 = (bf16[512,512]{1,0:T(8,128)(2,1)S(1)}, f32[512,512]{1,0:T(8,128)S(1)}, f32[512,512]{1,0:T(8,128)S(1)}, f32[512,1024]{1,0:T(8,128)S(1)}) custom-call(f32[48,128]{1,0:T(8,128)S(1)} %get-tuple-element.32.table.refs_0_, bf16[512,1536]{1,0:T(8,128)(2,1)S(1)} %shard_map.53.band, bf16[832,512]{1,0:T(8,128)(2,1)S(1)} %collective-permute-done.6.joint), custom_call_target="tpu_custom_call" | custom-call | flops 34359738368 | bytes 4194304 | tf_op jit(solution)/shard_map/pallas_call | solution.py:31
  57.8 0.9 %collective-permute-done.7.twin = bf16[832,512]{1,0:T(8,128)(2,1)S(1)} collective-permute-done((bf16[832,512]{1,0:T(8,128)(2,1)S(1)}, bf16[832,512]{1,0:T(8,128)(2,1)S(1)}, u32[]{:S(2)}, u32[]{:S(2)}) %collective-permute-start.7) | collective-permute-done | bytes 852000 | tf_op jit(solution)/shard_map/ppermute | solution.py:404
  58.7 1.3 %shard_map.55 = (bf16[512,1536]{1,0:T(8,128)(2,1)S(1)}, bf16[832,512]{1,0:T(8,128)(2,1)S(1)}, bf16[512,1024]{1,0:T(8,128)(2,1)S(1)}) custom-call(f32[48,128]{1,0:T(8,128)S(1)} %get-tuple-element.32.table.refs_0_, bf16[512,1536]{1,0:T(8,128)(2,1)S(1)} %shard_map.53.band, bf16[512,512]{1,0:T(8,128)(2,1)S(1)} %get-tuple-element.46.sq_r, ...), custom_call_target="tpu_custom_call" | custom-call | flops 536870912 | bytes 4194304 | tf_op jit(solution)/shard_map/pallas_call | solution.py:31
  60.0 8.8 %collective-permute-start.8 = (bf16[832,512]{1,0:T(8,128)(2,1)S(1)}, bf16[832,512]{1,0:T(8,128)(2,1)S(1)}, u32[]{:S(2)}, u32[]{:S(2)}) collective-permute-start(bf16[832,512]{1,0:T(8,128)(2,1)S(1)} %get-tuple-element.52), channel_id=1, source_target_pairs={{0,3},{2,5},{4,7},{6,9},{8,11},{10,13},{12,15},{14,17},{16,19},{18... | collective-permute-start | bytes 2555912 | tf_op jit(solution)/shard_map/ppermute | solution.py:401
  68.8 0.5 shard_map.56.band
  69.3 10.1 %collective-permute-done.8.joint = bf16[832,512]{1,0:T(8,128)(2,1)S(1)} collective-permute-done((bf16[832,512]{1,0:T(8,128)(2,1)S(1)}, bf16[832,512]{1,0:T(8,128)(2,1)S(1)}, u32[]{:S(2)}, u32[]{:S(2)}) %collective-permute-start.8) | collective-permute-done | bytes 852000 | tf_op jit(solution)/shard_map/ppermute | solution.py:401
  79.4 1.9 %collective-permute-start.9 = (bf16[832,512]{1,0:T(8,128)(2,1)S(1)}, bf16[832,512]{1,0:T(8,128)(2,1)S(1)}, u32[]{:S(2)}, u32[]{:S(2)}) collective-permute-start(bf16[832,512]{1,0:T(8,128)(2,1)S(1)} %collective-permute-done.8.joint), channel_id=1, source_target_pairs={{0,1},{1,0},{2,3},{3,2},{4,5},{5,4},{6,7},{7,6},{8,9},{9,8},{10,11... | collective-permute-start | bytes 2555912 | tf_op jit(solution)/shard_map/ppermute | solution.py:404
  81.3 1.5 %shard_map.57 = (bf16[512,512]{1,0:T(8,128)(2,1)S(1)}, f32[512,512]{1,0:T(8,128)S(1)}, f32[512,512]{1,0:T(8,128)S(1)}, f32[512,1024]{1,0:T(8,128)S(1)}) custom-call(f32[48,128]{1,0:T(8,128)S(1)} %get-tuple-element.32.table.refs_0_, bf16[512,1536]{1,0:T(8,128)(2,1)S(1)} %shard_map.56.band, bf16[832,512]{1,0:T(8,128)(2,1)S(1)} %collective-permute-done.8.joint), custom_call_target="tpu_custom_call" | custom-call | flops 34359738368 | bytes 4194304 | tf_op jit(solution)/shard_map/pallas_call | solution.py:31
  82.8 0.9 %collective-permute-done.9.twin = bf16[832,512]{1,0:T(8,128)(2,1)S(1)} collective-permute-done((bf16[832,512]{1,0:T(8,128)(2,1)S(1)}, bf16[832,512]{1,0:T(8,128)(2,1)S(1)}, u32[]{:S(2)}, u32[]{:S(2)}) %collective-permute-start.9) | collective-permute-done | bytes 852000 | tf_op jit(solution)/shard_map/ppermute | solution.py:404
  83.7 2.5 %shard_map.58 = bf16[4,4,128,128]{3,2,1,0:T(8,128)(2,1)} custom-call(s32[81]{0:T(128)S(4)} %get-tuple-element.31.table.index, f32[48,128]{1,0:T(8,128)S(1)} %get-tuple-element.32.table.refs_0_, bf16[512,1536]{1,0:T(8,128)(2,1)S(1)} %shard_map.56.band, bf16[512,512]{1,0:T(8,128)(2,1)S(1)} %get-tuple-element.53.sq_r, f32[512,512]{1,0:T(8,128)S(1)} %get-tuple-element.54.part_l, ...), custom_call_target="tpu_custom_call" | custom-call | flops 536870912 | bytes 4194304 | tf_op jit(solution)/shard_map/pallas_call | solution.py:31
Async XLA Ops:
  0.0 14.7 %copy-start = (bf16[4,8,128,128]{3,2,1,0:T(8,128)(2,1)S(1)}, bf16[4,8,128,128]{3,2,1,0:T(8,128)(2,1)}, u32[]{:S(2)}) copy-start(bf16[4,8,128,128]{3,2,1,0:T(8,128)(2,1)} %x_ref.3) | copy-start | bytes 3145732
  1.4 24.6 %collective-permute-start = (bf16[832,512]{1,0:T(8,128)(2,1)S(1)}, bf16[832,512]{1,0:T(8,128)(2,1)S(1)}, u32[]{:S(2)}, u32[]{:S(2)}) collective-permute-start(bf16[832,512]{1,0:T(8,128)(2,1)S(1)} %get-tuple-element.34), channel_id=1, source_target_pairs={{0,3},{2,5},{4,7},{6,9},{8,11},{10,13},{12,15},{14,17},{16,19},{18... | collective-permute-start | bytes 2555912 | tf_op jit(solution)/shard_map/ppermute | solution.py:401
  15.0 14.5 %collective-permute-start.3 = (bf16[10,128,128]{2,1,0:T(8,128)(2,1)S(1)}, bf16[10,128,128]{2,1,0:T(8,128)(2,1)S(1)}, u32[]{:S(2)}, u32[]{:S(2)}) collective-permute-start(bf16[10,128,128]{2,1,0:T(8,128)(2,1)S(1)} %get-tuple-element.38), channel_id=1, source_target_pairs={{0,3},{2,5},{4,7},{6,9},{8,11},{10,13},{12,15},{14,17},{16,19},{18... | collective-permute-start | bytes 983048 | tf_op jit(solution)/shard_map/ppermute | solution.py:401
  16.9 17.5 %collective-permute-start.2 = (bf16[512,512]{1,0:T(8,128)(2,1)S(1)}, bf16[512,512]{1,0:T(8,128)(2,1)S(1)}, u32[]{:S(2)}, u32[]{:S(2)}) collective-permute-start(bf16[512,512]{1,0:T(8,128)(2,1)S(1)} %get-tuple-element.37), channel_id=1, source_target_pairs={{0,3},{2,5},{4,7},{6,9},{8,11},{10,13},{12,15},{14,17},{16,19},{18... | collective-permute-start | bytes 1572872 | tf_op jit(solution)/shard_map/ppermute | solution.py:401
  26.0 6.0 %collective-permute-start.1 = (bf16[832,512]{1,0:T(8,128)(2,1)S(1)}, bf16[832,512]{1,0:T(8,128)(2,1)S(1)}, u32[]{:S(2)}, u32[]{:S(2)}) collective-permute-start(bf16[832,512]{1,0:T(8,128)(2,1)S(1)} %collective-permute-done.joint), channel_id=1, source_target_pairs={{0,1},{1,0},{2,3},{3,2},{4,5},{5,4},{6,7},{7,6},{8,9},{9,8},{10,11... | collective-permute-start | bytes 2555912 | tf_op jit(solution)/shard_map/ppermute | solution.py:404
  29.6 3.6 %collective-permute-start.4 = (bf16[10,128,128]{2,1,0:T(8,128)(2,1)S(1)}, bf16[10,128,128]{2,1,0:T(8,128)(2,1)S(1)}, u32[]{:S(2)}, u32[]{:S(2)}) collective-permute-start(bf16[10,128,128]{2,1,0:T(8,128)(2,1)S(1)} %get-tuple-element.40), channel_id=1, source_target_pairs={{0,1},{1,0},{2,3},{3,2},{4,5},{5,4},{6,7},{7,6},{8,9},{9,8},{10,11... | collective-permute-start | bytes 983048 | tf_op jit(solution)/shard_map/ppermute | solution.py:404
  35.0 19.4 %collective-permute-start.6 = (bf16[832,512]{1,0:T(8,128)(2,1)S(1)}, bf16[832,512]{1,0:T(8,128)(2,1)S(1)}, u32[]{:S(2)}, u32[]{:S(2)}) collective-permute-start(bf16[832,512]{1,0:T(8,128)(2,1)S(1)} %get-tuple-element.45), channel_id=1, source_target_pairs={{0,3},{2,5},{4,7},{6,9},{8,11},{10,13},{12,15},{14,17},{16,19},{18... | collective-permute-start | bytes 2555912 | tf_op jit(solution)/shard_map/ppermute | solution.py:401
  43.8 3.5 %collective-permute-start.5 = (bf16[10,128,128]{2,1,0:T(8,128)(2,1)S(1)}, bf16[10,128,128]{2,1,0:T(8,128)(2,1)S(1)}, u32[]{:S(2)}, u32[]{:S(2)}) collective-permute-start(bf16[10,128,128]{2,1,0:T(8,128)(2,1)S(1)} %get-tuple-element.44), channel_id=1, source_target_pairs={{0,1},{1,0},{2,3},{3,2},{4,5},{5,4},{6,7},{7,6},{8,9},{9,8},{10,11... | collective-permute-start | bytes 983048 | tf_op jit(solution)/shard_map/ppermute | solution.py:404
  54.4 4.3 %collective-permute-start.7 = (bf16[832,512]{1,0:T(8,128)(2,1)S(1)}, bf16[832,512]{1,0:T(8,128)(2,1)S(1)}, u32[]{:S(2)}, u32[]{:S(2)}) collective-permute-start(bf16[832,512]{1,0:T(8,128)(2,1)S(1)} %collective-permute-done.6.joint), channel_id=1, source_target_pairs={{0,1},{1,0},{2,3},{3,2},{4,5},{5,4},{6,7},{7,6},{8,9},{9,8},{10,11... | collective-permute-start | bytes 2555912 | tf_op jit(solution)/shard_map/ppermute | solution.py:404
  60.0 19.4 %collective-permute-start.8 = (bf16[832,512]{1,0:T(8,128)(2,1)S(1)}, bf16[832,512]{1,0:T(8,128)(2,1)S(1)}, u32[]{:S(2)}, u32[]{:S(2)}) collective-permute-start(bf16[832,512]{1,0:T(8,128)(2,1)S(1)} %get-tuple-element.52), channel_id=1, source_target_pairs={{0,3},{2,5},{4,7},{6,9},{8,11},{10,13},{12,15},{14,17},{16,19},{18... | collective-permute-start | bytes 2555912 | tf_op jit(solution)/shard_map/ppermute | solution.py:401
  79.4 4.3 %collective-permute-start.9 = (bf16[832,512]{1,0:T(8,128)(2,1)S(1)}, bf16[832,512]{1,0:T(8,128)(2,1)S(1)}, u32[]{:S(2)}, u32[]{:S(2)}) collective-permute-start(bf16[832,512]{1,0:T(8,128)(2,1)S(1)} %collective-permute-done.8.joint), channel_id=1, source_target_pairs={{0,1},{1,0},{2,3},{3,2},{4,5},{5,4},{6,7},{7,6},{8,9},{9,8},{10,11... | collective-permute-start | bytes 2555912 | tf_op jit(solution)/shard_map/ppermute | solution.py:404

commit v7 on v6

--- a/solution.py
+++ b/solution.py
@@ -45,8 +45,8 @@
     core = lax.axis_index("rep")
     k = cols_ref[a, s] - first
     k = jnp.clip(k, 0, 11)
-    k = jnp.where(core == 1, 11 - k, k)
-    row = jnp.where(core == 1, 3 - a, a)
+    k = jnp.where(core == 0, 11 - k, k)
+    row = jnp.where(core == 0, 3 - a, a)
     t = jnp.where(k < 4, 3 - k, k)
     return mask_ref[a, s] == 1, row, t
 
@@ -97,7 +97,7 @@
 
 
 def source_row(row):
-    return jnp.where(lax.axis_index("rep") == 1, 3 - row, row)
+    return jnp.where(lax.axis_index("rep") == 0, 3 - row, row)
 
 
 def row_block(ref, table, row, t, source=None):
@@ -395,7 +395,7 @@
 def on_device(hamiltonian, x_correction, cols, mask):
     n = lax.axis_size("rows")
     factor = 0.6 / math.sqrt(cols.shape[1] * hamiltonian.shape[-1])
-    outward = [(2 * i, 2 * i + 3) for i in range(n - 1)] + [(2 * i + 1, 2 * i - 2) for i in range(1, n)]
+    outward = [(2 * i + 1, 2 * i + 2) for i in range(n - 1)] + [(2 * i, 2 * i - 1) for i in range(1, n)]
 
     def link(x):
         return lax.ppermute(x, ("rows", "rep"), outward)

time: 86.5 us -> 86 us (level)
    ppermute x5, starting transfers between devices: 41.9 us -> 13.1 us  [link(): return lax.ppermute(x, ('rows', 'rep'), outward)]
    ppermute x5, starting transfers between devices: 10.1 us -> 38.2 us  [swap(): return lax.ppermute(x, 'rep', [(0, 1), (1, 0)])]
    ppermute x5, waiting for transfers between devices: 17.4 us -> 18.3 us  [link(): return lax.ppermute(x, ('rows', 'rep'), outward)]
where the time goes in v7:
time: 86 us; the launch traced here: 85.6 us
  starting transfers between devices  51.3 us (60%)
  waiting for transfers between devices  21.6 us (25%)
  Pallas kernels  12.6 us (15%)
    ppermute x5, starting transfers between devices, swap(): return lax.ppermute(x, 'rep', [(0, 1), (1, 0)])  38.2 us
    ppermute x5, waiting for transfers between devices, link(): return lax.ppermute(x, ('rows', 'rep'), outward)  18.3 us
    ppermute x5, starting transfers between devices, link(): return lax.ppermute(x, ('rows', 'rep'), outward)  13.1 us
    pallas_call x13, Pallas kernels, call(): pl.pallas_call(kernel, out_shape=outs, in_specs=in_specs, out_specs=out_s...  12.6 us
    ppermute x5, waiting for transfers between devices, swap(): return lax.ppermute(x, 'rep', [(0, 1), (1, 0)])  3.27 us
  transfers between devices with their start and end apart: 10, of which 7 were waited for; matrix products, arithmetic and copies ran while one was open for 0% of the time, Pallas kernels for 8%

profile of v7, /device:TPU:33, one launch (start us, length us, event | category | flops | bytes accessed | tf_op | source)
XLA Modules:
  0.0 85.6 jit_solution(16892370823934204299)
XLA Ops:
  0.0 0.0 copy-start
  0.0 1.4 %shard_map.46 = (bf16[832,512]{1,0:T(8,128)(2,1)S(1)}, s32[81]{0:T(128)S(4)}, bf16[4,8,128,128]{3,2,1,0:T(8,128)(2,1)S(1)}) custom-call(s32[4,8]{1,0:T(4,128)} %cols_hbm.1, s32[4,8]{1,0:T(4,128)} %mask_hbm.1, bf16[4,8,128,128]{3,2,1,0:T(8,128)(2,1)} %h_hbm.1), custom_call_target="tpu_custom_call" | custom-call | flops 536870912 | bytes 4194304 | tf_op jit(solution)/shard_map/pallas_call | solution.py:31
  1.4 3.7 %collective-permute-start = (bf16[832,512]{1,0:T(8,128)(2,1)S(1)}, bf16[832,512]{1,0:T(8,128)(2,1)S(1)}, u32[]{:S(2)}, u32[]{:S(2)}) collective-permute-start(bf16[832,512]{1,0:T(8,128)(2,1)S(1)} %get-tuple-element.34), channel_id=1, source_target_pairs={{1,2},{3,4},{5,6},{7,8},{9,10},{11,12},{13,14},{15,16},{17,18},{19... | collective-permute-start | bytes 2555912 | tf_op jit(solution)/shard_map/ppermute | solution.py:401
  5.1 0.0 copy-done
  5.1 0.3 shard_map.47
  5.4 1.9 %collective-permute-start.3 = (bf16[10,128,128]{2,1,0:T(8,128)(2,1)S(1)}, bf16[10,128,128]{2,1,0:T(8,128)(2,1)S(1)}, u32[]{:S(2)}, u32[]{:S(2)}) collective-permute-start(bf16[10,128,128]{2,1,0:T(8,128)(2,1)S(1)} %get-tuple-element.38), channel_id=1, source_target_pairs={{1,2},{3,4},{5,6},{7,8},{9,10},{11,12},{13,14},{15,16},{17,18},{19... | collective-permute-start | bytes 983048 | tf_op jit(solution)/shard_map/ppermute | solution.py:401
  7.3 3.6 %collective-permute-start.2 = (bf16[512,512]{1,0:T(8,128)(2,1)S(1)}, bf16[512,512]{1,0:T(8,128)(2,1)S(1)}, u32[]{:S(2)}, u32[]{:S(2)}) collective-permute-start(bf16[512,512]{1,0:T(8,128)(2,1)S(1)} %get-tuple-element.37), channel_id=1, source_target_pairs={{1,2},{3,4},{5,6},{7,8},{9,10},{11,12},{13,14},{15,16},{17,18},{19... | collective-permute-start | bytes 1572872 | tf_op jit(solution)/shard_map/ppermute | solution.py:401
  11.0 4.8 %collective-permute-done.joint = bf16[832,512]{1,0:T(8,128)(2,1)S(1)} collective-permute-done((bf16[832,512]{1,0:T(8,128)(2,1)S(1)}, bf16[832,512]{1,0:T(8,128)(2,1)S(1)}, u32[]{:S(2)}, u32[]{:S(2)}) %collective-permute-start) | collective-permute-done | bytes 852000 | tf_op jit(solution)/shard_map/ppermute | solution.py:401
  15.7 12.0 %collective-permute-start.1 = (bf16[832,512]{1,0:T(8,128)(2,1)S(1)}, bf16[832,512]{1,0:T(8,128)(2,1)S(1)}, u32[]{:S(2)}, u32[]{:S(2)}) collective-permute-start(bf16[832,512]{1,0:T(8,128)(2,1)S(1)} %collective-permute-done.joint), channel_id=1, source_target_pairs={{0,1},{1,0},{2,3},{3,2},{4,5},{5,4},{6,7},{7,6},{8,9},{9,8},{10,11... | collective-permute-start | bytes 2555912 | tf_op jit(solution)/shard_map/ppermute | solution.py:404
  27.8 1.5 %shard_map.48 = (bf16[512,1536]{1,0:T(8,128)(2,1)S(1)}, f32[512,1536]{1,0:T(8,128)S(1)}) custom-call(s32[81]{0:T(128)S(4)} %get-tuple-element.31.table.index, bf16[4,8,128,128]{3,2,1,0:T(8,128)(2,1)S(1)} %get-tuple-element.33.h_ref, bf16[4,8,128,128]{3,2,1,0:T(8,128)(2,1)S(1)} %copy-done, bf16[832,512]{1,0:T(8,128)(2,1)S(1)} %collective-permute-done.joint), custom_call_target="tpu_custom_call" | custom-call | flops 34359738368 | bytes 4194304 | tf_op jit(solution)/shard_map/pallas_call | solution.py:31
  29.3 0.0 collective-permute-done.3.xa
  29.3 0.1 shard_map.50
  29.4 1.9 %collective-permute-start.4 = (bf16[10,128,128]{2,1,0:T(8,128)(2,1)S(1)}, bf16[10,128,128]{2,1,0:T(8,128)(2,1)S(1)}, u32[]{:S(2)}, u32[]{:S(2)}) collective-permute-start(bf16[10,128,128]{2,1,0:T(8,128)(2,1)S(1)} %get-tuple-element.40), channel_id=1, source_target_pairs={{0,1},{1,0},{2,3},{3,2},{4,5},{5,4},{6,7},{7,6},{8,9},{9,8},{10,11... | collective-permute-start | bytes 983048 | tf_op jit(solution)/shard_map/ppermute | solution.py:404
  31.3 0.0 collective-permute-done.1.twin
  31.4 0.6 shard_map.49.refs_1_
  32.0 1.0 %collective-permute-done.4.refs_4_ = bf16[10,128,128]{2,1,0:T(8,128)(2,1)S(1)} collective-permute-done((bf16[10,128,128]{2,1,0:T(8,128)(2,1)S(1)}, bf16[10,128,128]{2,1,0:T(8,128)(2,1)S(1)}, u32[]{:S(2)}, u32[]{:S(2)}) %collective-permute-start.4) | collective-permute-done | bytes 327712 | tf_op jit(solution)/shard_map/ppermute | solution.py:404
  32.9 0.8 shard_map.51
  33.8 0.0 collective-permute-done.2.refs_3_
  33.8 0.5 shard_map.52
  34.3 1.9 %collective-permute-start.6 = (bf16[832,512]{1,0:T(8,128)(2,1)S(1)}, bf16[832,512]{1,0:T(8,128)(2,1)S(1)}, u32[]{:S(2)}, u32[]{:S(2)}) collective-permute-start(bf16[832,512]{1,0:T(8,128)(2,1)S(1)} %get-tuple-element.45), channel_id=1, source_target_pairs={{1,2},{3,4},{5,6},{7,8},{9,10},{11,12},{13,14},{15,16},{17,18},{19... | collective-permute-start | bytes 2555912 | tf_op jit(solution)/shard_map/ppermute | solution.py:401
  36.3 9.3 %collective-permute-start.5 = (bf16[10,128,128]{2,1,0:T(8,128)(2,1)S(1)}, bf16[10,128,128]{2,1,0:T(8,128)(2,1)S(1)}, u32[]{:S(2)}, u32[]{:S(2)}) collective-permute-start(bf16[10,128,128]{2,1,0:T(8,128)(2,1)S(1)} %get-tuple-element.44), channel_id=1, source_target_pairs={{0,1},{1,0},{2,3},{3,2},{4,5},{5,4},{6,7},{7,6},{8,9},{9,8},{10,11... | collective-permute-start | bytes 983048 | tf_op jit(solution)/shard_map/ppermute | solution.py:404
  45.6 1.2 %collective-permute-done.5.side = bf16[10,128,128]{2,1,0:T(8,128)(2,1)S(1)} collective-permute-done((bf16[10,128,128]{2,1,0:T(8,128)(2,1)S(1)}, bf16[10,128,128]{2,1,0:T(8,128)(2,1)S(1)}, u32[]{:S(2)}, u32[]{:S(2)}) %collective-permute-start.5) | collective-permute-done | bytes 327712 | tf_op jit(solution)/shard_map/ppermute | solution.py:404
  46.8 0.1 shard_map.53.band
  46.9 1.7 %collective-permute-done.6.joint = bf16[832,512]{1,0:T(8,128)(2,1)S(1)} collective-permute-done((bf16[832,512]{1,0:T(8,128)(2,1)S(1)}, bf16[832,512]{1,0:T(8,128)(2,1)S(1)}, u32[]{:S(2)}, u32[]{:S(2)}) %collective-permute-start.6) | collective-permute-done | bytes 852000 | tf_op jit(solution)/shard_map/ppermute | solution.py:401
  48.7 7.5 %collective-permute-start.7 = (bf16[832,512]{1,0:T(8,128)(2,1)S(1)}, bf16[832,512]{1,0:T(8,128)(2,1)S(1)}, u32[]{:S(2)}, u32[]{:S(2)}) collective-permute-start(bf16[832,512]{1,0:T(8,128)(2,1)S(1)} %collective-permute-done.6.joint), channel_id=1, source_target_pairs={{0,1},{1,0},{2,3},{3,2},{4,5},{5,4},{6,7},{7,6},{8,9},{9,8},{10,11... | collective-permute-start | bytes 2555912 | tf_op jit(solution)/shard_map/ppermute | solution.py:404
  56.2 1.5 %shard_map.54 = (bf16[512,512]{1,0:T(8,128)(2,1)S(1)}, f32[512,512]{1,0:T(8,128)S(1)}, f32[512,512]{1,0:T(8,128)S(1)}, f32[512,1024]{1,0:T(8,128)S(1)}) custom-call(f32[48,128]{1,0:T(8,128)S(1)} %get-tuple-element.32.table.refs_0_, bf16[512,1536]{1,0:T(8,128)(2,1)S(1)} %shard_map.53.band, bf16[832,512]{1,0:T(8,128)(2,1)S(1)} %collective-permute-done.6.joint), custom_call_target="tpu_custom_call" | custom-call | flops 34359738368 | bytes 4194304 | tf_op jit(solution)/shard_map/pallas_call | solution.py:31
  57.6 0.5 collective-permute-done.7.twin
  58.2 1.3 %shard_map.55 = (bf16[512,1536]{1,0:T(8,128)(2,1)S(1)}, bf16[832,512]{1,0:T(8,128)(2,1)S(1)}, bf16[512,1024]{1,0:T(8,128)(2,1)S(1)}) custom-call(f32[48,128]{1,0:T(8,128)S(1)} %get-tuple-element.32.table.refs_0_, bf16[512,1536]{1,0:T(8,128)(2,1)S(1)} %shard_map.53.band, bf16[512,512]{1,0:T(8,128)(2,1)S(1)} %get-tuple-element.46.sq_r, ...), custom_call_target="tpu_custom_call" | custom-call | flops 536870912 | bytes 4194304 | tf_op jit(solution)/shard_map/pallas_call | solution.py:31
  59.4 1.9 %collective-permute-start.8 = (bf16[832,512]{1,0:T(8,128)(2,1)S(1)}, bf16[832,512]{1,0:T(8,128)(2,1)S(1)}, u32[]{:S(2)}, u32[]{:S(2)}) collective-permute-start(bf16[832,512]{1,0:T(8,128)(2,1)S(1)} %get-tuple-element.52), channel_id=1, source_target_pairs={{1,2},{3,4},{5,6},{7,8},{9,10},{11,12},{13,14},{15,16},{17,18},{19... | collective-permute-start | bytes 2555912 | tf_op jit(solution)/shard_map/ppermute | solution.py:401
  61.4 0.5 shard_map.56.band
  61.9 11.8 %collective-permute-done.8.joint = bf16[832,512]{1,0:T(8,128)(2,1)S(1)} collective-permute-done((bf16[832,512]{1,0:T(8,128)(2,1)S(1)}, bf16[832,512]{1,0:T(8,128)(2,1)S(1)}, u32[]{:S(2)}, u32[]{:S(2)}) %collective-permute-start.8) | collective-permute-done | bytes 852000 | tf_op jit(solution)/shard_map/ppermute | solution.py:401
  73.8 7.4 %collective-permute-start.9 = (bf16[832,512]{1,0:T(8,128)(2,1)S(1)}, bf16[832,512]{1,0:T(8,128)(2,1)S(1)}, u32[]{:S(2)}, u32[]{:S(2)}) collective-permute-start(bf16[832,512]{1,0:T(8,128)(2,1)S(1)} %collective-permute-done.8.joint), channel_id=1, source_target_pairs={{0,1},{1,0},{2,3},{3,2},{4,5},{5,4},{6,7},{7,6},{8,9},{9,8},{10,11... | collective-permute-start | bytes 2555912 | tf_op jit(solution)/shard_map/ppermute | solution.py:404
  81.2 1.5 %shard_map.57 = (bf16[512,512]{1,0:T(8,128)(2,1)S(1)}, f32[512,512]{1,0:T(8,128)S(1)}, f32[512,512]{1,0:T(8,128)S(1)}, f32[512,1024]{1,0:T(8,128)S(1)}) custom-call(f32[48,128]{1,0:T(8,128)S(1)} %get-tuple-element.32.table.refs_0_, bf16[512,1536]{1,0:T(8,128)(2,1)S(1)} %shard_map.56.band, bf16[832,512]{1,0:T(8,128)(2,1)S(1)} %collective-permute-done.8.joint), custom_call_target="tpu_custom_call" | custom-call | flops 34359738368 | bytes 4194304 | tf_op jit(solution)/shard_map/pallas_call | solution.py:31
  82.6 0.5 collective-permute-done.9.twin
  83.2 2.5 %shard_map.58 = bf16[4,4,128,128]{3,2,1,0:T(8,128)(2,1)} custom-call(s32[81]{0:T(128)S(4)} %get-tuple-element.31.table.index, f32[48,128]{1,0:T(8,128)S(1)} %get-tuple-element.32.table.refs_0_, bf16[512,1536]{1,0:T(8,128)(2,1)S(1)} %shard_map.56.band, bf16[512,512]{1,0:T(8,128)(2,1)S(1)} %get-tuple-element.53.sq_r, f32[512,512]{1,0:T(8,128)S(1)} %get-tuple-element.54.part_l, ...), custom_call_target="tpu_custom_call" | custom-call | flops 536870912 | bytes 4194304 | tf_op jit(solution)/shard_map/pallas_call | solution.py:31
Async XLA Ops:
  0.0 5.1 %copy-start = (bf16[4,8,128,128]{3,2,1,0:T(8,128)(2,1)S(1)}, bf16[4,8,128,128]{3,2,1,0:T(8,128)(2,1)}, u32[]{:S(2)}) copy-start(bf16[4,8,128,128]{3,2,1,0:T(8,128)(2,1)} %x_ref.3) | copy-start | bytes 3145732
  1.4 14.3 %collective-permute-start = (bf16[832,512]{1,0:T(8,128)(2,1)S(1)}, bf16[832,512]{1,0:T(8,128)(2,1)S(1)}, u32[]{:S(2)}, u32[]{:S(2)}) collective-permute-start(bf16[832,512]{1,0:T(8,128)(2,1)S(1)} %get-tuple-element.34), channel_id=1, source_target_pairs={{1,2},{3,4},{5,6},{7,8},{9,10},{11,12},{13,14},{15,16},{17,18},{19... | collective-permute-start | bytes 2555912 | tf_op jit(solution)/shard_map/ppermute | solution.py:401
  5.4 23.9 %collective-permute-start.3 = (bf16[10,128,128]{2,1,0:T(8,128)(2,1)S(1)}, bf16[10,128,128]{2,1,0:T(8,128)(2,1)S(1)}, u32[]{:S(2)}, u32[]{:S(2)}) collective-permute-start(bf16[10,128,128]{2,1,0:T(8,128)(2,1)S(1)} %get-tuple-element.38), channel_id=1, source_target_pairs={{1,2},{3,4},{5,6},{7,8},{9,10},{11,12},{13,14},{15,16},{17,18},{19... | collective-permute-start | bytes 983048 | tf_op jit(solution)/shard_map/ppermute | solution.py:401
  7.3 26.5 %collective-permute-start.2 = (bf16[512,512]{1,0:T(8,128)(2,1)S(1)}, bf16[512,512]{1,0:T(8,128)(2,1)S(1)}, u32[]{:S(2)}, u32[]{:S(2)}) collective-permute-start(bf16[512,512]{1,0:T(8,128)(2,1)S(1)} %get-tuple-element.37), channel_id=1, source_target_pairs={{1,2},{3,4},{5,6},{7,8},{9,10},{11,12},{13,14},{15,16},{17,18},{19... | collective-permute-start | bytes 1572872 | tf_op jit(solution)/shard_map/ppermute | solution.py:401
  15.7 15.6 %collective-permute-start.1 = (bf16[832,512]{1,0:T(8,128)(2,1)S(1)}, bf16[832,512]{1,0:T(8,128)(2,1)S(1)}, u32[]{:S(2)}, u32[]{:S(2)}) collective-permute-start(bf16[832,512]{1,0:T(8,128)(2,1)S(1)} %collective-permute-done.joint), channel_id=1, source_target_pairs={{0,1},{1,0},{2,3},{3,2},{4,5},{5,4},{6,7},{7,6},{8,9},{9,8},{10,11... | collective-permute-start | bytes 2555912 | tf_op jit(solution)/shard_map/ppermute | solution.py:404
  29.4 3.5 %collective-permute-start.4 = (bf16[10,128,128]{2,1,0:T(8,128)(2,1)S(1)}, bf16[10,128,128]{2,1,0:T(8,128)(2,1)S(1)}, u32[]{:S(2)}, u32[]{:S(2)}) collective-permute-start(bf16[10,128,128]{2,1,0:T(8,128)(2,1)S(1)} %get-tuple-element.40), channel_id=1, source_target_pairs={{0,1},{1,0},{2,3},{3,2},{4,5},{5,4},{6,7},{7,6},{8,9},{9,8},{10,11... | collective-permute-start | bytes 983048 | tf_op jit(solution)/shard_map/ppermute | solution.py:404
  34.3 14.3 %collective-permute-start.6 = (bf16[832,512]{1,0:T(8,128)(2,1)S(1)}, bf16[832,512]{1,0:T(8,128)(2,1)S(1)}, u32[]{:S(2)}, u32[]{:S(2)}) collective-permute-start(bf16[832,512]{1,0:T(8,128)(2,1)S(1)} %get-tuple-element.45), channel_id=1, source_target_pairs={{1,2},{3,4},{5,6},{7,8},{9,10},{11,12},{13,14},{15,16},{17,18},{19... | collective-permute-start | bytes 2555912 | tf_op jit(solution)/shard_map/ppermute | solution.py:401
  36.3 10.5 %collective-permute-start.5 = (bf16[10,128,128]{2,1,0:T(8,128)(2,1)S(1)}, bf16[10,128,128]{2,1,0:T(8,128)(2,1)S(1)}, u32[]{:S(2)}, u32[]{:S(2)}) collective-permute-start(bf16[10,128,128]{2,1,0:T(8,128)(2,1)S(1)} %get-tuple-element.44), channel_id=1, source_target_pairs={{0,1},{1,0},{2,3},{3,2},{4,5},{5,4},{6,7},{7,6},{8,9},{9,8},{10,11... | collective-permute-start | bytes 983048 | tf_op jit(solution)/shard_map/ppermute | solution.py:404
  48.7 9.5 %collective-permute-start.7 = (bf16[832,512]{1,0:T(8,128)(2,1)S(1)}, bf16[832,512]{1,0:T(8,128)(2,1)S(1)}, u32[]{:S(2)}, u32[]{:S(2)}) collective-permute-start(bf16[832,512]{1,0:T(8,128)(2,1)S(1)} %collective-permute-done.6.joint), channel_id=1, source_target_pairs={{0,1},{1,0},{2,3},{3,2},{4,5},{5,4},{6,7},{7,6},{8,9},{9,8},{10,11... | collective-permute-start | bytes 2555912 | tf_op jit(solution)/shard_map/ppermute | solution.py:404
  59.4 14.3 %collective-permute-start.8 = (bf16[832,512]{1,0:T(8,128)(2,1)S(1)}, bf16[832,512]{1,0:T(8,128)(2,1)S(1)}, u32[]{:S(2)}, u32[]{:S(2)}) collective-permute-start(bf16[832,512]{1,0:T(8,128)(2,1)S(1)} %get-tuple-element.52), channel_id=1, source_target_pairs={{1,2},{3,4},{5,6},{7,8},{9,10},{11,12},{13,14},{15,16},{17,18},{19... | collective-permute-start | bytes 2555912 | tf_op jit(solution)/shard_map/ppermute | solution.py:401
  73.8 9.4 %collective-permute-start.9 = (bf16[832,512]{1,0:T(8,128)(2,1)S(1)}, bf16[832,512]{1,0:T(8,128)(2,1)S(1)}, u32[]{:S(2)}, u32[]{:S(2)}) collective-permute-start(bf16[832,512]{1,0:T(8,128)(2,1)S(1)} %collective-permute-done.8.joint), channel_id=1, source_target_pairs={{0,1},{1,0},{2,3},{3,2},{4,5},{5,4},{6,7},{7,6},{8,9},{9,8},{10,11... | collective-permute-start | bytes 2555912 | tf_op jit(solution)/shard_map/ppermute | solution.py:404

commit v8 on v7

--- a/solution.py
+++ b/solution.py
@@ -190,9 +190,9 @@
     return tile(ref, r, t)
 
 
-def product(left, right, columns, finish):
+def product(left, right, columns, finish, rows=(0, 1)):
     for u in columns:
-        for r in range(2):
+        for r in rows:
             if (r, u) in ((1, 1), (0, 5)):
                 continue
             xs, ys = [], []
@@ -256,7 +256,7 @@
     product(lambda r, t: left_tile(xo, r, t) if t in LEFT else None, right, range(6), keep)
 
 
-def center_kernel(factor, table, half, xo, xrc, xa2, band, send, xlc):
+def center_kernel(factor, table, half, xo, xrc, xa2, band, send, begun, xlc):
     spread_twin(lambda i: xa2[i], xlc)
     right = right_operand(None, xlc, lambda r, u: tile(xo, r, u), xrc, None)
     diag = eye()
@@ -273,12 +273,20 @@
         each_block(table, r, u, total, store)
 
     product(lambda r, t: left_tile(half, r, t), right, OWN, start)
-
-
-def side_kernel(factor, table, half, xo, xb, band_in, send_in, band, send, side):
-    right = right_operand(None, None, lambda r, u: tile(xo, r, u), None, xb)
+    product(
+        lambda r, t: left_tile(half, r, t) if t in OWN else None,
+        right,
+        RIGHT,
+        lambda r, u, total: put_tile(begun, r, u - 4, total),
+    )
+
+
+def side_kernel(factor, table, half, begun, xb, band_in, send_in, band, send, side):
+    right = right_operand(None, None, None, None, xb)
 
     def start(r, u, total):
+        total = total + tile(begun, r, u - 4)
+
         def store(row, t, block):
             value = (-factor * block).astype(BF)
             put(band, row, t, value)
@@ -288,7 +296,7 @@
 
         each_block(table, r, u, total, store)
 
-    product(lambda r, t: left_tile(half, r, t), right, RIGHT, start)
+    product(lambda r, t: left_tile(half, r, t) if t in RIGHT else None, right, RIGHT, start)
 
 
 def mine_squares_kernel(table, band, joint, sq_r, part_l, sums, more, rc):
@@ -334,10 +342,10 @@
         each_block(table, r, u, total, store)
 
     product(lambda r, t: left_tile(band, r, t) if t in LEFT else None, right, LEFT + OWN, keep)
-    product(lambda r, t: None if t in RIGHT else left_tile(sq, r, t), right, columns, step)
-    if after:
-        after(0)
-        after(1)
+    for half in range(2):
+        product(lambda r, t: None if t in RIGHT else left_tile(sq, r, t), right, columns, step, (half,))
+        if after:
+            after(half)
 
 
 def step_kernel(table, band, sq_r, part_l, sums, more, twin, new, send, sq, lc):
@@ -446,10 +454,10 @@
     xa_copy, x_corner = call(spread_kernel, [CORNER, SQUARE], [VMEM] * 2, [VMEM] * 2, [], 0, xa_halo, part)
     xa_twin = swap(xa_copy)
     half = call(half_kernel, BANDED, VMEM, [VMEM] + [VMEM] * 3, [square], 16 * flops, marks, xo, h_twin, part)
-    band, send = call(
+    band, send, begun = call(
         lambda *refs: center_kernel(factor, *refs),
-        [BANDED, SEND],
-        [VMEM] * 2,
+        [BANDED, SEND, SUMS],
+        [VMEM] * 3,
         [VMEM] * 5,
         [square],
         flops,
@@ -462,7 +470,7 @@
         [VMEM] * 6,
         [],
         flops,
-        marks, half, xo, xb_halo, band, send,
+        marks, half, begun, xb_halo, band, send,
         alias={4: 0, 5: 1},
     )
     halo = link(send)

time: 86 us -> 85.8 us (level)
  no operation moved by 1% of the time
where the time goes in v8:
time: 85.8 us; the launch traced here: 85.4 us
  starting transfers between devices  51 us (59%)
  waiting for transfers between devices  21.7 us (25%)
  Pallas kernels  12.5 us (15%)
    ppermute x5, starting transfers between devices, swap(): return lax.ppermute(x, 'rep', [(0, 1), (1, 0)])  37.9 us
    ppermute x5, waiting for transfers between devices, link(): return lax.ppermute(x, ('rows', 'rep'), outward)  18.5 us
    ppermute x5, starting transfers between devices, link(): return lax.ppermute(x, ('rows', 'rep'), outward)  13.1 us
    pallas_call x13, Pallas kernels, call(): pl.pallas_call(kernel, out_shape=outs, in_specs=in_specs, out_specs=out_s...  12.5 us
    ppermute x5, waiting for transfers between devices, swap(): return lax.ppermute(x, 'rep', [(0, 1), (1, 0)])  3.25 us
  transfers between devices with their start and end apart: 10, of which 7 were waited for; matrix products, arithmetic and copies ran while one was open for 0% of the time, Pallas kernels for 8%

profile of v8, /device:TPU:33, one launch (start us, length us, event | category | flops | bytes accessed | tf_op | source)
XLA Modules:
  0.0 85.4 jit_solution(8760645002608762576)
XLA Ops:
  0.0 0.0 copy-start
  0.0 1.4 %shard_map.46 = (bf16[832,512]{1,0:T(8,128)(2,1)S(1)}, s32[81]{0:T(128)S(4)}, bf16[4,8,128,128]{3,2,1,0:T(8,128)(2,1)S(1)}) custom-call(s32[4,8]{1,0:T(4,128)} %cols_hbm.1, s32[4,8]{1,0:T(4,128)} %mask_hbm.1, bf16[4,8,128,128]{3,2,1,0:T(8,128)(2,1)} %h_hbm.1), custom_call_target="tpu_custom_call" | custom-call | flops 536870912 | bytes 4194304 | tf_op jit(solution)/shard_map/pallas_call | solution.py:31
  1.4 3.7 %collective-permute-start = (bf16[832,512]{1,0:T(8,128)(2,1)S(1)}, bf16[832,512]{1,0:T(8,128)(2,1)S(1)}, u32[]{:S(2)}, u32[]{:S(2)}) collective-permute-start(bf16[832,512]{1,0:T(8,128)(2,1)S(1)} %get-tuple-element.35), channel_id=1, source_target_pairs={{1,2},{3,4},{5,6},{7,8},{9,10},{11,12},{13,14},{15,16},{17,18},{19... | collective-permute-start | bytes 2555912 | tf_op jit(solution)/shard_map/ppermute | solution.py:409
  5.1 0.0 copy-done
  5.1 0.3 shard_map.47
  5.4 1.9 %collective-permute-start.2 = (bf16[10,128,128]{2,1,0:T(8,128)(2,1)S(1)}, bf16[10,128,128]{2,1,0:T(8,128)(2,1)S(1)}, u32[]{:S(2)}, u32[]{:S(2)}) collective-permute-start(bf16[10,128,128]{2,1,0:T(8,128)(2,1)S(1)} %get-tuple-element.38), channel_id=1, source_target_pairs={{1,2},{3,4},{5,6},{7,8},{9,10},{11,12},{13,14},{15,16},{17,18},{19... | collective-permute-start | bytes 983048 | tf_op jit(solution)/shard_map/ppermute | solution.py:409
  7.3 3.6 %collective-permute-start.4 = (bf16[512,512]{1,0:T(8,128)(2,1)S(1)}, bf16[512,512]{1,0:T(8,128)(2,1)S(1)}, u32[]{:S(2)}, u32[]{:S(2)}) collective-permute-start(bf16[512,512]{1,0:T(8,128)(2,1)S(1)} %get-tuple-element.42), channel_id=1, source_target_pairs={{1,2},{3,4},{5,6},{7,8},{9,10},{11,12},{13,14},{15,16},{17,18},{19... | collective-permute-start | bytes 1572872 | tf_op jit(solution)/shard_map/ppermute | solution.py:409
  11.0 4.8 %collective-permute-done.joint = bf16[832,512]{1,0:T(8,128)(2,1)S(1)} collective-permute-done((bf16[832,512]{1,0:T(8,128)(2,1)S(1)}, bf16[832,512]{1,0:T(8,128)(2,1)S(1)}, u32[]{:S(2)}, u32[]{:S(2)}) %collective-permute-start) | collective-permute-done | bytes 852000 | tf_op jit(solution)/shard_map/ppermute | solution.py:409
  15.7 12.0 %collective-permute-start.1 = (bf16[832,512]{1,0:T(8,128)(2,1)S(1)}, bf16[832,512]{1,0:T(8,128)(2,1)S(1)}, u32[]{:S(2)}, u32[]{:S(2)}) collective-permute-start(bf16[832,512]{1,0:T(8,128)(2,1)S(1)} %collective-permute-done.joint), channel_id=1, source_target_pairs={{0,1},{1,0},{2,3},{3,2},{4,5},{5,4},{6,7},{7,6},{8,9},{9,8},{10,11... | collective-permute-start | bytes 2555912 | tf_op jit(solution)/shard_map/ppermute | solution.py:412
  27.8 1.5 %shard_map.48 = (bf16[512,1536]{1,0:T(8,128)(2,1)S(1)}, f32[512,1536]{1,0:T(8,128)S(1)}) custom-call(s32[81]{0:T(128)S(4)} %get-tuple-element.32.table.index, bf16[4,8,128,128]{3,2,1,0:T(8,128)(2,1)S(1)} %get-tuple-element.34.h_ref, bf16[4,8,128,128]{3,2,1,0:T(8,128)(2,1)S(1)} %copy-done, bf16[832,512]{1,0:T(8,128)(2,1)S(1)} %collective-permute-done.joint), custom_call_target="tpu_custom_call" | custom-call | flops 34359738368 | bytes 4194304 | tf_op jit(solution)/shard_map/pallas_call | solution.py:31
  29.3 0.0 collective-permute-done.2.xa
  29.3 0.1 shard_map.50
  29.4 1.9 %collective-permute-start.3 = (bf16[10,128,128]{2,1,0:T(8,128)(2,1)S(1)}, bf16[10,128,128]{2,1,0:T(8,128)(2,1)S(1)}, u32[]{:S(2)}, u32[]{:S(2)}) collective-permute-start(bf16[10,128,128]{2,1,0:T(8,128)(2,1)S(1)} %get-tuple-element.40), channel_id=1, source_target_pairs={{0,1},{1,0},{2,3},{3,2},{4,5},{5,4},{6,7},{7,6},{8,9},{9,8},{10,11... | collective-permute-start | bytes 983048 | tf_op jit(solution)/shard_map/ppermute | solution.py:412
  31.3 0.0 collective-permute-done.1.twin
  31.4 0.6 shard_map.49.refs_1_
  32.0 1.0 %collective-permute-done.3.refs_4_ = bf16[10,128,128]{2,1,0:T(8,128)(2,1)S(1)} collective-permute-done((bf16[10,128,128]{2,1,0:T(8,128)(2,1)S(1)}, bf16[10,128,128]{2,1,0:T(8,128)(2,1)S(1)}, u32[]{:S(2)}, u32[]{:S(2)}) %collective-permute-start.3) | collective-permute-done | bytes 327712 | tf_op jit(solution)/shard_map/ppermute | solution.py:412
  32.9 1.0 %shard_map.51 = (bf16[512,1536]{1,0:T(8,128)(2,1)S(1)}, bf16[832,512]{1,0:T(8,128)(2,1)S(1)}, f32[512,512]{1,0:T(8,128)S(1)}) custom-call(f32[48,128]{1,0:T(8,128)S(1)} %get-tuple-element.33.table.refs_0_, bf16[512,1536]{1,0:T(8,128)(2,1)S(1)} %shard_map.49.refs_1_, bf16[512,1536]{1,0:T(8,128)(2,1)S(1)} %get-tuple-element.36.xo.refs_2_, ...), custom_call_target="tpu_custom_call" | custom-call | flops 536870912 | bytes 4194304 | tf_op jit(solution)/shard_map/pallas_call | solution.py:31
  33.9 0.0 collective-permute-done.4.refs_3_
  34.0 0.4 shard_map.52
  34.3 1.9 %collective-permute-start.6 = (bf16[832,512]{1,0:T(8,128)(2,1)S(1)}, bf16[832,512]{1,0:T(8,128)(2,1)S(1)}, u32[]{:S(2)}, u32[]{:S(2)}) collective-permute-start(bf16[832,512]{1,0:T(8,128)(2,1)S(1)} %get-tuple-element.47), channel_id=1, source_target_pairs={{1,2},{3,4},{5,6},{7,8},{9,10},{11,12},{13,14},{15,16},{17,18},{19... | collective-permute-start | bytes 2555912 | tf_op jit(solution)/shard_map/ppermute | solution.py:409
  36.3 9.1 %collective-permute-start.5 = (bf16[10,128,128]{2,1,0:T(8,128)(2,1)S(1)}, bf16[10,128,128]{2,1,0:T(8,128)(2,1)S(1)}, u32[]{:S(2)}, u32[]{:S(2)}) collective-permute-start(bf16[10,128,128]{2,1,0:T(8,128)(2,1)S(1)} %get-tuple-element.46), channel_id=1, source_target_pairs={{0,1},{1,0},{2,3},{3,2},{4,5},{5,4},{6,7},{7,6},{8,9},{9,8},{10,11... | collective-permute-start | bytes 983048 | tf_op jit(solution)/shard_map/ppermute | solution.py:412
  45.4 1.2 %collective-permute-done.5.side = bf16[10,128,128]{2,1,0:T(8,128)(2,1)S(1)} collective-permute-done((bf16[10,128,128]{2,1,0:T(8,128)(2,1)S(1)}, bf16[10,128,128]{2,1,0:T(8,128)(2,1)S(1)}, u32[]{:S(2)}, u32[]{:S(2)}) %collective-permute-start.5) | collective-permute-done | bytes 327712 | tf_op jit(solution)/shard_map/ppermute | solution.py:412
  46.7 0.1 shard_map.53.band
  46.8 1.9 %collective-permute-done.6.joint = bf16[832,512]{1,0:T(8,128)(2,1)S(1)} collective-permute-done((bf16[832,512]{1,0:T(8,128)(2,1)S(1)}, bf16[832,512]{1,0:T(8,128)(2,1)S(1)}, u32[]{:S(2)}, u32[]{:S(2)}) %collective-permute-start.6) | collective-permute-done | bytes 852000 | tf_op jit(solution)/shard_map/ppermute | solution.py:409
  48.6 7.4 %collective-permute-start.7 = (bf16[832,512]{1,0:T(8,128)(2,1)S(1)}, bf16[832,512]{1,0:T(8,128)(2,1)S(1)}, u32[]{:S(2)}, u32[]{:S(2)}) collective-permute-start(bf16[832,512]{1,0:T(8,128)(2,1)S(1)} %collective-permute-done.6.joint), channel_id=1, source_target_pairs={{0,1},{1,0},{2,3},{3,2},{4,5},{5,4},{6,7},{7,6},{8,9},{9,8},{10,11... | collective-permute-start | bytes 2555912 | tf_op jit(solution)/shard_map/ppermute | solution.py:412
  56.0 1.5 %shard_map.54 = (bf16[512,512]{1,0:T(8,128)(2,1)S(1)}, f32[512,512]{1,0:T(8,128)S(1)}, f32[512,512]{1,0:T(8,128)S(1)}, f32[512,1024]{1,0:T(8,128)S(1)}) custom-call(f32[48,128]{1,0:T(8,128)S(1)} %get-tuple-element.33.table.refs_0_, bf16[512,1536]{1,0:T(8,128)(2,1)S(1)} %shard_map.53.band, bf16[832,512]{1,0:T(8,128)(2,1)S(1)} %collective-permute-done.6.joint), custom_call_target="tpu_custom_call" | custom-call | flops 34359738368 | bytes 4194304 | tf_op jit(solution)/shard_map/pallas_call | solution.py:31
  57.5 0.5 collective-permute-done.7.twin
  58.0 1.2 %shard_map.55 = (bf16[512,1536]{1,0:T(8,128)(2,1)S(1)}, bf16[832,512]{1,0:T(8,128)(2,1)S(1)}, bf16[512,1024]{1,0:T(8,128)(2,1)S(1)}) custom-call(f32[48,128]{1,0:T(8,128)S(1)} %get-tuple-element.33.table.refs_0_, bf16[512,1536]{1,0:T(8,128)(2,1)S(1)} %shard_map.53.band, bf16[512,512]{1,0:T(8,128)(2,1)S(1)} %get-tuple-element.48.sq_r, ...), custom_call_target="tpu_custom_call" | custom-call | flops 536870912 | bytes 4194304 | tf_op jit(solution)/shard_map/pallas_call | solution.py:31
  59.2 1.9 %collective-permute-start.8 = (bf16[832,512]{1,0:T(8,128)(2,1)S(1)}, bf16[832,512]{1,0:T(8,128)(2,1)S(1)}, u32[]{:S(2)}, u32[]{:S(2)}) collective-permute-start(bf16[832,512]{1,0:T(8,128)(2,1)S(1)} %get-tuple-element.54), channel_id=1, source_target_pairs={{1,2},{3,4},{5,6},{7,8},{9,10},{11,12},{13,14},{15,16},{17,18},{19... | collective-permute-start | bytes 2555912 | tf_op jit(solution)/shard_map/ppermute | solution.py:409
  61.2 0.5 shard_map.56.band
  61.7 11.8 %collective-permute-done.8.joint = bf16[832,512]{1,0:T(8,128)(2,1)S(1)} collective-permute-done((bf16[832,512]{1,0:T(8,128)(2,1)S(1)}, bf16[832,512]{1,0:T(8,128)(2,1)S(1)}, u32[]{:S(2)}, u32[]{:S(2)}) %collective-permute-start.8) | collective-permute-done | bytes 852000 | tf_op jit(solution)/shard_map/ppermute | solution.py:409
  73.6 7.4 %collective-permute-start.9 = (bf16[832,512]{1,0:T(8,128)(2,1)S(1)}, bf16[832,512]{1,0:T(8,128)(2,1)S(1)}, u32[]{:S(2)}, u32[]{:S(2)}) collective-permute-start(bf16[832,512]{1,0:T(8,128)(2,1)S(1)} %collective-permute-done.8.joint), channel_id=1, source_target_pairs={{0,1},{1,0},{2,3},{3,2},{4,5},{5,4},{6,7},{7,6},{8,9},{9,8},{10,11... | collective-permute-start | bytes 2555912 | tf_op jit(solution)/shard_map/ppermute | solution.py:412
  81.0 1.5 %shard_map.57 = (bf16[512,512]{1,0:T(8,128)(2,1)S(1)}, f32[512,512]{1,0:T(8,128)S(1)}, f32[512,512]{1,0:T(8,128)S(1)}, f32[512,1024]{1,0:T(8,128)S(1)}) custom-call(f32[48,128]{1,0:T(8,128)S(1)} %get-tuple-element.33.table.refs_0_, bf16[512,1536]{1,0:T(8,128)(2,1)S(1)} %shard_map.56.band, bf16[832,512]{1,0:T(8,128)(2,1)S(1)} %collective-permute-done.8.joint), custom_call_target="tpu_custom_call" | custom-call | flops 34359738368 | bytes 4194304 | tf_op jit(solution)/shard_map/pallas_call | solution.py:31
  82.4 0.5 collective-permute-done.9.twin
  83.0 2.5 %shard_map.58 = bf16[4,4,128,128]{3,2,1,0:T(8,128)(2,1)} custom-call(s32[81]{0:T(128)S(4)} %get-tuple-element.32.table.index, f32[48,128]{1,0:T(8,128)S(1)} %get-tuple-element.33.table.refs_0_, bf16[512,1536]{1,0:T(8,128)(2,1)S(1)} %shard_map.56.band, bf16[512,512]{1,0:T(8,128)(2,1)S(1)} %get-tuple-element.55.sq_r, f32[512,512]{1,0:T(8,128)S(1)} %get-tuple-element.56.part_l, ...), custom_call_target="tpu_custom_call" | custom-call | flops 536870912 | bytes 4194304 | tf_op jit(solution)/shard_map/pallas_call | solution.py:31
Async XLA Ops:
  0.0 5.1 %copy-start = (bf16[4,8,128,128]{3,2,1,0:T(8,128)(2,1)S(1)}, bf16[4,8,128,128]{3,2,1,0:T(8,128)(2,1)}, u32[]{:S(2)}) copy-start(bf16[4,8,128,128]{3,2,1,0:T(8,128)(2,1)} %x_ref.3) | copy-start | bytes 3145732
  1.4 14.3 %collective-permute-start = (bf16[832,512]{1,0:T(8,128)(2,1)S(1)}, bf16[832,512]{1,0:T(8,128)(2,1)S(1)}, u32[]{:S(2)}, u32[]{:S(2)}) collective-permute-start(bf16[832,512]{1,0:T(8,128)(2,1)S(1)} %get-tuple-element.35), channel_id=1, source_target_pairs={{1,2},{3,4},{5,6},{7,8},{9,10},{11,12},{13,14},{15,16},{17,18},{19... | collective-permute-start | bytes 2555912 | tf_op jit(solution)/shard_map/ppermute | solution.py:409
  5.4 23.9 %collective-permute-start.2 = (bf16[10,128,128]{2,1,0:T(8,128)(2,1)S(1)}, bf16[10,128,128]{2,1,0:T(8,128)(2,1)S(1)}, u32[]{:S(2)}, u32[]{:S(2)}) collective-permute-start(bf16[10,128,128]{2,1,0:T(8,128)(2,1)S(1)} %get-tuple-element.38), channel_id=1, source_target_pairs={{1,2},{3,4},{5,6},{7,8},{9,10},{11,12},{13,14},{15,16},{17,18},{19... | collective-permute-start | bytes 983048 | tf_op jit(solution)/shard_map/ppermute | solution.py:409
  7.3 26.6 %collective-permute-start.4 = (bf16[512,512]{1,0:T(8,128)(2,1)S(1)}, bf16[512,512]{1,0:T(8,128)(2,1)S(1)}, u32[]{:S(2)}, u32[]{:S(2)}) collective-permute-start(bf16[512,512]{1,0:T(8,128)(2,1)S(1)} %get-tuple-element.42), channel_id=1, source_target_pairs={{1,2},{3,4},{5,6},{7,8},{9,10},{11,12},{13,14},{15,16},{17,18},{19... | collective-permute-start | bytes 1572872 | tf_op jit(solution)/shard_map/ppermute | solution.py:409
  15.7 15.6 %collective-permute-start.1 = (bf16[832,512]{1,0:T(8,128)(2,1)S(1)}, bf16[832,512]{1,0:T(8,128)(2,1)S(1)}, u32[]{:S(2)}, u32[]{:S(2)}) collective-permute-start(bf16[832,512]{1,0:T(8,128)(2,1)S(1)} %collective-permute-done.joint), channel_id=1, source_target_pairs={{0,1},{1,0},{2,3},{3,2},{4,5},{5,4},{6,7},{7,6},{8,9},{9,8},{10,11... | collective-permute-start | bytes 2555912 | tf_op jit(solution)/shard_map/ppermute | solution.py:412
  29.4 3.5 %collective-permute-start.3 = (bf16[10,128,128]{2,1,0:T(8,128)(2,1)S(1)}, bf16[10,128,128]{2,1,0:T(8,128)(2,1)S(1)}, u32[]{:S(2)}, u32[]{:S(2)}) collective-permute-start(bf16[10,128,128]{2,1,0:T(8,128)(2,1)S(1)} %get-tuple-element.40), channel_id=1, source_target_pairs={{0,1},{1,0},{2,3},{3,2},{4,5},{5,4},{6,7},{7,6},{8,9},{9,8},{10,11... | collective-permute-start | bytes 983048 | tf_op jit(solution)/shard_map/ppermute | solution.py:412
  34.3 14.3 %collective-permute-start.6 = (bf16[832,512]{1,0:T(8,128)(2,1)S(1)}, bf16[832,512]{1,0:T(8,128)(2,1)S(1)}, u32[]{:S(2)}, u32[]{:S(2)}) collective-permute-start(bf16[832,512]{1,0:T(8,128)(2,1)S(1)} %get-tuple-element.47), channel_id=1, source_target_pairs={{1,2},{3,4},{5,6},{7,8},{9,10},{11,12},{13,14},{15,16},{17,18},{19... | collective-permute-start | bytes 2555912 | tf_op jit(solution)/shard_map/ppermute | solution.py:409
  36.3 10.4 %collective-permute-start.5 = (bf16[10,128,128]{2,1,0:T(8,128)(2,1)S(1)}, bf16[10,128,128]{2,1,0:T(8,128)(2,1)S(1)}, u32[]{:S(2)}, u32[]{:S(2)}) collective-permute-start(bf16[10,128,128]{2,1,0:T(8,128)(2,1)S(1)} %get-tuple-element.46), channel_id=1, source_target_pairs={{0,1},{1,0},{2,3},{3,2},{4,5},{5,4},{6,7},{7,6},{8,9},{9,8},{10,11... | collective-permute-start | bytes 983048 | tf_op jit(solution)/shard_map/ppermute | solution.py:412
  48.6 9.4 %collective-permute-start.7 = (bf16[832,512]{1,0:T(8,128)(2,1)S(1)}, bf16[832,512]{1,0:T(8,128)(2,1)S(1)}, u32[]{:S(2)}, u32[]{:S(2)}) collective-permute-start(bf16[832,512]{1,0:T(8,128)(2,1)S(1)} %collective-permute-done.6.joint), channel_id=1, source_target_pairs={{0,1},{1,0},{2,3},{3,2},{4,5},{5,4},{6,7},{7,6},{8,9},{9,8},{10,11... | collective-permute-start | bytes 2555912 | tf_op jit(solution)/shard_map/ppermute | solution.py:412
  59.2 14.3 %collective-permute-start.8 = (bf16[832,512]{1,0:T(8,128)(2,1)S(1)}, bf16[832,512]{1,0:T(8,128)(2,1)S(1)}, u32[]{:S(2)}, u32[]{:S(2)}) collective-permute-start(bf16[832,512]{1,0:T(8,128)(2,1)S(1)} %get-tuple-element.54), channel_id=1, source_target_pairs={{1,2},{3,4},{5,6},{7,8},{9,10},{11,12},{13,14},{15,16},{17,18},{19... | collective-permute-start | bytes 2555912 | tf_op jit(solution)/shard_map/ppermute | solution.py:409
  73.6 9.4 %collective-permute-start.9 = (bf16[832,512]{1,0:T(8,128)(2,1)S(1)}, bf16[832,512]{1,0:T(8,128)(2,1)S(1)}, u32[]{:S(2)}, u32[]{:S(2)}) collective-permute-start(bf16[832,512]{1,0:T(8,128)(2,1)S(1)} %collective-permute-done.8.joint), channel_id=1, source_target_pairs={{0,1},{1,0},{2,3},{3,2},{4,5},{5,4},{6,7},{7,6},{8,9},{9,8},{10,11... | collective-permute-start | bytes 2555912 | tf_op jit(solution)/shard_map/ppermute | solution.py:412

commit v9 on v7

--- a/solution.py
+++ b/solution.py
@@ -132,15 +132,13 @@
             joint_send(send, row, t, row_block(h_ref, table, row, t))
 
 
-def pack_x_kernel(table, x_ref, xa, xb, marks):
+def pack_x_kernel(table, x_ref, xa, xb):
     diag = eye()
     for index, (p, m) in enumerate(TRI):
         xa[index] = slot_block(x_ref, table, 3 - p, 11 - m)
     for row in range(4):
         for m in range(4):
             put(xb, 3 - row, 3 - m, x_slot_block(x_ref, table, diag, row, 4 + m))
-    for i in range(48):
-        marks[i : i + 1, :] = jnp.full((1, S), jnp.where(table[i] >= 0, 1.0, 0.0), F32)
 
 
 def spread_mine(get, square_ref):
@@ -226,7 +224,9 @@
     ref[i * H : (i + 1) * H, j * H : (j + 1) * H] = value
 
 
-def mine_kernel(table, h_ref, x_ref, joint, xo, part, ho, rc):
+def mine_kernel(table, h_ref, x_ref, joint, xo, part, marks, ho, rc):
+    for i in range(48):
+        marks[i : i + 1, :] = jnp.full((1, S), jnp.where(table[i] >= 0, 1.0, 0.0), F32)
     diag = eye()
     for row in range(4):
         for t in range(12):
@@ -422,10 +422,10 @@
         *(pltpu.with_memory_space_constraint(x, pltpu.HBM) for x in (cols, mask, hamiltonian)),
     )
     h_halo = link(h_send)
-    xa, xb, marks = call(
+    xa, xb = call(
         pack_x_kernel,
-        [CORNER, SQUARE, jax.ShapeDtypeStruct((48, S), F32)],
-        [VMEM] * 3,
+        [CORNER, SQUARE],
+        [VMEM] * 2,
         [SMEM, VMEM],
         [],
         0,
@@ -434,10 +434,10 @@
     xa_halo = link(xa)
     xb_halo = link(xb)
     h_twin = swap(h_halo)
-    xo, part = call(
+    xo, part, marks = call(
         mine_kernel,
-        [BANDED, WIDE],
-        [VMEM] * 2,
+        [BANDED, WIDE, jax.ShapeDtypeStruct((48, S), F32)],
+        [VMEM] * 3,
         [SMEM] + [VMEM] * 3,
         [pltpu.VMEM((Q, 3 * Q), BF), square],
         64 * flops,

time: 86 us -> 85.9 us (level)
  no operation moved by 1% of the time
where the time goes in v9:
time: 85.9 us; the launch traced here: 85.6 us
  starting transfers between devices  51.2 us (60%)
  waiting for transfers between devices  21.6 us (25%)
  Pallas kernels  12.5 us (15%)
    ppermute x5, starting transfers between devices, swap(): return lax.ppermute(x, 'rep', [(0, 1), (1, 0)])  38.1 us
    ppermute x5, waiting for transfers between devices, link(): return lax.ppermute(x, ('rows', 'rep'), outward)  18.3 us
    ppermute x5, starting transfers between devices, link(): return lax.ppermute(x, ('rows', 'rep'), outward)  13.1 us
    pallas_call x13, Pallas kernels, call(): pl.pallas_call(kernel, out_shape=outs, in_specs=in_specs, out_specs=out_s...  12.5 us
    ppermute x5, waiting for transfers between devices, swap(): return lax.ppermute(x, 'rep', [(0, 1), (1, 0)])  3.26 us
  transfers between devices with their start and end apart: 10, of which 7 were waited for; matrix products, arithmetic and copies ran while one was open for 0% of the time, Pallas kernels for 8%

profile of v9, /device:TPU:33, one launch (start us, length us, event | category | flops | bytes accessed | tf_op | source)
XLA Modules:
  0.0 85.6 jit_solution(998785190401899268)
XLA Ops:
  0.0 0.0 copy-start
  0.0 1.4 %shard_map.46 = (bf16[832,512]{1,0:T(8,128)(2,1)S(1)}, s32[81]{0:T(128)S(4)}, bf16[4,8,128,128]{3,2,1,0:T(8,128)(2,1)S(1)}) custom-call(s32[4,8]{1,0:T(4,128)} %cols_hbm.1, s32[4,8]{1,0:T(4,128)} %mask_hbm.1, bf16[4,8,128,128]{3,2,1,0:T(8,128)(2,1)} %h_hbm.1), custom_call_target="tpu_custom_call" | custom-call | flops 536870912 | bytes 4194304 | tf_op jit(solution)/shard_map/pallas_call | solution.py:31
  1.4 3.7 %collective-permute-start = (bf16[832,512]{1,0:T(8,128)(2,1)S(1)}, bf16[832,512]{1,0:T(8,128)(2,1)S(1)}, u32[]{:S(2)}, u32[]{:S(2)}) collective-permute-start(bf16[832,512]{1,0:T(8,128)(2,1)S(1)} %get-tuple-element.33), channel_id=1, source_target_pairs={{1,2},{3,4},{5,6},{7,8},{9,10},{11,12},{13,14},{15,16},{17,18},{19... | collective-permute-start | bytes 2555912 | tf_op jit(solution)/shard_map/ppermute | solution.py:401
  5.1 0.0 copy-done
  5.1 0.2 shard_map.49
  5.3 1.9 %collective-permute-start.3 = (bf16[10,128,128]{2,1,0:T(8,128)(2,1)S(1)}, bf16[10,128,128]{2,1,0:T(8,128)(2,1)S(1)}, u32[]{:S(2)}, u32[]{:S(2)}) collective-permute-start(bf16[10,128,128]{2,1,0:T(8,128)(2,1)S(1)} %get-tuple-element.38), channel_id=1, source_target_pairs={{1,2},{3,4},{5,6},{7,8},{9,10},{11,12},{13,14},{15,16},{17,18},{19... | collective-permute-start | bytes 983048 | tf_op jit(solution)/shard_map/ppermute | solution.py:401
  7.3 3.6 %collective-permute-start.2 = (bf16[512,512]{1,0:T(8,128)(2,1)S(1)}, bf16[512,512]{1,0:T(8,128)(2,1)S(1)}, u32[]{:S(2)}, u32[]{:S(2)}) collective-permute-start(bf16[512,512]{1,0:T(8,128)(2,1)S(1)} %get-tuple-element.37), channel_id=1, source_target_pairs={{1,2},{3,4},{5,6},{7,8},{9,10},{11,12},{13,14},{15,16},{17,18},{19... | collective-permute-start | bytes 1572872 | tf_op jit(solution)/shard_map/ppermute | solution.py:401
  10.9 4.8 %collective-permute-done.joint = bf16[832,512]{1,0:T(8,128)(2,1)S(1)} collective-permute-done((bf16[832,512]{1,0:T(8,128)(2,1)S(1)}, bf16[832,512]{1,0:T(8,128)(2,1)S(1)}, u32[]{:S(2)}, u32[]{:S(2)}) %collective-permute-start) | collective-permute-done | bytes 852000 | tf_op jit(solution)/shard_map/ppermute | solution.py:401
  15.7 12.0 %collective-permute-start.1 = (bf16[832,512]{1,0:T(8,128)(2,1)S(1)}, bf16[832,512]{1,0:T(8,128)(2,1)S(1)}, u32[]{:S(2)}, u32[]{:S(2)}) collective-permute-start(bf16[832,512]{1,0:T(8,128)(2,1)S(1)} %collective-permute-done.joint), channel_id=1, source_target_pairs={{0,1},{1,0},{2,3},{3,2},{4,5},{5,4},{6,7},{7,6},{8,9},{9,8},{10,11... | collective-permute-start | bytes 2555912 | tf_op jit(solution)/shard_map/ppermute | solution.py:404
  27.7 1.5 %shard_map.47 = (bf16[512,1536]{1,0:T(8,128)(2,1)S(1)}, f32[512,1536]{1,0:T(8,128)S(1)}, f32[48,128]{1,0:T(8,128)S(1)}) custom-call(s32[81]{0:T(128)S(4)} %get-tuple-element.31.table.index, bf16[4,8,128,128]{3,2,1,0:T(8,128)(2,1)S(1)} %get-tuple-element.32.h_ref, bf16[4,8,128,128]{3,2,1,0:T(8,128)(2,1)S(1)} %copy-done, ...), custom_call_target="tpu_custom_call" | custom-call | flops 34359738368 | bytes 4194304 | tf_op jit(solution)/shard_map/pallas_call | solution.py:31
  29.3 0.0 collective-permute-done.3.xa
  29.3 0.1 shard_map.50
  29.4 1.9 %collective-permute-start.4 = (bf16[10,128,128]{2,1,0:T(8,128)(2,1)S(1)}, bf16[10,128,128]{2,1,0:T(8,128)(2,1)S(1)}, u32[]{:S(2)}, u32[]{:S(2)}) collective-permute-start(bf16[10,128,128]{2,1,0:T(8,128)(2,1)S(1)} %get-tuple-element.40), channel_id=1, source_target_pairs={{0,1},{1,0},{2,3},{3,2},{4,5},{5,4},{6,7},{7,6},{8,9},{9,8},{10,11... | collective-permute-start | bytes 983048 | tf_op jit(solution)/shard_map/ppermute | solution.py:404
  31.3 0.0 collective-permute-done.1.twin
  31.3 0.6 shard_map.48.refs_1_
  31.9 1.0 %collective-permute-done.4.refs_4_ = bf16[10,128,128]{2,1,0:T(8,128)(2,1)S(1)} collective-permute-done((bf16[10,128,128]{2,1,0:T(8,128)(2,1)S(1)}, bf16[10,128,128]{2,1,0:T(8,128)(2,1)S(1)}, u32[]{:S(2)}, u32[]{:S(2)}) %collective-permute-start.4) | collective-permute-done | bytes 327712 | tf_op jit(solution)/shard_map/ppermute | solution.py:404
  32.9 0.8 shard_map.51
  33.8 0.0 collective-permute-done.2.refs_3_
  33.8 0.5 shard_map.52
  34.3 1.9 %collective-permute-start.6 = (bf16[832,512]{1,0:T(8,128)(2,1)S(1)}, bf16[832,512]{1,0:T(8,128)(2,1)S(1)}, u32[]{:S(2)}, u32[]{:S(2)}) collective-permute-start(bf16[832,512]{1,0:T(8,128)(2,1)S(1)} %get-tuple-element.45), channel_id=1, source_target_pairs={{1,2},{3,4},{5,6},{7,8},{9,10},{11,12},{13,14},{15,16},{17,18},{19... | collective-permute-start | bytes 2555912 | tf_op jit(solution)/shard_map/ppermute | solution.py:401
  36.2 9.3 %collective-permute-start.5 = (bf16[10,128,128]{2,1,0:T(8,128)(2,1)S(1)}, bf16[10,128,128]{2,1,0:T(8,128)(2,1)S(1)}, u32[]{:S(2)}, u32[]{:S(2)}) collective-permute-start(bf16[10,128,128]{2,1,0:T(8,128)(2,1)S(1)} %get-tuple-element.44), channel_id=1, source_target_pairs={{0,1},{1,0},{2,3},{3,2},{4,5},{5,4},{6,7},{7,6},{8,9},{9,8},{10,11... | collective-permute-start | bytes 983048 | tf_op jit(solution)/shard_map/ppermute | solution.py:404
  45.6 1.2 %collective-permute-done.5.side = bf16[10,128,128]{2,1,0:T(8,128)(2,1)S(1)} collective-permute-done((bf16[10,128,128]{2,1,0:T(8,128)(2,1)S(1)}, bf16[10,128,128]{2,1,0:T(8,128)(2,1)S(1)}, u32[]{:S(2)}, u32[]{:S(2)}) %collective-permute-start.5) | collective-permute-done | bytes 327712 | tf_op jit(solution)/shard_map/ppermute | solution.py:404
  46.8 0.1 shard_map.53.band
  46.9 1.7 %collective-permute-done.6.joint = bf16[832,512]{1,0:T(8,128)(2,1)S(1)} collective-permute-done((bf16[832,512]{1,0:T(8,128)(2,1)S(1)}, bf16[832,512]{1,0:T(8,128)(2,1)S(1)}, u32[]{:S(2)}, u32[]{:S(2)}) %collective-permute-start.6) | collective-permute-done | bytes 852000 | tf_op jit(solution)/shard_map/ppermute | solution.py:401
  48.6 7.5 %collective-permute-start.7 = (bf16[832,512]{1,0:T(8,128)(2,1)S(1)}, bf16[832,512]{1,0:T(8,128)(2,1)S(1)}, u32[]{:S(2)}, u32[]{:S(2)}) collective-permute-start(bf16[832,512]{1,0:T(8,128)(2,1)S(1)} %collective-permute-done.6.joint), channel_id=1, source_target_pairs={{0,1},{1,0},{2,3},{3,2},{4,5},{5,4},{6,7},{7,6},{8,9},{9,8},{10,11... | collective-permute-start | bytes 2555912 | tf_op jit(solution)/shard_map/ppermute | solution.py:404
  56.1 1.5 %shard_map.54 = (bf16[512,512]{1,0:T(8,128)(2,1)S(1)}, f32[512,512]{1,0:T(8,128)S(1)}, f32[512,512]{1,0:T(8,128)S(1)}, f32[512,1024]{1,0:T(8,128)S(1)}) custom-call(f32[48,128]{1,0:T(8,128)S(1)} %get-tuple-element.34.table.refs_0_, bf16[512,1536]{1,0:T(8,128)(2,1)S(1)} %shard_map.53.band, bf16[832,512]{1,0:T(8,128)(2,1)S(1)} %collective-permute-done.6.joint), custom_call_target="tpu_custom_call" | custom-call | flops 34359738368 | bytes 4194304 | tf_op jit(solution)/shard_map/pallas_call | solution.py:31
  57.6 0.5 collective-permute-done.7.twin
  58.1 1.3 %shard_map.55 = (bf16[512,1536]{1,0:T(8,128)(2,1)S(1)}, bf16[832,512]{1,0:T(8,128)(2,1)S(1)}, bf16[512,1024]{1,0:T(8,128)(2,1)S(1)}) custom-call(f32[48,128]{1,0:T(8,128)S(1)} %get-tuple-element.34.table.refs_0_, bf16[512,1536]{1,0:T(8,128)(2,1)S(1)} %shard_map.53.band, bf16[512,512]{1,0:T(8,128)(2,1)S(1)} %get-tuple-element.46.sq_r, ...), custom_call_target="tpu_custom_call" | custom-call | flops 536870912 | bytes 4194304 | tf_op jit(solution)/shard_map/pallas_call | solution.py:31
  59.4 1.9 %collective-permute-start.8 = (bf16[832,512]{1,0:T(8,128)(2,1)S(1)}, bf16[832,512]{1,0:T(8,128)(2,1)S(1)}, u32[]{:S(2)}, u32[]{:S(2)}) collective-permute-start(bf16[832,512]{1,0:T(8,128)(2,1)S(1)} %get-tuple-element.52), channel_id=1, source_target_pairs={{1,2},{3,4},{5,6},{7,8},{9,10},{11,12},{13,14},{15,16},{17,18},{19... | collective-permute-start | bytes 2555912 | tf_op jit(solution)/shard_map/ppermute | solution.py:401
  61.3 0.5 shard_map.56.band
  61.9 11.8 %collective-permute-done.8.joint = bf16[832,512]{1,0:T(8,128)(2,1)S(1)} collective-permute-done((bf16[832,512]{1,0:T(8,128)(2,1)S(1)}, bf16[832,512]{1,0:T(8,128)(2,1)S(1)}, u32[]{:S(2)}, u32[]{:S(2)}) %collective-permute-start.8) | collective-permute-done | bytes 852000 | tf_op jit(solution)/shard_map/ppermute | solution.py:401
  73.7 7.4 %collective-permute-start.9 = (bf16[832,512]{1,0:T(8,128)(2,1)S(1)}, bf16[832,512]{1,0:T(8,128)(2,1)S(1)}, u32[]{:S(2)}, u32[]{:S(2)}) collective-permute-start(bf16[832,512]{1,0:T(8,128)(2,1)S(1)} %collective-permute-done.8.joint), channel_id=1, source_target_pairs={{0,1},{1,0},{2,3},{3,2},{4,5},{5,4},{6,7},{7,6},{8,9},{9,8},{10,11... | collective-permute-start | bytes 2555912 | tf_op jit(solution)/shard_map/ppermute | solution.py:404
  81.1 1.5 %shard_map.57 = (bf16[512,512]{1,0:T(8,128)(2,1)S(1)}, f32[512,512]{1,0:T(8,128)S(1)}, f32[512,512]{1,0:T(8,128)S(1)}, f32[512,1024]{1,0:T(8,128)S(1)}) custom-call(f32[48,128]{1,0:T(8,128)S(1)} %get-tuple-element.34.table.refs_0_, bf16[512,1536]{1,0:T(8,128)(2,1)S(1)} %shard_map.56.band, bf16[832,512]{1,0:T(8,128)(2,1)S(1)} %collective-permute-done.8.joint), custom_call_target="tpu_custom_call" | custom-call | flops 34359738368 | bytes 4194304 | tf_op jit(solution)/shard_map/pallas_call | solution.py:31
  82.6 0.5 collective-permute-done.9.twin
  83.1 2.5 %shard_map.58 = bf16[4,4,128,128]{3,2,1,0:T(8,128)(2,1)} custom-call(s32[81]{0:T(128)S(4)} %get-tuple-element.31.table.index, f32[48,128]{1,0:T(8,128)S(1)} %get-tuple-element.34.table.refs_0_, bf16[512,1536]{1,0:T(8,128)(2,1)S(1)} %shard_map.56.band, bf16[512,512]{1,0:T(8,128)(2,1)S(1)} %get-tuple-element.53.sq_r, f32[512,512]{1,0:T(8,128)S(1)} %get-tuple-element.54.part_l, ...), custom_call_target="tpu_custom_call" | custom-call | flops 536870912 | bytes 4194304 | tf_op jit(solution)/shard_map/pallas_call | solution.py:31
Async XLA Ops:
  0.0 5.1 %copy-start = (bf16[4,8,128,128]{3,2,1,0:T(8,128)(2,1)S(1)}, bf16[4,8,128,128]{3,2,1,0:T(8,128)(2,1)}, u32[]{:S(2)}) copy-start(bf16[4,8,128,128]{3,2,1,0:T(8,128)(2,1)} %x_ref.3) | copy-start | bytes 3145732
  1.4 14.3 %collective-permute-start = (bf16[832,512]{1,0:T(8,128)(2,1)S(1)}, bf16[832,512]{1,0:T(8,128)(2,1)S(1)}, u32[]{:S(2)}, u32[]{:S(2)}) collective-permute-start(bf16[832,512]{1,0:T(8,128)(2,1)S(1)} %get-tuple-element.33), channel_id=1, source_target_pairs={{1,2},{3,4},{5,6},{7,8},{9,10},{11,12},{13,14},{15,16},{17,18},{19... | collective-permute-start | bytes 2555912 | tf_op jit(solution)/shard_map/ppermute | solution.py:401
  5.3 23.9 %collective-permute-start.3 = (bf16[10,128,128]{2,1,0:T(8,128)(2,1)S(1)}, bf16[10,128,128]{2,1,0:T(8,128)(2,1)S(1)}, u32[]{:S(2)}, u32[]{:S(2)}) collective-permute-start(bf16[10,128,128]{2,1,0:T(8,128)(2,1)S(1)} %get-tuple-element.38), channel_id=1, source_target_pairs={{1,2},{3,4},{5,6},{7,8},{9,10},{11,12},{13,14},{15,16},{17,18},{19... | collective-permute-start | bytes 983048 | tf_op jit(solution)/shard_map/ppermute | solution.py:401
  7.3 26.5 %collective-permute-start.2 = (bf16[512,512]{1,0:T(8,128)(2,1)S(1)}, bf16[512,512]{1,0:T(8,128)(2,1)S(1)}, u32[]{:S(2)}, u32[]{:S(2)}) collective-permute-start(bf16[512,512]{1,0:T(8,128)(2,1)S(1)} %get-tuple-element.37), channel_id=1, source_target_pairs={{1,2},{3,4},{5,6},{7,8},{9,10},{11,12},{13,14},{15,16},{17,18},{19... | collective-permute-start | bytes 1572872 | tf_op jit(solution)/shard_map/ppermute | solution.py:401
  15.7 15.6 %collective-permute-start.1 = (bf16[832,512]{1,0:T(8,128)(2,1)S(1)}, bf16[832,512]{1,0:T(8,128)(2,1)S(1)}, u32[]{:S(2)}, u32[]{:S(2)}) collective-permute-start(bf16[832,512]{1,0:T(8,128)(2,1)S(1)} %collective-permute-done.joint), channel_id=1, source_target_pairs={{0,1},{1,0},{2,3},{3,2},{4,5},{5,4},{6,7},{7,6},{8,9},{9,8},{10,11... | collective-permute-start | bytes 2555912 | tf_op jit(solution)/shard_map/ppermute | solution.py:404
  29.4 3.5 %collective-permute-start.4 = (bf16[10,128,128]{2,1,0:T(8,128)(2,1)S(1)}, bf16[10,128,128]{2,1,0:T(8,128)(2,1)S(1)}, u32[]{:S(2)}, u32[]{:S(2)}) collective-permute-start(bf16[10,128,128]{2,1,0:T(8,128)(2,1)S(1)} %get-tuple-element.40), channel_id=1, source_target_pairs={{0,1},{1,0},{2,3},{3,2},{4,5},{5,4},{6,7},{7,6},{8,9},{9,8},{10,11... | collective-permute-start | bytes 983048 | tf_op jit(solution)/shard_map/ppermute | solution.py:404
  34.3 14.3 %collective-permute-start.6 = (bf16[832,512]{1,0:T(8,128)(2,1)S(1)}, bf16[832,512]{1,0:T(8,128)(2,1)S(1)}, u32[]{:S(2)}, u32[]{:S(2)}) collective-permute-start(bf16[832,512]{1,0:T(8,128)(2,1)S(1)} %get-tuple-element.45), channel_id=1, source_target_pairs={{1,2},{3,4},{5,6},{7,8},{9,10},{11,12},{13,14},{15,16},{17,18},{19... | collective-permute-start | bytes 2555912 | tf_op jit(solution)/shard_map/ppermute | solution.py:401
  36.2 10.6 %collective-permute-start.5 = (bf16[10,128,128]{2,1,0:T(8,128)(2,1)S(1)}, bf16[10,128,128]{2,1,0:T(8,128)(2,1)S(1)}, u32[]{:S(2)}, u32[]{:S(2)}) collective-permute-start(bf16[10,128,128]{2,1,0:T(8,128)(2,1)S(1)} %get-tuple-element.44), channel_id=1, source_target_pairs={{0,1},{1,0},{2,3},{3,2},{4,5},{5,4},{6,7},{7,6},{8,9},{9,8},{10,11... | collective-permute-start | bytes 983048 | tf_op jit(solution)/shard_map/ppermute | solution.py:404
  48.6 9.5 %collective-permute-start.7 = (bf16[832,512]{1,0:T(8,128)(2,1)S(1)}, bf16[832,512]{1,0:T(8,128)(2,1)S(1)}, u32[]{:S(2)}, u32[]{:S(2)}) collective-permute-start(bf16[832,512]{1,0:T(8,128)(2,1)S(1)} %collective-permute-done.6.joint), channel_id=1, source_target_pairs={{0,1},{1,0},{2,3},{3,2},{4,5},{5,4},{6,7},{7,6},{8,9},{9,8},{10,11... | collective-permute-start | bytes 2555912 | tf_op jit(solution)/shard_map/ppermute | solution.py:404
  59.4 14.3 %collective-permute-start.8 = (bf16[832,512]{1,0:T(8,128)(2,1)S(1)}, bf16[832,512]{1,0:T(8,128)(2,1)S(1)}, u32[]{:S(2)}, u32[]{:S(2)}) collective-permute-start(bf16[832,512]{1,0:T(8,128)(2,1)S(1)} %get-tuple-element.52), channel_id=1, source_target_pairs={{1,2},{3,4},{5,6},{7,8},{9,10},{11,12},{13,14},{15,16},{17,18},{19... | collective-permute-start | bytes 2555912 | tf_op jit(solution)/shard_map/ppermute | solution.py:401
  73.7 9.4 %collective-permute-start.9 = (bf16[832,512]{1,0:T(8,128)(2,1)S(1)}, bf16[832,512]{1,0:T(8,128)(2,1)S(1)}, u32[]{:S(2)}, u32[]{:S(2)}) collective-permute-start(bf16[832,512]{1,0:T(8,128)(2,1)S(1)} %collective-permute-done.8.joint), channel_id=1, source_target_pairs={{0,1},{1,0},{2,3},{3,2},{4,5},{5,4},{6,7},{7,6},{8,9},{9,8},{10,11... | collective-permute-start | bytes 2555912 | tf_op jit(solution)/shard_map/ppermute | solution.py:404
